TPU v7x, 256 devices: a whole 4x4x8 slice. The times are simulated.
256 devices in a mesh: gx: 32 (over y, x, core), gy: 8 (over z).
Axes of the slice: x: 4, y: 4, z: 8, core: 2. Of those that a mesh axis runs over, the one named last changes fastest.
Arguments:
- position: float32 [3, 524288], P(None, ('gx', 'gy')), may hold values from -0.5 to 0.5
- velocity: float32 [3, 524288], P(None, ('gx', 'gy')), may hold values from -6 to 6
- cell_list: int32 [4, 256, 256, 16], P(None, 'gx', 'gy'), may hold values from 0 to 2048, as said below
- slot_weight: float32 [4, 256, 256, 16], P(None, 'gx', 'gy'), may hold values from 0.25 to 1
- particle_cell: int32 [524288], P(('gx', 'gy')), may hold values from 0 to 4095, as said below
- destination: int32 [524288, 1], P(('gx', 'gy')), may hold values from 0 to 8; in each aligned block of 2048 rows (0 to 2047, 2048 to 4095, ...) at most 512 rows name the same one
- lift: float32 [32, 4], replicated, may hold values from -3 to 3
- kernel_0a: bfloat16 [27, 32, 32], replicated, may hold values from -0.4375 to 0.4375
- kernel_1a: bfloat16 [27, 32, 32], replicated, may hold values from -0.4375 to 0.4375
- kernel_2: bfloat16 [27, 32, 32], replicated, may hold values from -0.4375 to 0.4375
- kernel_1b: bfloat16 [27, 32, 32], replicated, may hold values from -0.4375 to 0.4375
- kernel_0b: bfloat16 [27, 32, 32], replicated, may hold values from -0.4375 to 0.4375
- head: bfloat16 [3, 32], replicated, may hold values from -1 to 1
Outputs:
- moved_state: float32 [6, 1179648], P(None, ('gx', 'gy'))
Inputs may be any that keep to these rules, and one draw needn't show every extreme that they name: `cell_list`: on each device every local particle index below 2048 stands in exactly one slot of the device's cells, and 2048 marks an empty slot. `particle_cell`: the local cell in whose slots the particle stands. `destination`: direction 3 (a+1) + (b+1) means the device a steps along gx and b along gy, periodic; among the particles of one device at most 512 share a direction.
All inputs are finite; a program needn't handle non-finite values.
Results may differ from a plain program's by a relative error of at most 0.034.
Values may be sent and summed in bfloat16 or wider, within the bound.
No kernel may reach another device: no remote copies, remote signals or barrier semaphores. Data moves between devices by JAX's collectives and lax.ppermute only.
A program may use at most 128 MiB of HBM per device.

v0:
```python
import jax
import jax.numpy as jnp
import numpy as np
from jax import lax
from jax.experimental import pallas as pl
from jax.experimental.pallas import tpu as pltpu
from jax.sharding import PartitionSpec as P

f32 = jnp.float32
bf16 = jnp.bfloat16
i32 = jnp.int32

CAP = 512
DRIFT = 0.25
CH = 32
NZ = 16
COLS = 28
ROWS = 32


def iota(shape, dim):
    return lax.broadcasted_iota(i32, shape, dim)


def dot(a, b):
    return jnp.dot(a, b, preferred_element_type=f32)


def gelu(x):
    inner = x * (0.7978845608028654 + 0.035677408136300125 * (x * x))
    return (0.5 * x) * (1.0 + jnp.tanh(inner))


def deposit_kernel(vel_ref, cells_ref, weight_ref, out_ref, stage):
    totals = [jnp.zeros((32, 128), f32) for _ in range(4)]
    for s in range(4):
        entry = jnp.concatenate([cells_ref[s, x] for x in range(8)], axis=1)
        weight = jnp.concatenate([weight_ref[s, x] for x in range(8)], axis=1)
        lane = jnp.bitwise_and(entry, 127)
        row = jnp.right_shift(entry, 7)
        picked = [jnp.zeros((32, 128), f32) for _ in range(3)]
        for r in range(16):
            here = row == r
            for q in range(3):
                table = jnp.broadcast_to(vel_ref[q : q + 1, r * 128 : (r + 1) * 128], (32, 128))
                got = jnp.take_along_axis(table, lane, axis=1)
                picked[q] = jnp.where(here, got, picked[q])
        totals[0] = totals[0] + jnp.where(entry < 2048, weight, 0.0)
        for q in range(3):
            totals[q + 1] = totals[q + 1] + weight * picked[q]
    group = iota((32, 128), 1) // 16
    for t in range(4):
        piece = jnp.zeros((32, 128), f32)
        for half in range(2):
            for q in range(4):
                source, target = (2 * t + half) * 16, half * 64 + q * 16
                shift = (target - source) % 128
                moved = pltpu.roll(totals[q], shift, 1) if shift else totals[q]
                piece = jnp.where(group == half * 4 + q, moved, piece)
        stage[t * 32 : t * 32 + 32, :] = piece
    for t in range(4):
        lanes = slice(t * 128, (t + 1) * 128)
        for parity in range(2):
            out_ref[parity * 16 : parity * 16 + 16, lanes] = stage[
                pl.ds(t * 32 + parity, 16, stride=2), :
            ].astype(bf16)


def deposit(velocity, cells, weight):
    return pl.pallas_call(
        deposit_kernel,
        out_shape=jax.ShapeDtypeStruct((32, 512), bf16),
        scratch_shapes=[pltpu.VMEM((128, 128), f32)],
        cost_estimate=pl.CostEstimate(flops=2_000_000, bytes_accessed=1_000_000, transcendentals=0),
    )(velocity, cells, weight)


def prep_kernel(
    first_ref, taps_ref, dest_ref, w0a_ref, w1a_ref, w2_ref, w1b_ref, w0b_ref, rank_ref
):
    row = iota((16, 128), 0)
    masks = []
    for t in range(4):
        diff = jnp.bitwise_and(row - (4 * t + iota((16, 128), 1) // 32), 15)
        masks.append((diff == 15, diff == 0, diff == 1))
    for ox in range(3):
        for oy in range(3):
            for q in range(4):
                at = (9 * ox + 3 * oy) * 4 + q
                low = jnp.broadcast_to(first_ref[at : at + 1, :], (16, 128))
                mid = jnp.broadcast_to(first_ref[at + 4 : at + 5, :], (16, 128))
                high = jnp.broadcast_to(first_ref[at + 8 : at + 9, :], (16, 128))
                for t in range(4):
                    below, same, above = masks[t]
                    piece = jnp.where(
                        same, mid, jnp.where(below, low, jnp.where(above, high, 0.0))
                    )
                    begin = oy * 256 + ox * 64 + q * 16
                    w0a_ref[begin : begin + 16, t * 128 : (t + 1) * 128] = piece.astype(bf16)
    for oy in range(3):
        w0a_ref[oy * 256 + 192 : oy * 256 + 256, :] = jnp.zeros((64, 512), bf16)

    group = iota((32, 128), 1) // 32

    def bands(number, out_ref, depth):
        tiles = depth // 4

        def one(tap, carry):
            at = number * 27 + 3 * tap
            low = taps_ref[at].astype(f32)
            mid = taps_ref[at + 1].astype(f32)
            high = taps_ref[at + 2].astype(f32)
            zero = jnp.zeros((32, 128), f32)

            def pick(*wanted):
                value = zero
                for index, piece in wanted:
                    value = jnp.where(group == index, piece, value)
                return value

            patterns = (
                {0: pick((0, mid), (1, low)), -1: pick((3, high))},
                {0: pick((0, high), (1, mid), (2, low))},
                {0: pick((1, high), (2, mid), (3, low))},
                {0: pick((2, high), (3, mid)), 1: pick((0, low))},
            )
            for z in range(depth):
                content = {}
                for step, piece in patterns[z % 4].items():
                    tile = (z // 4 + step) % tiles
                    content[tile] = content[tile] + piece if tile in content else piece
                for tile in range(tiles):
                    out_ref[tap, z * 32 : (z + 1) * 32, tile * 128 : (tile + 1) * 128] = (
                        content.get(tile, zero).astype(bf16)
                    )
            return carry

        lax.fori_loop(0, 9, one, 0)

    bands(0, w1a_ref, 8)
    bands(1, w2_ref, 4)
    bands(2, w1b_ref, 8)
    bands(3, w0b_ref, 16)

    dest = dest_ref[...]
    upper = (iota((128, 128), 0) <= iota((128, 128), 1)).astype(f32).astype(bf16)
    before = (iota((16, 16), 1) < iota((16, 16), 0)).astype(f32).astype(bf16)
    rank = jnp.zeros((16, 128), f32)
    for k in range(9):
        chosen = (dest == k).astype(f32)
        marks = chosen.astype(bf16)
        inside = dot(marks, upper)
        earlier = jnp.sum(dot(before, marks), axis=1, keepdims=True)
        rank = rank + chosen * (inside - 1.0 + earlier)
    rank_ref[...] = rank.astype(i32)


def prepare(first, taps, dest):
    return pl.pallas_call(
        prep_kernel,
        out_shape=(
            jax.ShapeDtypeStruct((768, 512), bf16),
            jax.ShapeDtypeStruct((9, 256, 256), bf16),
            jax.ShapeDtypeStruct((9, 128, 128), bf16),
            jax.ShapeDtypeStruct((9, 256, 256), bf16),
            jax.ShapeDtypeStruct((9, 512, 512), bf16),
            jax.ShapeDtypeStruct((16, 128), i32),
        ),
        compiler_params=pltpu.CompilerParams(vmem_limit_bytes=24 * 2**20),
        cost_estimate=pl.CostEstimate(
            flops=5_000_000, bytes_accessed=20_000_000, transcendentals=0
        ),
    )(first, taps, dest)


def network_kernel(
    own_ref,
    low_ref,
    high_ref,
    w0a_ref,
    w1a_ref,
    w2_ref,
    w1b_ref,
    w0b_hbm,
    head_ref,
    pool_ref,
    grow_ref,
    pool1_ref,
    grow1_ref,
    rowpool_ref,
    rowgrow_ref,
    pos_ref,
    vel_ref,
    where_ref,
    dest_ref,
    rank_ref,
    out_ref,
    w0b_ref,
    even,
    odd,
    vm,
    v0,
    vp,
    e0_ref,
    p1_ref,
    p2_ref,
    u1_ref,
    ue_ref,
    uo_ref,
    um,
    u0,
    up,
    sem,
):
    fetch = pltpu.make_async_copy(w0b_hbm, w0b_ref, sem)
    fetch.start()

    low = low_ref[...].astype(f32)
    high = high_ref[...].astype(f32)
    own = own_ref[...].astype(f32)
    for parity, ref in ((0, even), (1, odd)):
        ref[0:6, :] = low[6 * parity : 6 * parity + 6]
        ref[6:22, :] = own[16 * parity : 16 * parity + 16]
        ref[22:28, :] = high[6 * parity : 6 * parity + 6]
        ref[28:40, :] = jnp.zeros((12, 2048), f32)

    def spread(value, targets):
        plain = value.astype(bf16)
        rolled = pltpu.roll(value, 2048 - 64, 1).astype(bf16)
        for column in range(COLS):
            if column % 2:
                piece = plain[:, 64 * (column + 1) : 64 * (column + 1) + 256]
            else:
                piece = rolled[:, 64 * column : 64 * column + 256]
            for ref, half in targets:
                begin = column * 64 + half * 32
                ref[begin : begin + 32, :] = piece

    spread(odd[0:32, :], ((vm, 0),))
    spread(even[1:33, :], ((vm, 1), (v0, 0)))
    spread(odd[1:33, :], ((v0, 1), (vp, 0)))
    spread(even[2:34, :], ((vp, 1),))

    p1_ref[0:8, :] = jnp.zeros((8, 256), f32)
    p1_ref[456:464, :] = jnp.zeros((8, 256), f32)

    def fine(block, carry):
        begin = pl.multiple_of(block * 256, 256)
        rows = pl.ds(begin, 256)
        total = dot(vm[rows, :], w0a_ref[0:256, :])
        total = total + dot(v0[rows, :], w0a_ref[256:512, :])
        total = total + dot(vp[rows, :], w0a_ref[512:768, :])
        value = gelu(total).astype(bf16)
        e0_ref[rows, :] = value
        quads = value.astype(f32).reshape(2, 4, 32, 512)
        summed = (quads[:, 0] + quads[:, 1]) + (quads[:, 2] + quads[:, 3])
        pooled = dot(summed.reshape(64, 512).astype(bf16), pool_ref[...])
        p1_ref[pl.ds(pl.multiple_of(8 + block * 64, 8), 64), :] = pooled.astype(bf16).astype(f32)
        return carry

    lax.fori_loop(0, 7, fine, 0)

    def middle(ref, blocks, weight_ref, stride, size, pad):
        shifted = [ref[pad + oy - 1 : pad + oy - 1 + size, :].astype(bf16) for oy in range(3)]
        total = None
        for ox in range(3):
            for oy in range(3):
                piece = shifted[oy][ox * stride : ox * stride + blocks * stride]
                term = dot(piece, weight_ref[ox * 3 + oy])
                total = term if total is None else total + term
        return gelu(total).astype(bf16)

    e1 = middle(p1_ref, 12, w1a_ref, 32, 448, 8)
    part = dot(rowpool_ref[...], e1).astype(bf16)
    p2_ref[0:8, :] = jnp.zeros((8, 128), f32)
    p2_ref[104:112, :] = jnp.zeros((8, 128), f32)
    p2_ref[8:104, :] = dot(part, pool1_ref[...]).astype(bf16).astype(f32)
    e2 = middle(p2_ref, 4, w2_ref, 16, 96, 8)
    grown = dot(dot(rowgrow_ref[...], e2).astype(bf16), grow1_ref[...])
    u1_ref[0:8, :] = jnp.zeros((8, 256), f32)
    u1_ref[264:272, :] = jnp.zeros((8, 256), f32)
    u1_ref[8:264, :] = (e1[64:320].astype(f32) + grown).astype(bf16).astype(f32)
    f1 = middle(u1_ref, 6, w1b_ref, 32, 256, 8)
    grown = dot(f1, grow_ref[...])
    for n in range(10):
        add = grown[((n + 1) // 2) * 32 : ((n + 1) // 2) * 32 + 32]
        begin = (n + 9) * 64
        ue_ref[...] = (e0_ref[begin : begin + 32, :].astype(f32) + add).astype(bf16).astype(f32)
        uo_ref[...] = (e0_ref[begin + 32 : begin + 64, :].astype(f32) + add).astype(bf16).astype(f32)
        at = n * 32
        even_here = ue_ref[5:21, :].astype(bf16)
        odd_here = uo_ref[5:21, :].astype(bf16)
        um[at : at + 16, :] = uo_ref[4:20, :].astype(bf16)
        um[at + 16 : at + 32, :] = even_here
        u0[at : at + 16, :] = even_here
        u0[at + 16 : at + 32, :] = odd_here
        up[at : at + 16, :] = odd_here
        up[at + 16 : at + 32, :] = ue_ref[6:22, :].astype(bf16)

    fetch.wait()
    total = None
    for ox in range(3):
        for oy, ref in enumerate((um, u0, up)):
            term = dot(ref[ox * 32 : ox * 32 + 256, :], w0b_ref[ox * 3 + oy])
            total = term if total is None else total + term
    change = dot(gelu(total).astype(bf16), head_ref[...])

    lane16 = iota((32, 128), 1) // 16
    tables = []
    for comp in range(3):
        table = jnp.zeros((32, 128), f32)
        for x in range(8):
            block = change[x * 32 : x * 32 + 32]
            shift = ((x - comp) * 16) % 128
            moved = pltpu.roll(block, shift, 1) if shift else block
            table = jnp.where(lane16 == x, moved, table)
        tables.append(table)
    cell = where_ref[...]
    y = jnp.bitwise_and(jnp.right_shift(cell, 4), 31)
    row = jnp.bitwise_and(y, 1) * 16 + jnp.right_shift(y, 1)
    lane = jnp.right_shift(cell, 9) * 16 + jnp.bitwise_and(cell, 15)
    kick = [jnp.zeros((16, 128), f32) for _ in range(3)]
    for r in range(32):
        here = row == r
        for comp in range(3):
            source = jnp.broadcast_to(tables[comp][r : r + 1], (16, 128))
            kick[comp] = jnp.where(here, jnp.take_along_axis(source, lane, axis=1), kick[comp])
    payload = []
    speeds = [vel_ref[comp] + kick[comp] for comp in range(3)]
    for comp in range(3):
        payload.append(pos_ref[comp] + DRIFT * speeds[comp])
    payload = payload + speeds

    rank = rank_ref[...]
    key = dest_ref[...] * 4 + jnp.right_shift(rank, 7)
    slot = jnp.bitwise_and(rank, 127)
    line = iota((216, 128), 0)
    line_key = (line // 24) * 4 + jnp.bitwise_and(line, 3)
    slots = iota((128, 128), 0)
    packed = jnp.zeros((216, 128), f32)
    for pair in range(8):
        left, right = [], []
        for c in (2 * pair, 2 * pair + 1):
            rows = jnp.concatenate(
                [jnp.broadcast_to(part[c : c + 1], (4, 128)) for part in payload], axis=0
            )
            full = jnp.concatenate([rows] * 9, axis=0)
            left.append(jnp.where(line_key == key[c : c + 1], full, 0.0).astype(bf16))
            right.append((slots == slot[c : c + 1]).astype(f32).astype(bf16))
        packed = packed + lax.dot_general(
            jnp.concatenate(left, axis=1),
            jnp.concatenate(right, axis=1),
            (((1,), (1,)), ((), ())),
            preferred_element_type=f32,
        )
    out_ref[...] = packed.astype(bf16)


def constants():
    pool = np.zeros((NZ * CH, NZ // 2 * CH), np.float32)
    for z in range(NZ):
        for c in range(CH):
            pool[z * CH + c, z // 2 * CH + c] = 1.0
    pool1 = pool[: 8 * CH, : 4 * CH]
    rowpool = np.zeros((96, 384), np.float32)
    for a in range(6):
        for s in range(12):
            for dx in range(2):
                for dy in range(2):
                    rowpool[a * 16 + s, (2 * a + dx) * 32 + 2 * s + 1 + dy] = 0.25
    rowgrow = np.zeros((256, 64), np.float32)
    for c in range(8):
        for r in range(3, 23):
            rowgrow[c * 32 + r, (c // 2) * 16 + (r - 1) // 2] = 1.0
    made = (pool * 0.125, pool.T, pool1 * 0.5, pool1.T, rowpool, rowgrow)
    return [jnp.asarray(np.ascontiguousarray(value), bf16) for value in made]


def network(own, low, high, weights, head, pos, vel, where, dest, rank):
    w0a, w1a, w2, w1b, w0b = weights
    pool, grow, pool1, grow1, rowpool, rowgrow = constants()
    vmem = pl.BlockSpec(memory_space=pltpu.VMEM)
    specs = [vmem] * 20
    specs[7] = pl.BlockSpec(memory_space=pl.ANY)
    return pl.pallas_call(
        network_kernel,
        out_shape=jax.ShapeDtypeStruct((216, 128), bf16),
        in_specs=specs,
        out_specs=vmem,
        scratch_shapes=[
            pltpu.VMEM((9, 512, 512), bf16),
            pltpu.VMEM((40, 2048), f32),
            pltpu.VMEM((40, 2048), f32),
            pltpu.VMEM((COLS * 64, 256), bf16),
            pltpu.VMEM((COLS * 64, 256), bf16),
            pltpu.VMEM((COLS * 64, 256), bf16),
            pltpu.VMEM((COLS * 64, 512), bf16),
            pltpu.VMEM((464, 256), f32),
            pltpu.VMEM((112, 128), f32),
            pltpu.VMEM((272, 256), f32),
            pltpu.VMEM((32, 512), f32),
            pltpu.VMEM((32, 512), f32),
            pltpu.VMEM((320, 512), bf16),
            pltpu.VMEM((320, 512), bf16),
            pltpu.VMEM((320, 512), bf16),
            pltpu.SemaphoreType.DMA,
        ],
        compiler_params=pltpu.CompilerParams(vmem_limit_bytes=40 * 2**20),
        cost_estimate=pl.CostEstimate(
            flops=3_000_000_000, bytes_accessed=10_000_000, transcendentals=1_000_000
        ),
    )(
        own, low, high, w0a, w1a, w2, w1b, w0b, head,
        pool, grow, pool1, grow1, rowpool, rowgrow,
        pos, vel, where, dest, rank,
    )


def exchange(value, count_x, count_y, rule):
    pairs = []
    for i in range(count_x):
        for j in range(count_y):
            a, b = rule(i, j)
            pairs.append((i * count_y + j, (a % count_x) * count_y + b % count_y))
    return lax.ppermute(value, ("gx", "gy"), pairs)


def body(
    position,
    velocity,
    cell_list,
    slot_weight,
    particle_cell,
    destination,
    lift,
    kernel_0a,
    kernel_1a,
    kernel_2,
    kernel_1b,
    kernel_0b,
    head,
):
    count_x, count_y = lax.axis_size("gx"), lax.axis_size("gy")
    first_core = lax.rem(lax.axis_index("gx"), 2) == 0

    def mate(value):
        return exchange(value, count_x, count_y, lambda i, j: (i ^ 1, j))

    def cross(value):
        return exchange(value, count_x, count_y, lambda i, j: (i + 1 if i % 2 else i - 1, j))

    def along_y(value):
        return exchange(value, count_x, count_y, lambda i, j: (i, j - 1 if i % 2 else j + 1))

    def either(if_first, if_second):
        return jnp.where(first_core, if_first, if_second)

    def cat(parts, axis):
        return jnp.concatenate(parts, axis=axis)

    combined = jnp.sum(
        kernel_0a.astype(f32)[:, :, :, None] * lift[None, None, :, :], axis=2
    )
    first = jnp.tile(combined.transpose(0, 2, 1), (1, 1, 4)).reshape(108, 128)
    taps = jnp.concatenate([kernel_1a, kernel_2, kernel_1b, kernel_0b], axis=0)
    taps = jnp.tile(taps.transpose(0, 2, 1), (1, 1, 4))
    eye = jnp.eye(NZ, dtype=bf16)
    headed = (eye[:, None, None, :] * head.T[None, :, :, None]).reshape(NZ * CH, 3 * NZ)
    headed = jnp.pad(headed, ((0, 0), (0, 128 - 3 * NZ)))
    dest = destination.reshape(16, 128)
    *weights, rank = prepare(first, taps, dest)

    mine = deposit(velocity, cell_list, slot_weight)
    theirs = mate(mine)
    chip = either(cat([mine, theirs], 1), cat([theirs, mine], 1))
    near = cross(either(chip[:, :768], chip[:, 256:]))
    far = mate(near)
    wide = cat([either(near, far), chip, either(far, near)], 1)
    rim = either(cat([wide[10:16], wide[26:32]], 0), cat([wide[0:6], wide[16:22]], 0))
    near = along_y(rim)
    far = mate(either(near[:, 512:], near[:, :2048]))
    near = either(near[:, :2048], near[:, 512:])
    own = either(wide[:, :2048], wide[:, 512:])
    low, high = either(near, far), either(far, near)

    packed = network(
        own,
        low,
        high,
        weights,
        headed,
        position.reshape(3, 16, 128),
        velocity.reshape(3, 16, 128),
        particle_cell.reshape(16, 128),
        dest,
        rank,
    )

    behind, level, ahead = packed[0:72], packed[72:144], packed[144:216]
    from_mate = mate(either(ahead, behind))
    from_cross = cross(either(behind, ahead))
    behind = either(from_mate, from_cross)
    ahead = either(from_cross, from_mate)
    groups = (behind, level, ahead)
    down = cat([group[0:24] for group in groups], 0)
    upward = cat([group[48:72] for group in groups], 0)
    passed = mate(either(down, upward))
    near = along_y(cat([either(upward, down), passed], 0))
    far = mate(near[72:])
    near = near[:72]
    upward, down = either(near, far), either(far, near)
    blocks = []
    for a in range(3):
        blocks.append(down[24 * a : 24 * a + 24])
        blocks.append(groups[a][24:48])
        blocks.append(upward[24 * a : 24 * a + 24])
    inbox = jnp.stack(blocks, axis=0).reshape(9, 6, CAP)
    return inbox.astype(f32).transpose(1, 0, 2).reshape(6, 9 * CAP)


def solution(mesh):
    in_specs = (
        P(None, ("gx", "gy")),
        P(None, ("gx", "gy")),
        P(None, "gx", "gy", None),
        P(None, "gx", "gy", None),
        P(("gx", "gy")),
        P(("gx", "gy"), None),
        P(),
        P(),
        P(),
        P(),
        P(),
        P(),
        P(),
    )
    out_specs = P(None, ("gx", "gy"))
    return jax.shard_map(body, mesh=mesh, in_specs=in_specs, out_specs=out_specs, check_vma=False)
```

profile of v0, /device:TPU:1, one launch (start us, length us, event | category | flops | bytes accessed | tf_op | source)
XLA Modules:
  0.0 58.8 jit_solution(16061803690715097902)
XLA Ops:
  0.0 2.0 %copy.41.cells_ref = s32[4,8,32,16]{3,2,1,0:T(8,128)} copy(s32[4,8,32,16]{2,3,1,0:T(8,128)} %param.21) | data formatting | bytes 131072 | tf_op args[2]
  2.0 2.0 %copy.42.weight_ref = f32[4,8,32,16]{3,2,1,0:T(8,128)} copy(f32[4,8,32,16]{2,3,1,0:T(8,128)} %param.22) | data formatting | bytes 131072 | tf_op args[3]
  4.1 4.7 %shard_map.181 = bf16[32,512]{1,0:T(8,128)(2,1)} custom-call(f32[3,2048]{1,0:T(4,128)} %vel_ref.1, s32[4,8,32,16]{3,2,1,0:T(8,128)} %copy.41.cells_ref, f32[4,8,32,16]{3,2,1,0:T(8,128)} %copy.42.weight_ref), custom_call_target="tpu_custom_call" | custom-call | flops 2000000 | bytes 1000000 | tf_op jit(solution)/shard_map/pallas_call | solution.py:70
  8.8 3.2 %collective-permute-start = (bf16[32,512]{1,0:T(8,128)(2,1)}, bf16[32,512]{1,0:T(8,128)(2,1)S(1)}, u32[]{:S(2)}, u32[]{:S(2)}) collective-permute-start(bf16[32,512]{1,0:T(8,128)(2,1)} %shard_map.181), channel_id=1, source_target_pairs={{0,8},{1,9},{2,10},{3,11},{4,12},{5,13},{6,14},{7,15},{8,0},{9,1},... | collective-permute-start | bytes 98312 | tf_op jit(solution)/shard_map/ppermute | solution.py:425
  12.0 1.1 %collective-permute-done = bf16[32,512]{1,0:T(8,128)(2,1)S(1)} collective-permute-done((bf16[32,512]{1,0:T(8,128)(2,1)}, bf16[32,512]{1,0:T(8,128)(2,1)S(1)}, u32[]{:S(2)}, u32[]{:S(2)}) %collective-permute-start) | collective-permute-done | bytes 32800 | tf_op jit(solution)/shard_map/ppermute | solution.py:425
  13.1 0.8 %maximum_select_fusion.1 = bf16[32,1024]{1,0:T(8,128)(2,1)S(1)} fusion(bf16[32,512]{1,0:T(8,128)(2,1)S(1)} %collective-permute-done, bf16[32,512]{1,0:T(8,128)(2,1)} %shard_map.181, pred[]{:T(512)S(6)} %eq.10), kind=kLoop, calls=%fused_computation.6 | loop fusion | flops 294912 | bytes 131073 | tf_op jit(solution)/shard_map/jit(_where)/select_n | solution.py:456
  13.9 0.1 collective-permute-start.1
  14.0 0.0 copy-done.16
  14.0 0.1 broadcast_multiply_fusion
  14.1 0.0 copy-done.12
  14.2 3.3 %collective-permute-done.1 = bf16[32,768]{1,0:T(8,128)(2,1)S(1)} collective-permute-done((bf16[32,768]{1,0:T(8,128)(2,1)S(1)}, bf16[32,768]{1,0:T(8,128)(2,1)S(1)}, u32[]{:S(2)}, u32[]{:S(2)}) %collective-permute-start.1) | collective-permute-done | bytes 49184 | tf_op jit(solution)/shard_map/ppermute | solution.py:425
  17.5 3.7 %collective-permute-start.2 = (bf16[32,768]{1,0:T(8,128)(2,1)S(1)}, bf16[32,768]{1,0:T(8,128)(2,1)S(1)}, u32[]{:S(2)}, u32[]{:S(2)}) collective-permute-start(bf16[32,768]{1,0:T(8,128)(2,1)S(1)} %collective-permute-done.1), channel_id=1, source_target_pairs={{0,8},{1,9},{2,10},{3,11},{4,12},{5,13},{6,14},{7,15},{8,0},{9,1},... | collective-permute-start | bytes 147464 | tf_op jit(solution)/shard_map/ppermute | solution.py:425
  21.2 0.0 copy-done.15
  21.2 0.6 multiply_reduce_fusion
  21.8 0.0 copy-done.8
  21.8 0.4 copy.43
  22.1 0.0 copy-done.9
  22.2 0.4 copy.44
  22.5 0.0 copy-done.10
  22.5 0.4 copy.45
  22.9 0.0 copy-done.11
  22.9 0.4 copy.46
  23.3 0.0 collective-permute-done.2
  23.3 0.1 maximum_select_fusion
  23.4 3.9 %collective-permute-start.3 = (bf16[12,2560]{1,0:T(8,128)(2,1)S(1)}, bf16[12,2560]{1,0:T(8,128)(2,1)S(1)}, u32[]{:S(2)}, u32[]{:S(2)}) collective-permute-start(bf16[12,2560]{1,0:T(8,128)(2,1)S(1)} %maximum_select_fusion), channel_id=1, source_target_pairs={{0,1},{1,2},{2,3},{3,4},{4,5},{5,6},{6,7},{7,0},{8,15},{9,8},{10,9... | collective-permute-start | bytes 184328 | tf_op jit(solution)/shard_map/ppermute | solution.py:425
  27.3 0.4 maximum_bitcast_fusion
  27.7 0.1 copy.47
  27.8 0.2 tile.19
  28.0 0.0 copy-start.13
  28.0 0.0 copy-start.14
  28.0 0.0 copy-start
  28.0 0.9 %copy.48.taps_ref = bf16[108,32,128]{2,1,0:T(8,128)(2,1)S(1)} copy(bf16[108,32,128]{0,2,1:T(8,128)(2,1)S(1)} %bitcast.29) | data formatting | bytes 1769472 | tf_op jit(solution)/shard_map/tile | solution.py:466
  28.9 0.0 copy-start.1
  28.9 0.0 copy-start.2
  29.0 0.0 copy-start.3
  29.0 0.0 copy-start.4
  29.0 0.0 copy-start.5
  29.0 0.0 copy-start.6
  29.0 0.0 copy-start.7
  29.1 0.1 tile.18.first_ref
  29.2 0.2 mul.36
  29.4 0.1 copy.49
  29.5 0.0 copy-done.13
  29.6 0.0 copy-done.14
  29.6 0.0 copy-done
  29.6 1.6 %shard_map.182 = (bf16[768,512]{1,0:T(8,128)(2,1)S(1)}, bf16[9,256,256]{2,1,0:T(8,128)(2,1)S(1)}, bf16[9,128,128]{2,1,0:T(8,128)(2,1)S(1)}, bf16[9,256,256]{2,1,...) custom-call(f32[108,128]{1,0:T(8,128)S(1)} %tile.18.first_ref, ...), custom_call_target="tpu_custom_call" | custom-call | flops 5000000 | bytes 20000000 | tf_op jit(solution)/shard_map/pallas_call | solution.py:159
  31.2 0.0 collective-permute-done.3
  31.2 0.3 collective-permute-start.4
  31.5 1.2 %collective-permute-done.4 = bf16[12,2048]{1,0:T(8,128)(2,1)S(1)} collective-permute-done((bf16[12,2048]{1,0:T(8,128)(2,1)S(1)}, bf16[12,2048]{1,0:T(8,128)(2,1)S(1)}, u32[]{:S(2)}, u32[]{:S(2)}) %collective-permute-start.4) | collective-permute-done | bytes 49184 | tf_op jit(solution)/shard_map/ppermute | solution.py:425
  32.7 0.0 copy-done.1
  32.8 0.0 copy-done.2
  32.8 0.0 copy-done.3
  32.8 10.5 %shard_map.183 = bf16[216,128]{1,0:T(8,128)(2,1)S(1)} custom-call(bf16[32,2048]{1,0:T(8,128)(2,1)S(1)} %slice_select_fusion.own_ref, bf16[12,2048]{1,0:T(8,128)(2,1)S(1)} %get-tuple-element.22.low_ref, bf16[12,2048]{1,0:T(8,128)(2,1)S(1)} %get-tuple-element.21.high_ref, bf16[768,512]{1,0:T(8,128)(2,1)S(1)} %get-tuple-element.11.w0a_ref, ...), custom_call_target="tpu_custom_call" | custom-call | flops 3000000000 | bytes 10000000 | tf_op jit(solution)/shard_map/pallas_call | solution.py:385
  43.4 0.2 collective-permute-start.5
  43.6 0.0 collective-permute-start.6
  43.6 1.0 %collective-permute-done.5 = bf16[72,128]{1,0:T(8,128)(2,1)S(1)} collective-permute-done((bf16[72,128]{1,0:T(8,128)(2,1)S(1)}, bf16[72,128]{1,0:T(8,128)(2,1)S(1)}, u32[]{:S(2)}, u32[]{:S(2)}) %collective-permute-start.5) | collective-permute-done | bytes 18464 | tf_op jit(solution)/shard_map/ppermute | solution.py:425
  44.6 2.2 %collective-permute-done.6 = bf16[72,128]{1,0:T(8,128)(2,1)S(1)} collective-permute-done((bf16[72,128]{1,0:T(8,128)(2,1)S(1)}, bf16[72,128]{1,0:T(8,128)(2,1)S(1)}, u32[]{:S(2)}, u32[]{:S(2)}) %collective-permute-start.6) | collective-permute-done | bytes 18464 | tf_op jit(solution)/shard_map/ppermute | solution.py:425
  46.8 3.8 %collective-permute-start.7 = (bf16[72,128]{1,0:T(8,128)(2,1)S(1)}, bf16[72,128]{1,0:T(8,128)(2,1)S(1)}, u32[]{:S(2)}, u32[]{:S(2)}) collective-permute-start(bf16[72,128]{1,0:T(8,128)(2,1)S(1)} %get-tuple-element.33), channel_id=1, source_target_pairs={{0,8},{1,9},{2,10},{3,11},{4,12},{5,13},{6,14},{7,15},{8,0},{9,1},... | collective-permute-start | bytes 55304 | tf_op jit(solution)/shard_map/ppermute | solution.py:425
  50.6 0.8 %collective-permute-done.7 = bf16[72,128]{1,0:T(8,128)(2,1)S(1)} collective-permute-done((bf16[72,128]{1,0:T(8,128)(2,1)S(1)}, bf16[72,128]{1,0:T(8,128)(2,1)S(1)}, u32[]{:S(2)}, u32[]{:S(2)}) %collective-permute-start.7) | collective-permute-done | bytes 18464 | tf_op jit(solution)/shard_map/ppermute | solution.py:425
  51.5 0.7 %collective-permute-start.8 = (bf16[144,128]{1,0:T(8,128)(2,1)S(1)}, bf16[144,128]{1,0:T(8,128)(2,1)S(1)}, u32[]{:S(2)}, u32[]{:S(2)}) collective-permute-start(bf16[144,128]{1,0:T(8,128)(2,1)S(1)} %pad_maximum_fusion.1), channel_id=1, source_target_pairs={{0,1},{1,2},{2,3},{3,4},{4,5},{5,6},{6,7},{7,0},{8,15},{9,8},{10,9... | collective-permute-start | bytes 110600 | tf_op jit(solution)/shard_map/ppermute | solution.py:425
  52.2 2.1 %collective-permute-done.8 = bf16[144,128]{1,0:T(8,128)(2,1)S(1)} collective-permute-done((bf16[144,128]{1,0:T(8,128)(2,1)S(1)}, bf16[144,128]{1,0:T(8,128)(2,1)S(1)}, u32[]{:S(2)}, u32[]{:S(2)}) %collective-permute-start.8) | collective-permute-done | bytes 36896 | tf_op jit(solution)/shard_map/ppermute | solution.py:425
  54.3 2.7 %collective-permute-start.9 = (bf16[72,128]{1,0:T(8,128)(2,1)S(1)}, bf16[72,128]{1,0:T(8,128)(2,1)S(1)}, u32[]{:S(2)}, u32[]{:S(2)}) collective-permute-start(bf16[72,128]{1,0:T(8,128)(2,1)S(1)} %slice.140), channel_id=1, source_target_pairs={{0,8},{1,9},{2,10},{3,11},{4,12},{5,13},{6,14},{7,15},{8,0},{9,1},... | collective-permute-start | bytes 55304 | tf_op jit(solution)/shard_map/ppermute | solution.py:425
  57.0 0.8 %collective-permute-done.9 = bf16[72,128]{1,0:T(8,128)(2,1)S(1)} collective-permute-done((bf16[72,128]{1,0:T(8,128)(2,1)S(1)}, bf16[72,128]{1,0:T(8,128)(2,1)S(1)}, u32[]{:S(2)}, u32[]{:S(2)}) %collective-permute-start.9) | collective-permute-done | bytes 18464 | tf_op jit(solution)/shard_map/ppermute | solution.py:425
  58.1 0.7 %reshape.68 = f32[9,6,512]{2,1,0:T(8,128)} convert(bf16[9,6,512]{2,1,0:T(8,128)(2,1)S(1)} %constant_dynamic-update-slice_fusion) | non-fusion elementwise | flops 27648 | bytes 165888 | tf_op jit(solution)/shard_map/reshape | solution.py:518
  (52 shorter events, 0.5 us)
Async XLA Ops:
  0.0 14.0 %copy-start.16 = (bf16[3,32]{1,0:T(4,128)(2,1)S(1)}, bf16[3,32]{1,0:T(4,128)(2,1)}, u32[]{:S(2)}) copy-start(bf16[3,32]{1,0:T(4,128)(2,1)} %param.31) | copy-start | bytes 580
  0.0 14.1 %copy-start.12 = (bf16[27,32,32]{2,1,0:T(8,128)(2,1)S(1)}, bf16[27,32,32]{2,1,0:T(8,128)(2,1)}, u32[]{:S(2)}) copy-start(bf16[27,32,32]{2,1,0:T(8,128)(2,1)} %param.26) | copy-start | bytes 165892
  0.0 21.2 %copy-start.15 = (f32[32,4]{0,1:T(4,128)S(1)}, f32[32,4]{0,1:T(4,128)}, u32[]{:S(2)}) copy-start(f32[32,4]{0,1:T(4,128)} %param.25) | copy-start | bytes 1540
  2.0 19.8 %copy-start.8 = (bf16[27,32,32]{2,1,0:T(8,128)(2,1)S(1)}, bf16[27,32,32]{2,1,0:T(8,128)(2,1)}, u32[]{:S(2)}) copy-start(bf16[27,32,32]{2,1,0:T(8,128)(2,1)} %param.27) | copy-start | bytes 165892
  4.1 18.1 %copy-start.9 = (bf16[27,32,32]{2,1,0:T(8,128)(2,1)S(1)}, bf16[27,32,32]{2,1,0:T(8,128)(2,1)}, u32[]{:S(2)}) copy-start(bf16[27,32,32]{2,1,0:T(8,128)(2,1)} %param.28) | copy-start | bytes 165892
  4.1 18.5 %copy-start.10 = (bf16[27,32,32]{2,1,0:T(8,128)(2,1)S(1)}, bf16[27,32,32]{2,1,0:T(8,128)(2,1)}, u32[]{:S(2)}) copy-start(bf16[27,32,32]{2,1,0:T(8,128)(2,1)} %param.29) | copy-start | bytes 165892
  8.7 14.1 %copy-start.11 = (bf16[27,32,32]{2,1,0:T(8,128)(2,1)S(1)}, bf16[27,32,32]{2,1,0:T(8,128)(2,1)}, u32[]{:S(2)}) copy-start(bf16[27,32,32]{2,1,0:T(8,128)(2,1)} %param.30) | copy-start | bytes 165892
  8.8 4.3 %collective-permute-start = (bf16[32,512]{1,0:T(8,128)(2,1)}, bf16[32,512]{1,0:T(8,128)(2,1)S(1)}, u32[]{:S(2)}, u32[]{:S(2)}) collective-permute-start(bf16[32,512]{1,0:T(8,128)(2,1)} %shard_map.181), channel_id=1, source_target_pairs={{0,8},{1,9},{2,10},{3,11},{4,12},{5,13},{6,14},{7,15},{8,0},{9,1},... | collective-permute-start | bytes 98312 | tf_op jit(solution)/shard_map/ppermute | solution.py:425
  13.9 3.6 %collective-permute-start.1 = (bf16[32,768]{1,0:T(8,128)(2,1)S(1)}, bf16[32,768]{1,0:T(8,128)(2,1)S(1)}, u32[]{:S(2)}, u32[]{:S(2)}) collective-permute-start(bf16[32,768]{1,0:T(8,128)(2,1)S(1)} %slice_select_fusion.1), channel_id=1, source_target_pairs={{0,248},{1,249},{2,250},{3,251},{4,252},{5,253},{6,254},{7,255},{8... | collective-permute-start | bytes 147464 | tf_op jit(solution)/shard_map/ppermute | solution.py:425
  17.5 5.7 %collective-permute-start.2 = (bf16[32,768]{1,0:T(8,128)(2,1)S(1)}, bf16[32,768]{1,0:T(8,128)(2,1)S(1)}, u32[]{:S(2)}, u32[]{:S(2)}) collective-permute-start(bf16[32,768]{1,0:T(8,128)(2,1)S(1)} %collective-permute-done.1), channel_id=1, source_target_pairs={{0,8},{1,9},{2,10},{3,11},{4,12},{5,13},{6,14},{7,15},{8,0},{9,1},... | collective-permute-start | bytes 147464 | tf_op jit(solution)/shard_map/ppermute | solution.py:425
  23.4 7.8 %collective-permute-start.3 = (bf16[12,2560]{1,0:T(8,128)(2,1)S(1)}, bf16[12,2560]{1,0:T(8,128)(2,1)S(1)}, u32[]{:S(2)}, u32[]{:S(2)}) collective-permute-start(bf16[12,2560]{1,0:T(8,128)(2,1)S(1)} %maximum_select_fusion), channel_id=1, source_target_pairs={{0,1},{1,2},{2,3},{3,4},{4,5},{5,6},{6,7},{7,0},{8,15},{9,8},{10,9... | collective-permute-start | bytes 184328 | tf_op jit(solution)/shard_map/ppermute | solution.py:425
  28.0 1.6 %copy-start.13 = (f32[3,2048]{1,0:T(4,128)S(1)}, f32[3,2048]{1,0:T(4,128)}, u32[]{:S(2)}) copy-start(f32[3,2048]{1,0:T(4,128)} %vel_ref.1) | copy-start | bytes 73732
  28.0 1.6 %copy-start.14 = (f32[3,2048]{1,0:T(4,128)S(1)}, f32[3,2048]{1,0:T(4,128)}, u32[]{:S(2)}) copy-start(f32[3,2048]{1,0:T(4,128)} %param.19) | copy-start | bytes 73732
  28.0 1.6 %copy-start = (s32[2048,1]{0,1:T(1,128)S(1)}, s32[2048,1]{0,1:T(1,128)}, u32[]{:S(2)}) copy-start(s32[2048,1]{0,1:T(1,128)} %param.24) | copy-start | bytes 24580
  28.9 3.8 %copy-start.1 = (s32[2048]{0:T(1024)S(1)}, s32[2048]{0:T(1024)}, u32[]{:S(2)}) copy-start(s32[2048]{0:T(1024)} %param.23) | copy-start | bytes 24580
  28.9 3.8 %copy-start.2 = (bf16[512,256]{1,0:T(8,128)(2,1)S(1)}, bf16[512,256]{1,0:T(8,128)(2,1)}, u32[]{:S(2)}) copy-start(bf16[512,256]{1,0:T(8,128)(2,1)} %constant.28.clone.pool_ref) | copy-start | bytes 786436
  29.0 3.8 %copy-start.3 = (bf16[256,512]{1,0:T(8,128)(2,1)S(1)}, bf16[256,512]{1,0:T(8,128)(2,1)}, u32[]{:S(2)}) copy-start(bf16[256,512]{1,0:T(8,128)(2,1)} %constant.29.clone.grow_ref) | copy-start | bytes 786436
  29.0 3.8 %copy-start.4 = (bf16[96,384]{1,0:T(8,128)(2,1)S(1)}, bf16[96,384]{1,0:T(8,128)(2,1)}, u32[]{:S(2)}) copy-start(bf16[96,384]{1,0:T(8,128)(2,1)} %constant.32.clone.rowpool_ref) | copy-start | bytes 221188
  29.0 3.8 %copy-start.5 = (bf16[256,128]{1,0:T(8,128)(2,1)S(1)}, bf16[256,128]{1,0:T(8,128)(2,1)}, u32[]{:S(2)}) copy-start(bf16[256,128]{1,0:T(8,128)(2,1)} %constant.30.clone.pool1_ref) | copy-start | bytes 196612
  29.0 3.8 %copy-start.6 = (bf16[128,256]{1,0:T(8,128)(2,1)S(1)}, bf16[128,256]{1,0:T(8,128)(2,1)}, u32[]{:S(2)}) copy-start(bf16[128,256]{1,0:T(8,128)(2,1)} %constant.31.clone.grow1_ref) | copy-start | bytes 196612
  29.0 3.8 %copy-start.7 = (bf16[256,64]{1,0:T(8,128)(2,1)S(1)}, bf16[256,64]{1,0:T(8,128)(2,1)}, u32[]{:S(2)}) copy-start(bf16[256,64]{1,0:T(8,128)(2,1)} %constant.33.clone.rowgrow_ref) | copy-start | bytes 98308
  31.2 1.5 %collective-permute-start.4 = (bf16[12,2048]{1,0:T(8,128)(2,1)S(1)}, bf16[12,2048]{1,0:T(8,128)(2,1)S(1)}, u32[]{:S(2)}, u32[]{:S(2)}) collective-permute-start(bf16[12,2048]{1,0:T(8,128)(2,1)S(1)} %broadcast_select_fusion.2), channel_id=1, source_target_pairs={{0,8},{1,9},{2,10},{3,11},{4,12},{5,13},{6,14},{7,15},{8,0},{9,1},... | collective-permute-start | bytes 147464 | tf_op jit(solution)/shard_map/ppermute | solution.py:425
  43.4 1.3 %collective-permute-start.5 = (bf16[72,128]{1,0:T(8,128)(2,1)S(1)}, bf16[72,128]{1,0:T(8,128)(2,1)S(1)}, u32[]{:S(2)}, u32[]{:S(2)}) collective-permute-start(bf16[72,128]{1,0:T(8,128)(2,1)S(1)} %get-tuple-element.30), channel_id=1, source_target_pairs={{0,8},{1,9},{2,10},{3,11},{4,12},{5,13},{6,14},{7,15},{8,0},{9,1},... | collective-permute-start | bytes 55304 | tf_op jit(solution)/shard_map/ppermute | solution.py:425
  43.6 3.2 %collective-permute-start.6 = (bf16[72,128]{1,0:T(8,128)(2,1)S(1)}, bf16[72,128]{1,0:T(8,128)(2,1)S(1)}, u32[]{:S(2)}, u32[]{:S(2)}) collective-permute-start(bf16[72,128]{1,0:T(8,128)(2,1)S(1)} %get-tuple-element.31), channel_id=1, source_target_pairs={{0,248},{1,249},{2,250},{3,251},{4,252},{5,253},{6,254},{7,255},{8... | collective-permute-start | bytes 55304 | tf_op jit(solution)/shard_map/ppermute | solution.py:425
  46.8 4.6 %collective-permute-start.7 = (bf16[72,128]{1,0:T(8,128)(2,1)S(1)}, bf16[72,128]{1,0:T(8,128)(2,1)S(1)}, u32[]{:S(2)}, u32[]{:S(2)}) collective-permute-start(bf16[72,128]{1,0:T(8,128)(2,1)S(1)} %get-tuple-element.33), channel_id=1, source_target_pairs={{0,8},{1,9},{2,10},{3,11},{4,12},{5,13},{6,14},{7,15},{8,0},{9,1},... | collective-permute-start | bytes 55304 | tf_op jit(solution)/shard_map/ppermute | solution.py:425
  51.5 2.8 %collective-permute-start.8 = (bf16[144,128]{1,0:T(8,128)(2,1)S(1)}, bf16[144,128]{1,0:T(8,128)(2,1)S(1)}, u32[]{:S(2)}, u32[]{:S(2)}) collective-permute-start(bf16[144,128]{1,0:T(8,128)(2,1)S(1)} %pad_maximum_fusion.1), channel_id=1, source_target_pairs={{0,1},{1,2},{2,3},{3,4},{4,5},{5,6},{6,7},{7,0},{8,15},{9,8},{10,9... | collective-permute-start | bytes 110600 | tf_op jit(solution)/shard_map/ppermute | solution.py:425
  54.3 3.5 %collective-permute-start.9 = (bf16[72,128]{1,0:T(8,128)(2,1)S(1)}, bf16[72,128]{1,0:T(8,128)(2,1)S(1)}, u32[]{:S(2)}, u32[]{:S(2)}) collective-permute-start(bf16[72,128]{1,0:T(8,128)(2,1)S(1)} %slice.140), channel_id=1, source_target_pairs={{0,8},{1,9},{2,10},{3,11},{4,12},{5,13},{6,14},{7,15},{8,0},{9,1},... | collective-permute-start | bytes 55304 | tf_op jit(solution)/shard_map/ppermute | solution.py:425
where the time goes:
time: 59 us; the launch traced here: 58.8 us
  starting transfers between devices  18.6 us (32%)
  Pallas kernels  16.8 us (28%)
  waiting for transfers between devices  12.5 us (21%)
  local copies, waits for them, and re-layouts  7.51 us (13%)
  other arithmetic  2.8 us (5%)
    ppermute x10, starting transfers between devices, exchange(): return lax.ppermute(value, ('gx', 'gy'), pairs)  18.6 us
    ppermute x10, waiting for transfers between devices, exchange(): return lax.ppermute(value, ('gx', 'gy'), pairs)  12.5 us
    pallas_call x1, Pallas kernels, network(): pl.pallas_call(network_kernel, out_shape=jax.ShapeDtypeStruct((216, 128),...  10.5 us
    unnamed x50, local copies, waits for them, and re-layouts  5.6 us
    pallas_call x1, Pallas kernels, deposit(): pl.pallas_call(deposit_kernel, out_shape=jax.ShapeDtypeStruct((32, 512),...  4.69 us
    pallas_call x1, Pallas kernels, prepare(): pl.pallas_call(prep_kernel, out_shape=(jax.ShapeDtypeStruct((768, 512), b...  1.55 us
  transfers between devices with their start and end apart: 10, of which 8 were waited for; matrix products, arithmetic and copies ran while one was open for 7% of the time, Pallas kernels for 3%

commit v1 on v0

v1 whole, which is shorter than its diff:
```python
import jax
import jax.numpy as jnp
import numpy as np
from jax import lax
from jax.experimental import pallas as pl
from jax.experimental.pallas import tpu as pltpu
from jax.sharding import PartitionSpec as P

f32 = jnp.float32
bf16 = jnp.bfloat16
i32 = jnp.int32

CAP = 512
DRIFT = 0.25
CH = 32
NZ = 16
COLS = 28


def iota(shape, dim):
    return lax.broadcasted_iota(i32, shape, dim)


def dot(a, b):
    return jnp.dot(a, b, preferred_element_type=f32)


def gelu(x):
    inner = x * (0.7978845608028654 + 0.035677408136300125 * (x * x))
    return (0.5 * x) * (1.0 + jnp.tanh(inner))


def pick_lanes(table, lane):
    numbers = lax.GatherDimensionNumbers(
        offset_dims=(),
        collapsed_slice_dims=(1,),
        start_index_map=(1,),
        operand_batching_dims=(0,),
        start_indices_batching_dims=(0,),
    )
    return lax.gather(
        table,
        lane[..., None],
        numbers,
        (1, 1),
        mode=lax.GatherScatterMode.PROMISE_IN_BOUNDS,
    )


def fetch_all(pairs, sems):
    copies = [
        pltpu.make_async_copy(source, target, sems.at[index])
        for index, (source, target) in enumerate(pairs)
    ]
    for copy in copies:
        copy.start()
    return copies


def deposit_kernel(
    vel_hbm, cells_hbm, weight_hbm, out_ref, stage, vel_ref, cells_ref, weight_ref, sems
):
    fetch_vel, fetch_cells, fetch_weight = fetch_all(
        ((vel_hbm, vel_ref), (cells_hbm, cells_ref), (weight_hbm, weight_ref)), sems
    )

    def dense(ref, s):
        return jnp.concatenate(
            [jnp.concatenate([ref[s, 2 * a + b] for a in range(4)], axis=1) for b in range(2)],
            axis=0,
        )

    fetch_vel.wait()
    fetch_cells.wait()
    entries, picked = [], []
    for s in range(4):
        entry = dense(cells_ref, s)
        lane = jnp.bitwise_and(entry, 127)
        row = jnp.right_shift(entry, 7)
        found = [jnp.zeros((32, 128), f32) for _ in range(3)]
        for r in range(16):
            here = row == r
            for q in range(3):
                table = jnp.broadcast_to(vel_ref[q : q + 1, r * 128 : (r + 1) * 128], (32, 128))
                found[q] = jnp.where(here, pick_lanes(table, lane), found[q])
        entries.append(entry)
        picked.append(found)
    fetch_weight.wait()
    totals = [jnp.zeros((32, 128), f32) for _ in range(4)]
    for s in range(4):
        weight = dense(weight_ref, s)
        totals[0] = totals[0] + jnp.where(entries[s] < 2048, weight, 0.0)
        for q in range(3):
            totals[q + 1] = totals[q + 1] + weight * picked[s][q]
    stage[...] = jnp.concatenate(
        [totals[q][b * 16 : b * 16 + 16] for b in range(2) for q in range(4)], axis=0
    ).T
    for t in range(4):
        for parity in range(2):
            lanes = slice((t % 2) * 128, (t % 2) * 128 + 128)
            out_ref[t // 2, parity * 16 : parity * 16 + 16, lanes] = stage[
                pl.ds(t * 32 + parity, 16, stride=2), :
            ].astype(bf16)


def deposit(velocity, cells, weight):
    return pl.pallas_call(
        deposit_kernel,
        out_shape=pltpu.VMEM((2, 32, 256), bf16),
        in_specs=[pl.BlockSpec(memory_space=pltpu.HBM)] * 3,
        out_specs=pl.BlockSpec(memory_space=pltpu.VMEM),
        scratch_shapes=[
            pltpu.VMEM((128, 128), f32),
            pltpu.VMEM((3, 2048), f32),
            pltpu.VMEM((4, 8, 16, 32), i32),
            pltpu.VMEM((4, 8, 16, 32), f32),
            pltpu.SemaphoreType.DMA((3,)),
        ],
        cost_estimate=pl.CostEstimate(flops=2_000_000, bytes_accessed=1_000_000, transcendentals=0),
    )(velocity, jnp.swapaxes(cells, 2, 3), jnp.swapaxes(weight, 2, 3))


def contract_last(a, b):
    return lax.dot_general(a, b, (((1,), (1,)), ((), ())), preferred_element_type=f32)


def first_kernel(lift_hbm, kernel_hbm, after_ref, w0a_ref, lift_ref, kernel_ref, sems):
    fetch_lift, fetch = fetch_all(((lift_hbm, lift_ref), (kernel_hbm, kernel_ref)), sems)
    fetch_lift.wait()
    rest = lift_ref[...]
    terms = []
    for _ in range(3):
        term = rest.astype(bf16).astype(f32)
        terms.append(term)
        rest = rest - term
    terms = jnp.concatenate(terms + [jnp.zeros((4, 32), f32)], axis=0).astype(bf16)
    row = iota((16, 128), 0)
    masks = []
    for t in range(4):
        diff = jnp.bitwise_and(row - (4 * t + iota((16, 128), 1) // 32), 15)
        masks.append((diff == 15, diff == 0, diff == 1))
    fetch.wait()
    for ox in range(3):
        for oy in range(3):
            at = 9 * ox + 3 * oy
            repeated = [kernel_ref[at + oz] for oz in range(3) for _ in range(4)]
            parts = contract_last(terms, jnp.concatenate(repeated, axis=0))
            both = parts[0:4] + parts[4:8] + parts[8:12]
            for q in range(4):
                low, mid, high = (
                    jnp.broadcast_to(both[q : q + 1, oz * 128 : oz * 128 + 128], (16, 128))
                    for oz in range(3)
                )
                for t in range(4):
                    below, same, above = masks[t]
                    piece = jnp.where(
                        same, mid, jnp.where(below, low, jnp.where(above, high, 0.0))
                    )
                    begin = oy * 256 + ox * 64 + q * 16
                    w0a_ref[begin : begin + 16, t * 128 : (t + 1) * 128] = piece.astype(bf16)
    for oy in range(3):
        w0a_ref[oy * 256 + 192 : oy * 256 + 256, :] = jnp.zeros((64, 512), bf16)


def bands(kernel_ref, out_ref, depth):
    group = iota((32, 128), 1) // 32
    zero = jnp.zeros((32, 128), f32)
    tiles = depth // 4

    def one(tap, carry):
        row = jnp.concatenate(
            [kernel_ref[3 * tap + oz].astype(f32) for oz in range(3)] + [zero[:, 0:32]], axis=1
        )
        turned = jnp.concatenate([row] * 4, axis=0).T
        low, mid, high = (turned[oz * 32 : oz * 32 + 32] for oz in range(3))

        def pick(*wanted):
            value = zero
            for index, piece in wanted:
                value = jnp.where(group == index, piece, value)
            return value

        patterns = (
            {0: pick((0, mid), (1, low)), -1: pick((3, high))},
            {0: pick((0, high), (1, mid), (2, low))},
            {0: pick((1, high), (2, mid), (3, low))},
            {0: pick((2, high), (3, mid)), 1: pick((0, low))},
        )
        for z in range(depth):
            content = {}
            for step, piece in patterns[z % 4].items():
                tile = (z // 4 + step) % tiles
                content[tile] = content[tile] + piece if tile in content else piece
            for tile in range(tiles):
                out_ref[tap, z * 32 : (z + 1) * 32, tile * 128 : (tile + 1) * 128] = (
                    content.get(tile, zero).astype(bf16)
                )
        return carry

    lax.fori_loop(0, 9, one, 0, unroll=3)


def middle_kernel(k1a_hbm, k2_hbm, after_ref, w1a_ref, w2_ref, k1a_ref, k2_ref, sems):
    fetches = fetch_all(((k1a_hbm, k1a_ref), (k2_hbm, k2_ref)), sems)
    for fetch, ref, out_ref, depth in zip(fetches, (k1a_ref, k2_ref), (w1a_ref, w2_ref), (8, 4)):
        fetch.wait()
        bands(ref, out_ref, depth)


def last_kernel(
    head_hbm, dest_hbm, k1b_hbm, k0b_hbm, after_ref, w1b_ref, w0b_ref, headed_ref, rank_ref,
    head_ref, dest_ref, k1b_ref, k0b_ref, sems,
):
    fetches = fetch_all(
        (
            (head_hbm, head_ref), (dest_hbm, dest_ref), (k1b_hbm, k1b_ref), (k0b_hbm, k0b_ref)
        ),
        sems,
    )
    for fetch in fetches:
        fetch.wait()
    bands(k1b_ref, w1b_ref, 8)
    bands(k0b_ref, w0b_ref, 16)

    row16 = iota((16, 128), 0)
    names = head_ref[...].astype(f32)
    names = jnp.concatenate([names] * 4, axis=1)
    for t in range(4):
        same = row16 == 4 * t + iota((16, 128), 1) // 32
        rows = [
            jnp.where(same, jnp.broadcast_to(names[k : k + 1], (16, 128)), 0.0) for k in range(3)
        ]
        rows.append(jnp.zeros((80, 128), f32))
        headed_ref[t * 128 : t * 128 + 128, :] = jnp.concatenate(rows, axis=0).T.astype(bf16)

    dest = dest_ref[...]
    upper = (iota((128, 128), 0) <= iota((128, 128), 1)).astype(f32).astype(bf16)
    before = (iota((16, 16), 1) < iota((16, 16), 0)).astype(f32).astype(bf16)
    rank = jnp.zeros((16, 128), f32)
    for k in range(9):
        chosen = (dest == k).astype(f32)
        marks = chosen.astype(bf16)
        inside = dot(marks, upper)
        earlier = jnp.sum(dot(before, marks), axis=1, keepdims=True)
        rank = rank + chosen * (inside - 1.0 + earlier)
    rank_ref[...] = rank.astype(i32)


def first_weights(kernel, lift, after):
    hbm = pl.BlockSpec(memory_space=pltpu.HBM)
    any_ = pl.BlockSpec(memory_space=pl.ANY)
    vmem = pl.BlockSpec(memory_space=pltpu.VMEM)
    return pl.pallas_call(
        first_kernel,
        out_shape=jax.ShapeDtypeStruct((768, 512), bf16),
        in_specs=[hbm, hbm, any_],
        out_specs=vmem,
        scratch_shapes=[
            pltpu.VMEM((4, 32), f32),
            pltpu.VMEM((27, 32, 32), bf16),
            pltpu.SemaphoreType.DMA((2,)),
        ],
        compiler_params=pltpu.CompilerParams(vmem_limit_bytes=8 * 2**20),
        cost_estimate=pl.CostEstimate(flops=500_000, bytes_accessed=2_000_000, transcendentals=0),
    )(lift, kernel, after)


def middle_weights(kernels, after):
    hbm = pl.BlockSpec(memory_space=pltpu.HBM)
    any_ = pl.BlockSpec(memory_space=pl.ANY)
    vmem = pl.BlockSpec(memory_space=pltpu.VMEM)
    return pl.pallas_call(
        middle_kernel,
        out_shape=(
            jax.ShapeDtypeStruct((9, 256, 256), bf16),
            jax.ShapeDtypeStruct((9, 128, 128), bf16),
        ),
        in_specs=[hbm, hbm, any_],
        out_specs=(vmem,) * 2,
        scratch_shapes=[pltpu.VMEM((27, 32, 32), bf16)] * 2 + [pltpu.SemaphoreType.DMA((2,))],
        compiler_params=pltpu.CompilerParams(vmem_limit_bytes=12 * 2**20),
        cost_estimate=pl.CostEstimate(
            flops=5_000_000, bytes_accessed=5_000_000, transcendentals=0
        ),
    )(*kernels, after)


def last_weights(head, dest, kernels, after):
    hbm = pl.BlockSpec(memory_space=pltpu.HBM)
    any_ = pl.BlockSpec(memory_space=pl.ANY)
    vmem = pl.BlockSpec(memory_space=pltpu.VMEM)
    return pl.pallas_call(
        last_kernel,
        out_shape=(
            jax.ShapeDtypeStruct((9, 256, 256), bf16),
            jax.ShapeDtypeStruct((9, 512, 512), bf16),
            jax.ShapeDtypeStruct((512, 128), bf16),
            jax.ShapeDtypeStruct((16, 128), i32),
        ),
        in_specs=[hbm] * 4 + [any_],
        out_specs=(vmem,) * 4,
        scratch_shapes=[
            pltpu.VMEM((3, 32), bf16),
            pltpu.VMEM((16, 128), i32),
            pltpu.VMEM((27, 32, 32), bf16),
            pltpu.VMEM((27, 32, 32), bf16),
            pltpu.SemaphoreType.DMA((4,)),
        ],
        compiler_params=pltpu.CompilerParams(vmem_limit_bytes=16 * 2**20),
        cost_estimate=pl.CostEstimate(
            flops=5_000_000, bytes_accessed=5_000_000, transcendentals=0
        ),
    )(head, dest, *kernels, after)


def lanes_of(ref):
    return jnp.concatenate([ref[chunk].astype(f32) for chunk in range(8)], axis=1)


def spread(value, taps_ref, targets):
    plain = value.astype(bf16)
    rolled = pltpu.roll(value, 2048 - 64, 1).astype(bf16)
    for column in range(COLS):
        if column % 2:
            piece = plain[:, 64 * (column + 1) : 64 * (column + 1) + 256]
        else:
            piece = rolled[:, 64 * column : 64 * column + 256]
        for oy, half in targets:
            begin = column * 32 + half * 16
            taps_ref[begin : begin + 16, oy * 256 : oy * 256 + 256] = piece


def first_conv(taps_ref, weight_ref, sums_ref, keep):
    for block in range(COLS // 4):
        value = gelu(dot(taps_ref[block * 128 : block * 128 + 128, :], weight_ref[...])).astype(bf16)
        keep(block, value)
        quads = value.astype(f32).reshape(2, 4, 16, 512)
        summed = (quads[:, 0] + quads[:, 1]) + (quads[:, 2] + quads[:, 3])
        sums_ref[block * 32 : block * 32 + 32, :] = summed.reshape(32, 512).astype(bf16)


def own_kernel(own_ref, w0a_ref, pool_ref, e0_ref, p1_ref, taps, sums):
    own = lanes_of(own_ref)
    even, odd = own[0:16], own[16:32]
    spread(pltpu.roll(odd, 1, 0), taps, ((0, 0),))
    spread(even, taps, ((0, 1), (1, 0)))
    spread(odd, taps, ((1, 1), (2, 0)))
    spread(pltpu.roll(even, 15, 0), taps, ((2, 1),))

    def keep(block, value):
        for column in range(4):
            n = block * 4 + column - 9
            if 0 <= n < 10:
                e0_ref[n * 32 : n * 32 + 32, :] = value[column * 32 : column * 32 + 32]

    first_conv(taps, w0a_ref, sums, keep)
    p1_ref[...] = dot(sums[...], pool_ref[...]).astype(bf16)


def own_part(own, w0a, pool):
    return pl.pallas_call(
        own_kernel,
        out_shape=(
            jax.ShapeDtypeStruct((320, 512), bf16),
            jax.ShapeDtypeStruct((224, 256), bf16),
        ),
        scratch_shapes=[pltpu.VMEM((COLS * 32, 768), bf16), pltpu.VMEM((224, 512), bf16)],
        compiler_params=pltpu.CompilerParams(vmem_limit_bytes=16 * 2**20),
        cost_estimate=pl.CostEstimate(
            flops=2_000_000_000, bytes_accessed=2_000_000, transcendentals=500_000
        ),
    )(own, w0a, pool)


def network_kernel(
    own_ref,
    low_ref,
    high_ref,
    own_e0_ref,
    own_p1_ref,
    w0a_ref,
    w1a_ref,
    w2_ref,
    w1b_ref,
    w0b_hbm,
    head_ref,
    pool_ref,
    grow_ref,
    pool1_ref,
    grow1_ref,
    rowpool_ref,
    rowgrow_ref,
    pos_ref,
    vel_ref,
    where_ref,
    dest_ref,
    rank_ref,
    out_ref,
    w0b_ref,
    even,
    odd,
    taps,
    sums,
    e0_ref,
    p1_ref,
    p2_ref,
    u1_ref,
    ue_ref,
    uo_ref,
    um,
    u0,
    up,
    sem,
):
    fetch = pltpu.make_async_copy(w0b_hbm, w0b_ref, sem)
    fetch.start()

    low = lanes_of(low_ref)
    high = lanes_of(high_ref)
    own = lanes_of(own_ref)
    for parity, ref in ((0, even), (1, odd)):
        ref[0:2, :] = jnp.zeros((2, 2048), f32)
        ref[2:8, :] = low[6 * parity : 6 * parity + 6]
        ref[8:24, :] = own[16 * parity : 16 * parity + 16]
        ref[24:30, :] = high[6 * parity : 6 * parity + 6]
        ref[30:32, :] = jnp.zeros((2, 2048), f32)

    def outer(ref, first):
        return jnp.concatenate([ref[first : first + 8, :], ref[first + 22 : first + 30, :]], axis=0)

    spread(outer(odd, 0), taps, ((0, 0),))
    spread(outer(even, 1), taps, ((0, 1), (1, 0)))
    spread(outer(odd, 1), taps, ((1, 1), (2, 0)))
    spread(outer(even, 2), taps, ((2, 1),))

    for n in range(10):
        for parity in range(2):
            at = n * 64 + parity * 32
            begin = n * 32 + parity * 16
            e0_ref[at + 8 : at + 24, :] = own_e0_ref[begin : begin + 16, :].astype(f32)

    def keep(block, value):
        for column in range(4):
            n = block * 4 + column - 9
            if 0 <= n < 10:
                for parity in range(2):
                    at = n * 64 + parity * 32
                    begin = column * 32 + parity * 16
                    rows = value[begin : begin + 16].astype(f32)
                    e0_ref[at + 1 : at + 9, :] = rows[0:8]
                    e0_ref[at + 23 : at + 31, :] = rows[8:16]

    first_conv(taps, w0a_ref, sums, keep)
    pooled = dot(sums[...], pool_ref[...]).astype(bf16).astype(f32)
    own_pooled = own_p1_ref[...].astype(f32)
    p1_ref[...] = jnp.zeros((464, 256), f32)
    for column in range(14):
        at = 8 + column * 32
        p1_ref[at + 8 : at + 24, :] = own_pooled[column * 16 : column * 16 + 16]
        p1_ref[at + 1 : at + 9, :] = pooled[column * 16 : column * 16 + 8]
        p1_ref[at + 23 : at + 31, :] = pooled[column * 16 + 8 : column * 16 + 16]

    def middle(ref, blocks, weight_ref, stride, size, pad):
        shifted = [ref[pad + oy - 1 : pad + oy - 1 + size, :].astype(bf16) for oy in range(3)]
        total = None
        for ox in range(3):
            for oy in range(3):
                piece = shifted[oy][ox * stride : ox * stride + blocks * stride]
                term = dot(piece, weight_ref[ox * 3 + oy])
                total = term if total is None else total + term
        return gelu(total).astype(bf16)

    e1 = middle(p1_ref, 12, w1a_ref, 32, 448, 8)
    part = dot(rowpool_ref[...], e1).astype(bf16)
    p2_ref[0:8, :] = jnp.zeros((8, 128), f32)
    p2_ref[104:112, :] = jnp.zeros((8, 128), f32)
    p2_ref[8:104, :] = dot(part, pool1_ref[...]).astype(bf16).astype(f32)
    e2 = middle(p2_ref, 4, w2_ref, 16, 96, 8)
    grown = dot(dot(rowgrow_ref[...], e2).astype(bf16), grow1_ref[...])
    u1_ref[0:8, :] = jnp.zeros((8, 256), f32)
    u1_ref[264:272, :] = jnp.zeros((8, 256), f32)
    u1_ref[8:264, :] = (e1[64:320].astype(f32) + grown).astype(bf16).astype(f32)
    f1 = middle(u1_ref, 6, w1b_ref, 32, 256, 8)
    grown = dot(f1, grow_ref[...])
    for n in range(10):
        add = grown[((n + 1) // 2) * 32 : ((n + 1) // 2) * 32 + 32]
        begin = n * 64
        ue_ref[...] = (e0_ref[begin : begin + 32, :] + add).astype(bf16).astype(f32)
        uo_ref[...] = (e0_ref[begin + 32 : begin + 64, :] + add).astype(bf16).astype(f32)
        at = n * 32
        even_here = ue_ref[8:24, :].astype(bf16)
        odd_here = uo_ref[8:24, :].astype(bf16)
        um[at : at + 16, :] = uo_ref[7:23, :].astype(bf16)
        um[at + 16 : at + 32, :] = even_here
        u0[at : at + 16, :] = even_here
        u0[at + 16 : at + 32, :] = odd_here
        up[at : at + 16, :] = odd_here
        up[at + 16 : at + 32, :] = ue_ref[9:25, :].astype(bf16)

    fetch.wait()
    total = None
    for ox in range(3):
        for oy, ref in enumerate((um, u0, up)):
            term = dot(ref[ox * 32 : ox * 32 + 256, :], w0b_ref[ox * 3 + oy])
            total = term if total is None else total + term
    change = dot(gelu(total).astype(bf16), head_ref[...])

    lane16 = iota((32, 128), 1) // 16
    tables = []
    for comp in range(3):
        table = jnp.zeros((32, 128), f32)
        for x in range(8):
            block = change[x * 32 : x * 32 + 32]
            shift = ((x - comp) * 16) % 128
            moved = pltpu.roll(block, shift, 1) if shift else block
            table = jnp.where(lane16 == x, moved, table)
        tables.append(table)
    cell = where_ref[...]
    y = jnp.bitwise_and(jnp.right_shift(cell, 4), 31)
    row = jnp.bitwise_and(y, 1) * 16 + jnp.right_shift(y, 1)
    lane = jnp.right_shift(cell, 9) * 16 + jnp.bitwise_and(cell, 15)
    kick = [jnp.zeros((16, 128), f32) for _ in range(3)]
    for r in range(32):
        here = row == r
        for comp in range(3):
            source = jnp.broadcast_to(tables[comp][r : r + 1], (16, 128))
            kick[comp] = jnp.where(here, pick_lanes(source, lane), kick[comp])
    payload = []
    speeds = [vel_ref[comp] + kick[comp] for comp in range(3)]
    for comp in range(3):
        payload.append(pos_ref[comp] + DRIFT * speeds[comp])
    payload = payload + speeds

    rank = rank_ref[...]
    key = dest_ref[...] * 4 + jnp.right_shift(rank, 7)
    slot = jnp.bitwise_and(rank, 127)
    line = iota((216, 128), 0)
    line_key = (line // 24) * 4 + jnp.bitwise_and(line, 3)
    slots = iota((128, 128), 0)
    packed = jnp.zeros((216, 128), f32)
    for pair in range(8):
        left, right = [], []
        for c in (2 * pair, 2 * pair + 1):
            rows = jnp.concatenate(
                [jnp.broadcast_to(part[c : c + 1], (4, 128)) for part in payload], axis=0
            )
            full = jnp.concatenate([rows] * 9, axis=0)
            left.append(jnp.where(line_key == key[c : c + 1], full, 0.0).astype(bf16))
            right.append((slots == slot[c : c + 1]).astype(f32).astype(bf16))
        packed = packed + contract_last(
            jnp.concatenate(left, axis=1), jnp.concatenate(right, axis=1)
        )
    out_ref[...] = packed.astype(bf16)


def constants():
    pool = np.zeros((NZ * CH, NZ // 2 * CH), np.float32)
    for z in range(NZ):
        for c in range(CH):
            pool[z * CH + c, z // 2 * CH + c] = 1.0
    pool1 = pool[: 8 * CH, : 4 * CH]
    rowpool = np.zeros((96, 384), np.float32)
    for a in range(6):
        for s in range(12):
            for dx in range(2):
                for dy in range(2):
                    rowpool[a * 16 + s, (2 * a + dx) * 32 + 2 * s + 4 + dy] = 0.25
    rowgrow = np.zeros((256, 64), np.float32)
    for c in range(8):
        for r in range(6, 26):
            rowgrow[c * 32 + r, (c // 2) * 16 + (r - 4) // 2] = 1.0
    made = (pool * 0.125, pool.T, pool1 * 0.5, pool1.T, rowpool, rowgrow)
    return [jnp.asarray(np.ascontiguousarray(value), bf16) for value in made]


def network(own, low, high, fine, weights, head, fixed, pos, vel, where, dest, rank):
    vmem = pl.BlockSpec(memory_space=pltpu.VMEM)
    specs = [vmem] * 22
    specs[9] = pl.BlockSpec(memory_space=pl.ANY)
    return pl.pallas_call(
        network_kernel,
        out_shape=jax.ShapeDtypeStruct((216, 128), bf16),
        in_specs=specs,
        out_specs=vmem,
        scratch_shapes=[
            pltpu.VMEM((9, 512, 512), bf16),
            pltpu.VMEM((32, 2048), f32),
            pltpu.VMEM((32, 2048), f32),
            pltpu.VMEM((COLS * 32, 768), bf16),
            pltpu.VMEM((224, 512), bf16),
            pltpu.VMEM((640, 512), f32),
            pltpu.VMEM((464, 256), f32),
            pltpu.VMEM((112, 128), f32),
            pltpu.VMEM((272, 256), f32),
            pltpu.VMEM((32, 512), f32),
            pltpu.VMEM((32, 512), f32),
            pltpu.VMEM((320, 512), bf16),
            pltpu.VMEM((320, 512), bf16),
            pltpu.VMEM((320, 512), bf16),
            pltpu.SemaphoreType.DMA,
        ],
        compiler_params=pltpu.CompilerParams(vmem_limit_bytes=36 * 2**20),
        cost_estimate=pl.CostEstimate(
            flops=3_000_000_000, bytes_accessed=10_000_000, transcendentals=1_000_000
        ),
    )(own, low, high, *fine, *weights, head, *fixed, pos, vel, where, dest, rank)


def exchange(value, count_x, count_y, rule):
    pairs = []
    for i in range(count_x):
        for j in range(count_y):
            a, b = rule(i, j)
            pairs.append((i * count_y + j, (a % count_x) * count_y + b % count_y))
    return lax.ppermute(value, ("gx", "gy"), pairs)


def body(
    position,
    velocity,
    cell_list,
    slot_weight,
    particle_cell,
    destination,
    lift,
    kernel_0a,
    kernel_1a,
    kernel_2,
    kernel_1b,
    kernel_0b,
    head,
):
    count_x, count_y = lax.axis_size("gx"), lax.axis_size("gy")
    first_core = lax.rem(lax.axis_index("gx"), 2) == 0

    def mate(value):
        return exchange(value, count_x, count_y, lambda i, j: (i ^ 1, j))

    def cross(value):
        return exchange(value, count_x, count_y, lambda i, j: (i + 1 if i % 2 else i - 1, j))

    def along_y(value):
        return exchange(value, count_x, count_y, lambda i, j: (i, j - 1 if i % 2 else j + 1))

    def either(if_first, if_second):
        return jnp.where(first_core, if_first, if_second)

    def cat(parts, axis):
        return jnp.concatenate(parts, axis=axis)

    def barrier(*values):
        return lax.optimization_barrier(values)

    fixed = constants()
    dest = destination.reshape(16, 128)

    mine = deposit(velocity, cell_list, slot_weight)
    theirs = mate(mine)
    near = cross(cat([mine, either(theirs[0:1], theirs[1:2])], 0))
    chip = cat([either(mine, theirs), either(theirs, mine)], 0)

    w0a = first_weights(kernel_0a, lift.T, mine)
    w1a, w2 = middle_weights((kernel_1a, kernel_2), theirs)
    near, w0a, w1a, w2 = barrier(near, w0a, w1a, w2)
    far = mate(near)
    left, right = either(near, far), either(far, near)
    wide = cat([left[2:3], left[0:2], chip, right], 0)
    near = along_y(
        either(
            cat([wide[:, 10:16], wide[:, 26:32]], 1), cat([wide[:, 0:6], wide[:, 16:22]], 1)
        )
    )
    own = either(wide[0:8], wide[2:10])
    fine = own_part(own, w0a, fixed[0])
    w1b, w0b, headed, rank = last_weights(head, dest, (kernel_1b, kernel_0b), own)
    weights = (w0a, w1a, w2, w1b, w0b)
    near, fine, weights, headed, rank = barrier(near, fine, weights, headed, rank)
    far = mate(either(near[2:10], near[0:8]))
    near = either(near[0:8], near[2:10])
    low, high = either(near, far), either(far, near)

    packed = network(
        own,
        low,
        high,
        fine,
        weights,
        headed,
        fixed,
        position.reshape(3, 16, 128),
        velocity.reshape(3, 16, 128),
        particle_cell.reshape(16, 128),
        dest,
        rank,
    )

    behind, level, ahead = packed[0:72], packed[72:144], packed[144:216]
    from_mate = mate(either(ahead, behind))
    from_cross = cross(either(behind, ahead))
    behind = either(from_mate, from_cross)
    ahead = either(from_cross, from_mate)
    groups = (behind, level, ahead)
    down = cat([group[0:24] for group in groups], 0)
    upward = cat([group[48:72] for group in groups], 0)
    passed = mate(either(down, upward))
    near = along_y(cat([either(upward, down), passed], 0))
    far = mate(near[72:])
    near = near[:72]
    upward, down = either(near, far), either(far, near)
    blocks = []
    for a in range(3):
        blocks.append(down[24 * a : 24 * a + 24])
        blocks.append(groups[a][24:48])
        blocks.append(upward[24 * a : 24 * a + 24])
    inbox = jnp.stack(blocks, axis=0).reshape(9, 6, CAP)
    return inbox.astype(f32).transpose(1, 0, 2).reshape(6, 9 * CAP)


def solution(mesh):
    in_specs = (
        P(None, ("gx", "gy")),
        P(None, ("gx", "gy")),
        P(None, "gx", "gy", None),
        P(None, "gx", "gy", None),
        P(("gx", "gy")),
        P(("gx", "gy"), None),
        P(),
        P(),
        P(),
        P(),
        P(),
        P(),
        P(),
    )
    out_specs = P(None, ("gx", "gy"))
    return jax.shard_map(body, mesh=mesh, in_specs=in_specs, out_specs=out_specs, check_vma=False)
```

time: 59 us -> 50.7 us (0.86)
  local copies, waits for them, and re-layouts: 7.51 us -> 1.94 us
  waiting for transfers between devices: 12.5 us -> 9.83 us
  other arithmetic: 2.8 us -> 0.9 us
  starting transfers between devices: 18.6 us -> 20.4 us
    unnamed x50 -> x45, local copies, waits for them, and re-layouts: 5.6 us -> 1.74 us
    pallas_call x2 -> x5, Pallas kernels: 6.24 us -> 9.97 us  [the longest x1 3.78 us: deposit(): pl.pallas_call(deposit_kernel, out_shape=pltpu.VMEM((2, 32, 256), bf16),...]
    pallas_call x1, Pallas kernels: 10.5 us -> 6.91 us  [network(): pl.pallas_call(network_kernel, out_shape=jax.ShapeDtypeStruct((216, 128),...]
    ppermute x10, waiting for transfers between devices: 12.5 us -> 9.83 us  [exchange(): return lax.ppermute(value, ('gx', 'gy'), pairs)]
    ppermute x10, starting transfers between devices: 18.6 us -> 20.4 us  [exchange(): return lax.ppermute(value, ('gx', 'gy'), pairs)]
    another operation x4 -> x0, local copies, waits for them, and re-layouts: 1.27 us -> none  [the longest x2 1.08 us: body(): taps = jnp.tile(taps.transpose(0, 2, 1), (1, 1, 4))]
    select_n x11 -> x10, other arithmetic: 1.03 us -> 0.17 us  [either(): return jnp.where(first_core, if_first, if_second)]
  transfers between devices with their start and end apart: 10 -> 10, of which waited for: 8 -> 8; matrix products, arithmetic and copies ran while one was open for 7% -> 0% of each run, Pallas kernels for 3% -> 12%
where the time goes in v1:
time: 50.7 us; the launch traced here: 50.6 us
  starting transfers between devices  20.4 us (40%)
  Pallas kernels  16.9 us (33%)
  waiting for transfers between devices  9.83 us (19%)
  local copies, waits for them, and re-layouts  1.94 us (4%)
  other arithmetic  0.9 us (2%)
  between operations  0.57 us (1%)
    ppermute x10, starting transfers between devices, exchange(): return lax.ppermute(value, ('gx', 'gy'), pairs)  20.4 us
    ppermute x10, waiting for transfers between devices, exchange(): return lax.ppermute(value, ('gx', 'gy'), pairs)  9.83 us
    pallas_call x1, Pallas kernels, network(): pl.pallas_call(network_kernel, out_shape=jax.ShapeDtypeStruct((216, 128),...  6.91 us
    pallas_call x1, Pallas kernels, deposit(): pl.pallas_call(deposit_kernel, out_shape=pltpu.VMEM((2, 32, 256), bf16),...  3.78 us
    pallas_call x1, Pallas kernels, last_weights(): pl.pallas_call(last_kernel, out_shape=(jax.ShapeDtypeStruct((9, 256, 256)...  2.38 us
    pallas_call x1, Pallas kernels, middle_weights(): pl.pallas_call(middle_kernel, out_shape=(jax.ShapeDtypeStruct((9, 256, 25...  1.75 us
    unnamed x45, local copies, waits for them, and re-layouts  1.74 us
    pallas_call x1, Pallas kernels, own_part(): pl.pallas_call(own_kernel, out_shape=(jax.ShapeDtypeStruct((320, 512), bf...  1.3 us
  transfers between devices with their start and end apart: 10, of which 8 were waited for; matrix products, arithmetic and copies ran while one was open for 0% of the time, Pallas kernels for 12%

profile of v1, /device:TPU:1, one launch (start us, length us, event | category | flops | bytes accessed | tf_op | source)
XLA Modules:
  0.0 50.6 jit_solution(12070125115435282143)
XLA Ops:
  0.0 0.0 copy-start.2
  0.0 0.0 copy-start.3
  0.0 3.8 %shard_map.181.after_ref = bf16[2,32,256]{2,1,0:T(8,128)(2,1)S(1)} custom-call(f32[3,2048]{1,0:T(4,128)} %vel_hbm.1, s32[4,8,16,32]{3,2,1,0:T(8,128)} %bitcast.22, f32[4,8,16,32]{3,2,1,0:T(8,128)} %bitcast.23), custom_call_target="tpu_custom_call" | custom-call | flops 2000000 | bytes 1000000 | tf_op jit(solution)/shard_map/pallas_call | solution.py:107
  3.8 3.3 %collective-permute-start = (bf16[2,32,256]{2,1,0:T(8,128)(2,1)S(1)}, bf16[2,32,256]{2,1,0:T(8,128)(2,1)S(1)}, u32[]{:S(2)}, u32[]{:S(2)}) collective-permute-start(bf16[2,32,256]{2,1,0:T(8,128)(2,1)S(1)} %shard_map.181.after_ref), channel_id=1, source_target_pairs={{0,8},{1,9},{2,10},{3,11},{4,12},{5,13},{6,14},{7,15},{8,0},{9,1},... | collective-permute-start | bytes 98312 | tf_op jit(solution)/shard_map/ppermute | solution.py:615
  7.1 0.9 %collective-permute-done.after_ref = bf16[2,32,256]{2,1,0:T(8,128)(2,1)S(1)} collective-permute-done((bf16[2,32,256]{2,1,0:T(8,128)(2,1)S(1)}, bf16[2,32,256]{2,1,0:T(8,128)(2,1)S(1)}, u32[]{:S(2)}, u32[]{:S(2)}) %collective-permute-start) | collective-permute-done | bytes 32800 | tf_op jit(solution)/shard_map/ppermute | solution.py:615
  8.0 0.1 collective-permute-start.1
  8.1 0.0 copy-start.4
  8.1 0.9 %copy-done.4 = bf16[27,32,32]{2,1,0:T(8,128)(2,1)S(1)} copy-done((bf16[27,32,32]{2,1,0:T(8,128)(2,1)S(1)}, bf16[27,32,32]{2,1,0:T(8,128)(2,1)}, u32[]{:S(2)}) %copy-start.4) | copy-done | bytes 55320
  9.0 0.0 copy-start.6
  9.0 0.7 %copy-done.6 = f32[32,4]{0,1:T(4,128)S(1)} copy-done((f32[32,4]{0,1:T(4,128)S(1)}, f32[32,4]{0,1:T(4,128)}, u32[]{:S(2)}) %copy-start.6) | copy-done | bytes 536
  9.7 0.7 %shard_map.182.w0a_ref = bf16[768,512]{1,0:T(8,128)(2,1)S(1)} custom-call(f32[4,32]{1,0:T(4,128)S(1)} %bitcast.20, bf16[27,32,32]{2,1,0:T(8,128)(2,1)S(1)} %copy-done.4, bf16[2,32,256]{2,1,0:T(8,128)(2,1)S(1)} %shard_map.181.after_ref), custom_call_target="tpu_custom_call" | custom-call | flops 500000 | bytes 2000000 | tf_op jit(solution)/shard_map/pallas_call | solution.py:253
  10.5 0.0 copy-done.2
  10.5 0.0 copy-done.3
  10.5 0.0 copy-start.9
  10.5 1.8 %shard_map.183 = (bf16[9,256,256]{2,1,0:T(8,128)(2,1)S(1)}, bf16[9,128,128]{2,1,0:T(8,128)(2,1)S(1)}) custom-call(bf16[27,32,32]{2,1,0:T(8,128)(2,1)S(1)} %copy-done.2, bf16[27,32,32]{2,1,0:T(8,128)(2,1)S(1)} %copy-done.3, bf16[2,32,256]{2,1,0:T(8,128)(2,1)S(1)} %collective-permute-done.after_ref), custom_call_target="tpu_custom_call" | custom-call | flops 5000000 | bytes 5000000 | tf_op jit(solution)/shard_map/pallas_call | solution.py:272
  12.3 0.0 collective-permute-done.1
  12.3 3.7 %collective-permute-start.2 = (bf16[3,32,256]{2,1,0:T(8,128)(2,1)S(1)}, bf16[3,32,256]{2,1,0:T(8,128)(2,1)S(1)}, u32[]{:S(2)}, u32[]{:S(2)}) collective-permute-start(bf16[3,32,256]{2,1,0:T(8,128)(2,1)S(1)} %collective-permute-done.1), channel_id=1, source_target_pairs={{0,8},{1,9},{2,10},{3,11},{4,12},{5,13},{6,14},{7,15},{8,0},{9,1},... | collective-permute-start | bytes 147464 | tf_op jit(solution)/shard_map/ppermute | solution.py:615
  15.9 0.9 %collective-permute-done.2 = bf16[3,32,256]{2,1,0:T(8,128)(2,1)S(1)} collective-permute-done((bf16[3,32,256]{2,1,0:T(8,128)(2,1)S(1)}, bf16[3,32,256]{2,1,0:T(8,128)(2,1)S(1)}, u32[]{:S(2)}, u32[]{:S(2)}) %collective-permute-start.2) | collective-permute-done | bytes 49184 | tf_op jit(solution)/shard_map/ppermute | solution.py:615
  17.0 0.1 maximum_select_fusion
  17.0 5.7 %collective-permute-start.3 = (bf16[10,12,256]{2,1,0:T(8,128)(2,1)S(1)}, bf16[10,12,256]{2,1,0:T(8,128)(2,1)S(1)}, u32[]{:S(2)}, u32[]{:S(2)}) collective-permute-start(bf16[10,12,256]{2,1,0:T(8,128)(2,1)S(1)} %maximum_select_fusion), channel_id=1, source_target_pairs={{0,1},{1,2},{2,3},{3,4},{4,5},{5,6},{6,7},{7,0},{8,15},{9,8},{10,9... | collective-permute-start | bytes 184328 | tf_op jit(solution)/shard_map/ppermute | solution.py:615
  22.7 0.0 copy-done.9
  22.7 0.0 copy-start
  22.7 0.0 copy-start.1
  22.7 0.0 copy-start.5
  22.7 0.0 copy-start.7
  22.8 0.0 copy-start.16
  22.8 0.0 copy-start.15
  22.8 1.3 %shard_map.184 = (bf16[320,512]{1,0:T(8,128)(2,1)S(1)}, bf16[224,256]{1,0:T(8,128)(2,1)S(1)}) custom-call(bf16[8,32,256]{2,1,0:T(8,128)(2,1)S(1)} %fusion.own_ref.after_ref, bf16[768,512]{1,0:T(8,128)(2,1)S(1)} %shard_map.182.w0a_ref, bf16[512,256]{1,0:T(8,128)(2,1)S(1)} %copy-done.9), custom_call_target="tpu_custom_call" | custom-call | flops 2000000000 | bytes 2000000 | tf_op jit(solution)/shard_map/pallas_call | solution.py:361
  24.1 0.0 copy-start.8
  24.1 0.0 copy-start.10
  24.1 0.0 copy-start.11
  24.1 0.0 copy-start.12
  24.1 0.0 copy-start.13
  24.1 0.0 copy-start.14
  24.2 0.0 copy-done
  24.2 0.0 copy-done.1
  24.2 0.0 copy-done.5
  24.2 0.0 copy-done.7
  24.2 2.4 %shard_map.185 = (bf16[9,256,256]{2,1,0:T(8,128)(2,1)S(1)}, bf16[9,512,512]{2,1,0:T(8,128)(2,1)S(1)}, bf16[512,128]{1,0:T(8,128)(2,1)S(1)}, s32[16,128]{1,0:T(8,128)S(1)}) custom-call(bf16[3,32]{1,0:T(4,128)(2,1)S(1)} %copy-done.7, s32[16,128]{1,0:T(8,128)S(1)} %bitcast.18, bf16[27,32,32]{2,1,0:T(8,128)(2,1)S(1)} %copy-done, ...), custom_call_target="tpu_custom_call" | custom-call | flops 5000000 | bytes 5000000 | tf_op jit(solution)/shard_map/pallas_call | solution.py:292
  26.6 0.0 collective-permute-done.3
  26.6 0.1 collective-permute-start.4
  26.7 0.0 copy-done.16
  26.7 0.0 copy-done.15
  26.8 1.2 %collective-permute-done.4 = bf16[8,12,256]{2,1,0:T(8,128)(2,1)S(1)} collective-permute-done((bf16[8,12,256]{2,1,0:T(8,128)(2,1)S(1)}, bf16[8,12,256]{2,1,0:T(8,128)(2,1)S(1)}, u32[]{:S(2)}, u32[]{:S(2)}) %collective-permute-start.4) | collective-permute-done | bytes 49184 | tf_op jit(solution)/shard_map/ppermute | solution.py:615
  28.0 0.0 copy-done.8
  28.0 0.0 copy-done.10
  28.0 0.0 copy-done.11
  28.0 0.0 copy-done.12
  28.0 0.0 copy-done.13
  28.0 0.0 copy-done.14
  28.0 6.9 %shard_map.186 = bf16[216,128]{1,0:T(8,128)(2,1)S(1)} custom-call(bf16[8,32,256]{2,1,0:T(8,128)(2,1)S(1)} %fusion.own_ref.after_ref, bf16[8,12,256]{2,1,0:T(8,128)(2,1)S(1)} %get-tuple-element.60.low_ref, bf16[8,12,256]{2,1,0:T(8,128)(2,1)S(1)} %get-tuple-element.59.high_ref, bf16[320,512]{1,0:T(8,128)(2,1)S(1)} %get-tuple-element.40.own_e0_ref, ...), custom_call_target="tpu_custom_call" | custom-call | flops 3000000000 | bytes 10000000 | tf_op jit(solution)/shard_map/pallas_call | solution.py:580
  35.0 0.4 collective-permute-start.5
  35.4 0.0 collective-permute-start.6
  35.4 1.0 %collective-permute-done.5 = bf16[72,128]{1,0:T(8,128)(2,1)S(1)} collective-permute-done((bf16[72,128]{1,0:T(8,128)(2,1)S(1)}, bf16[72,128]{1,0:T(8,128)(2,1)S(1)}, u32[]{:S(2)}, u32[]{:S(2)}) %collective-permute-start.5) | collective-permute-done | bytes 18464 | tf_op jit(solution)/shard_map/ppermute | solution.py:615
  36.4 2.2 %collective-permute-done.6 = bf16[72,128]{1,0:T(8,128)(2,1)S(1)} collective-permute-done((bf16[72,128]{1,0:T(8,128)(2,1)S(1)}, bf16[72,128]{1,0:T(8,128)(2,1)S(1)}, u32[]{:S(2)}, u32[]{:S(2)}) %collective-permute-start.6) | collective-permute-done | bytes 18464 | tf_op jit(solution)/shard_map/ppermute | solution.py:615
  38.6 3.8 %collective-permute-start.7 = (bf16[72,128]{1,0:T(8,128)(2,1)S(1)}, bf16[72,128]{1,0:T(8,128)(2,1)S(1)}, u32[]{:S(2)}, u32[]{:S(2)}) collective-permute-start(bf16[72,128]{1,0:T(8,128)(2,1)S(1)} %get-tuple-element.71), channel_id=1, source_target_pairs={{0,8},{1,9},{2,10},{3,11},{4,12},{5,13},{6,14},{7,15},{8,0},{9,1},... | collective-permute-start | bytes 55304 | tf_op jit(solution)/shard_map/ppermute | solution.py:615
  42.4 0.8 %collective-permute-done.7 = bf16[72,128]{1,0:T(8,128)(2,1)S(1)} collective-permute-done((bf16[72,128]{1,0:T(8,128)(2,1)S(1)}, bf16[72,128]{1,0:T(8,128)(2,1)S(1)}, u32[]{:S(2)}, u32[]{:S(2)}) %collective-permute-start.7) | collective-permute-done | bytes 18464 | tf_op jit(solution)/shard_map/ppermute | solution.py:615
  43.2 0.7 %collective-permute-start.8 = (bf16[144,128]{1,0:T(8,128)(2,1)S(1)}, bf16[144,128]{1,0:T(8,128)(2,1)S(1)}, u32[]{:S(2)}, u32[]{:S(2)}) collective-permute-start(bf16[144,128]{1,0:T(8,128)(2,1)S(1)} %pad_maximum_fusion.4), channel_id=1, source_target_pairs={{0,1},{1,2},{2,3},{3,4},{4,5},{5,6},{6,7},{7,0},{8,15},{9,8},{10,9... | collective-permute-start | bytes 110600 | tf_op jit(solution)/shard_map/ppermute | solution.py:615
  44.0 2.1 %collective-permute-done.8 = bf16[144,128]{1,0:T(8,128)(2,1)S(1)} collective-permute-done((bf16[144,128]{1,0:T(8,128)(2,1)S(1)}, bf16[144,128]{1,0:T(8,128)(2,1)S(1)}, u32[]{:S(2)}, u32[]{:S(2)}) %collective-permute-start.8) | collective-permute-done | bytes 36896 | tf_op jit(solution)/shard_map/ppermute | solution.py:615
  46.1 2.7 %collective-permute-start.9 = (bf16[72,128]{1,0:T(8,128)(2,1)S(1)}, bf16[72,128]{1,0:T(8,128)(2,1)S(1)}, u32[]{:S(2)}, u32[]{:S(2)}) collective-permute-start(bf16[72,128]{1,0:T(8,128)(2,1)S(1)} %slice.148), channel_id=1, source_target_pairs={{0,8},{1,9},{2,10},{3,11},{4,12},{5,13},{6,14},{7,15},{8,0},{9,1},... | collective-permute-start | bytes 55304 | tf_op jit(solution)/shard_map/ppermute | solution.py:615
  48.8 0.8 %collective-permute-done.9 = bf16[72,128]{1,0:T(8,128)(2,1)S(1)} collective-permute-done((bf16[72,128]{1,0:T(8,128)(2,1)S(1)}, bf16[72,128]{1,0:T(8,128)(2,1)S(1)}, u32[]{:S(2)}, u32[]{:S(2)}) %collective-permute-start.9) | collective-permute-done | bytes 18464 | tf_op jit(solution)/shard_map/ppermute | solution.py:615
  49.9 0.7 %reshape.45 = f32[9,6,512]{2,1,0:T(8,128)} convert(bf16[9,6,512]{2,1,0:T(8,128)(2,1)S(1)} %constant_dynamic-update-slice_fusion.5) | non-fusion elementwise | flops 27648 | bytes 165888 | tf_op jit(solution)/shard_map/reshape | solution.py:716
  (42 shorter events, 0.4 us)
Async XLA Ops:
  0.0 10.5 %copy-start.2 = (bf16[27,32,32]{2,1,0:T(8,128)(2,1)S(1)}, bf16[27,32,32]{2,1,0:T(8,128)(2,1)}, u32[]{:S(2)}) copy-start(bf16[27,32,32]{2,1,0:T(8,128)(2,1)} %k1a_hbm.1) | copy-start | bytes 165892
  0.0 10.5 %copy-start.3 = (bf16[27,32,32]{2,1,0:T(8,128)(2,1)S(1)}, bf16[27,32,32]{2,1,0:T(8,128)(2,1)}, u32[]{:S(2)}) copy-start(bf16[27,32,32]{2,1,0:T(8,128)(2,1)} %k2_hbm.1) | copy-start | bytes 165892
  3.8 4.2 %collective-permute-start = (bf16[2,32,256]{2,1,0:T(8,128)(2,1)S(1)}, bf16[2,32,256]{2,1,0:T(8,128)(2,1)S(1)}, u32[]{:S(2)}, u32[]{:S(2)}) collective-permute-start(bf16[2,32,256]{2,1,0:T(8,128)(2,1)S(1)} %shard_map.181.after_ref), channel_id=1, source_target_pairs={{0,8},{1,9},{2,10},{3,11},{4,12},{5,13},{6,14},{7,15},{8,0},{9,1},... | collective-permute-start | bytes 98312 | tf_op jit(solution)/shard_map/ppermute | solution.py:615
  8.0 4.3 %collective-permute-start.1 = (bf16[3,32,256]{2,1,0:T(8,128)(2,1)S(1)}, bf16[3,32,256]{2,1,0:T(8,128)(2,1)S(1)}, u32[]{:S(2)}, u32[]{:S(2)}) collective-permute-start(bf16[3,32,256]{2,1,0:T(8,128)(2,1)S(1)} %pad_maximum_fusion.3), channel_id=1, source_target_pairs={{0,248},{1,249},{2,250},{3,251},{4,252},{5,253},{6,254},{7,255},{8... | collective-permute-start | bytes 147464 | tf_op jit(solution)/shard_map/ppermute | solution.py:615
  8.1 0.9 %copy-start.4 = (bf16[27,32,32]{2,1,0:T(8,128)(2,1)S(1)}, bf16[27,32,32]{2,1,0:T(8,128)(2,1)}, u32[]{:S(2)}) copy-start(bf16[27,32,32]{2,1,0:T(8,128)(2,1)} %kernel_hbm.1) | copy-start | bytes 165892
  9.0 0.7 %copy-start.6 = (f32[32,4]{0,1:T(4,128)S(1)}, f32[32,4]{0,1:T(4,128)}, u32[]{:S(2)}) copy-start(f32[32,4]{0,1:T(4,128)} %param.25) | copy-start | bytes 1540
  10.5 12.2 %copy-start.9 = (bf16[512,256]{1,0:T(8,128)(2,1)S(1)}, bf16[512,256]{1,0:T(8,128)(2,1)}, u32[]{:S(2)}) copy-start(bf16[512,256]{1,0:T(8,128)(2,1)} %constant.24.clone.pool_ref) | copy-start | bytes 786436
  12.3 4.5 %collective-permute-start.2 = (bf16[3,32,256]{2,1,0:T(8,128)(2,1)S(1)}, bf16[3,32,256]{2,1,0:T(8,128)(2,1)S(1)}, u32[]{:S(2)}, u32[]{:S(2)}) collective-permute-start(bf16[3,32,256]{2,1,0:T(8,128)(2,1)S(1)} %collective-permute-done.1), channel_id=1, source_target_pairs={{0,8},{1,9},{2,10},{3,11},{4,12},{5,13},{6,14},{7,15},{8,0},{9,1},... | collective-permute-start | bytes 147464 | tf_op jit(solution)/shard_map/ppermute | solution.py:615
  17.0 9.6 %collective-permute-start.3 = (bf16[10,12,256]{2,1,0:T(8,128)(2,1)S(1)}, bf16[10,12,256]{2,1,0:T(8,128)(2,1)S(1)}, u32[]{:S(2)}, u32[]{:S(2)}) collective-permute-start(bf16[10,12,256]{2,1,0:T(8,128)(2,1)S(1)} %maximum_select_fusion), channel_id=1, source_target_pairs={{0,1},{1,2},{2,3},{3,4},{4,5},{5,6},{6,7},{7,0},{8,15},{9,8},{10,9... | collective-permute-start | bytes 184328 | tf_op jit(solution)/shard_map/ppermute | solution.py:615
  22.7 1.5 %copy-start = (bf16[27,32,32]{2,1,0:T(8,128)(2,1)S(1)}, bf16[27,32,32]{2,1,0:T(8,128)(2,1)}, u32[]{:S(2)}) copy-start(bf16[27,32,32]{2,1,0:T(8,128)(2,1)} %k1b_hbm.1) | copy-start | bytes 165892
  22.7 1.5 %copy-start.1 = (bf16[27,32,32]{2,1,0:T(8,128)(2,1)S(1)}, bf16[27,32,32]{2,1,0:T(8,128)(2,1)}, u32[]{:S(2)}) copy-start(bf16[27,32,32]{2,1,0:T(8,128)(2,1)} %k0b_hbm.1) | copy-start | bytes 165892
  22.7 1.4 %copy-start.5 = (s32[2048,1]{0,1:T(1,128)S(1)}, s32[2048,1]{0,1:T(1,128)}, u32[]{:S(2)}) copy-start(s32[2048,1]{0,1:T(1,128)} %param.24) | copy-start | bytes 24580
  22.7 1.4 %copy-start.7 = (bf16[3,32]{1,0:T(4,128)(2,1)S(1)}, bf16[3,32]{1,0:T(4,128)(2,1)}, u32[]{:S(2)}) copy-start(bf16[3,32]{1,0:T(4,128)(2,1)} %head_hbm.1) | copy-start | bytes 580
  22.8 4.0 %copy-start.16 = (f32[3,2048]{1,0:T(4,128)S(1)}, f32[3,2048]{1,0:T(4,128)}, u32[]{:S(2)}) copy-start(f32[3,2048]{1,0:T(4,128)} %param.19) | copy-start | bytes 73732
  22.8 4.0 %copy-start.15 = (f32[3,2048]{1,0:T(4,128)S(1)}, f32[3,2048]{1,0:T(4,128)}, u32[]{:S(2)}) copy-start(f32[3,2048]{1,0:T(4,128)} %vel_hbm.1) | copy-start | bytes 73732
  24.1 3.9 %copy-start.8 = (s32[2048]{0:T(1024)S(1)}, s32[2048]{0:T(1024)}, u32[]{:S(2)}) copy-start(s32[2048]{0:T(1024)} %param.23) | copy-start | bytes 24580
  24.1 3.9 %copy-start.10 = (bf16[256,512]{1,0:T(8,128)(2,1)S(1)}, bf16[256,512]{1,0:T(8,128)(2,1)}, u32[]{:S(2)}) copy-start(bf16[256,512]{1,0:T(8,128)(2,1)} %constant.25.clone.grow_ref) | copy-start | bytes 786436
  24.1 3.9 %copy-start.11 = (bf16[96,384]{1,0:T(8,128)(2,1)S(1)}, bf16[96,384]{1,0:T(8,128)(2,1)}, u32[]{:S(2)}) copy-start(bf16[96,384]{1,0:T(8,128)(2,1)} %constant.28.clone.rowpool_ref) | copy-start | bytes 221188
  24.1 3.9 %copy-start.12 = (bf16[256,128]{1,0:T(8,128)(2,1)S(1)}, bf16[256,128]{1,0:T(8,128)(2,1)}, u32[]{:S(2)}) copy-start(bf16[256,128]{1,0:T(8,128)(2,1)} %constant.26.clone.pool1_ref) | copy-start | bytes 196612
  24.1 3.9 %copy-start.13 = (bf16[128,256]{1,0:T(8,128)(2,1)S(1)}, bf16[128,256]{1,0:T(8,128)(2,1)}, u32[]{:S(2)}) copy-start(bf16[128,256]{1,0:T(8,128)(2,1)} %constant.27.clone.grow1_ref) | copy-start | bytes 196612
  24.1 3.9 %copy-start.14 = (bf16[256,64]{1,0:T(8,128)(2,1)S(1)}, bf16[256,64]{1,0:T(8,128)(2,1)}, u32[]{:S(2)}) copy-start(bf16[256,64]{1,0:T(8,128)(2,1)} %constant.29.clone.rowgrow_ref) | copy-start | bytes 98308
  26.6 1.3 %collective-permute-start.4 = (bf16[8,12,256]{2,1,0:T(8,128)(2,1)S(1)}, bf16[8,12,256]{2,1,0:T(8,128)(2,1)S(1)}, u32[]{:S(2)}, u32[]{:S(2)}) collective-permute-start(bf16[8,12,256]{2,1,0:T(8,128)(2,1)S(1)} %broadcast_select_fusion.2), channel_id=1, source_target_pairs={{0,8},{1,9},{2,10},{3,11},{4,12},{5,13},{6,14},{7,15},{8,0},{9,1},... | collective-permute-start | bytes 147464 | tf_op jit(solution)/shard_map/ppermute | solution.py:615
  35.0 1.5 %collective-permute-start.5 = (bf16[72,128]{1,0:T(8,128)(2,1)S(1)}, bf16[72,128]{1,0:T(8,128)(2,1)S(1)}, u32[]{:S(2)}, u32[]{:S(2)}) collective-permute-start(bf16[72,128]{1,0:T(8,128)(2,1)S(1)} %get-tuple-element.66), channel_id=1, source_target_pairs={{0,8},{1,9},{2,10},{3,11},{4,12},{5,13},{6,14},{7,15},{8,0},{9,1},... | collective-permute-start | bytes 55304 | tf_op jit(solution)/shard_map/ppermute | solution.py:615
  35.4 3.2 %collective-permute-start.6 = (bf16[72,128]{1,0:T(8,128)(2,1)S(1)}, bf16[72,128]{1,0:T(8,128)(2,1)S(1)}, u32[]{:S(2)}, u32[]{:S(2)}) collective-permute-start(bf16[72,128]{1,0:T(8,128)(2,1)S(1)} %get-tuple-element.67), channel_id=1, source_target_pairs={{0,248},{1,249},{2,250},{3,251},{4,252},{5,253},{6,254},{7,255},{8... | collective-permute-start | bytes 55304 | tf_op jit(solution)/shard_map/ppermute | solution.py:615
  38.6 4.6 %collective-permute-start.7 = (bf16[72,128]{1,0:T(8,128)(2,1)S(1)}, bf16[72,128]{1,0:T(8,128)(2,1)S(1)}, u32[]{:S(2)}, u32[]{:S(2)}) collective-permute-start(bf16[72,128]{1,0:T(8,128)(2,1)S(1)} %get-tuple-element.71), channel_id=1, source_target_pairs={{0,8},{1,9},{2,10},{3,11},{4,12},{5,13},{6,14},{7,15},{8,0},{9,1},... | collective-permute-start | bytes 55304 | tf_op jit(solution)/shard_map/ppermute | solution.py:615
  43.2 2.8 %collective-permute-start.8 = (bf16[144,128]{1,0:T(8,128)(2,1)S(1)}, bf16[144,128]{1,0:T(8,128)(2,1)S(1)}, u32[]{:S(2)}, u32[]{:S(2)}) collective-permute-start(bf16[144,128]{1,0:T(8,128)(2,1)S(1)} %pad_maximum_fusion.4), channel_id=1, source_target_pairs={{0,1},{1,2},{2,3},{3,4},{4,5},{5,6},{6,7},{7,0},{8,15},{9,8},{10,9... | collective-permute-start | bytes 110600 | tf_op jit(solution)/shard_map/ppermute | solution.py:615
  46.1 3.5 %collective-permute-start.9 = (bf16[72,128]{1,0:T(8,128)(2,1)S(1)}, bf16[72,128]{1,0:T(8,128)(2,1)S(1)}, u32[]{:S(2)}, u32[]{:S(2)}) collective-permute-start(bf16[72,128]{1,0:T(8,128)(2,1)S(1)} %slice.148), channel_id=1, source_target_pairs={{0,8},{1,9},{2,10},{3,11},{4,12},{5,13},{6,14},{7,15},{8,0},{9,1},... | collective-permute-start | bytes 55304 | tf_op jit(solution)/shard_map/ppermute | solution.py:615

commit v2 on v1

--- a/solution.py
+++ b/solution.py
@@ -57,12 +57,14 @@
     return copies
 
 
-def deposit_kernel(
-    vel_hbm, cells_hbm, weight_hbm, out_ref, stage, vel_ref, cells_ref, weight_ref, sems
-):
+def deposit_kernel(*refs):
+    vel_hbm, cells_hbm, weight_hbm = refs[:3]
+    raw_in, out_ref, raw_out = refs[3:11], refs[11], refs[12:20]
+    stage, vel_ref, cells_ref, weight_ref, sems, raw_sems = refs[20:]
     fetch_vel, fetch_cells, fetch_weight = fetch_all(
         ((vel_hbm, vel_ref), (cells_hbm, cells_ref), (weight_hbm, weight_ref)), sems
     )
+    raw_fetches = fetch_all(zip(raw_in, raw_out), raw_sems)
 
     def dense(ref, s):
         return jnp.concatenate(
@@ -101,32 +103,36 @@
             out_ref[t // 2, parity * 16 : parity * 16 + 16, lanes] = stage[
                 pl.ds(t * 32 + parity, 16, stride=2), :
             ].astype(bf16)
-
-
-def deposit(velocity, cells, weight):
+    for fetch in raw_fetches:
+        fetch.wait()
+
+
+def deposit(velocity, cells, weight, raw):
     return pl.pallas_call(
         deposit_kernel,
-        out_shape=pltpu.VMEM((2, 32, 256), bf16),
-        in_specs=[pl.BlockSpec(memory_space=pltpu.HBM)] * 3,
-        out_specs=pl.BlockSpec(memory_space=pltpu.VMEM),
+        out_shape=(
+            pltpu.VMEM((2, 32, 256), bf16),
+            *(pltpu.VMEM(value.shape, value.dtype) for value in raw),
+        ),
+        in_specs=[pl.BlockSpec(memory_space=pltpu.HBM)] * 11,
+        out_specs=[pl.BlockSpec(memory_space=pltpu.VMEM)] * 9,
         scratch_shapes=[
             pltpu.VMEM((128, 128), f32),
             pltpu.VMEM((3, 2048), f32),
             pltpu.VMEM((4, 8, 16, 32), i32),
             pltpu.VMEM((4, 8, 16, 32), f32),
             pltpu.SemaphoreType.DMA((3,)),
+            pltpu.SemaphoreType.DMA((8,)),
         ],
         cost_estimate=pl.CostEstimate(flops=2_000_000, bytes_accessed=1_000_000, transcendentals=0),
-    )(velocity, jnp.swapaxes(cells, 2, 3), jnp.swapaxes(weight, 2, 3))
+    )(velocity, jnp.swapaxes(cells, 2, 3), jnp.swapaxes(weight, 2, 3), *raw)
 
 
 def contract_last(a, b):
     return lax.dot_general(a, b, (((1,), (1,)), ((), ())), preferred_element_type=f32)
 
 
-def first_kernel(lift_hbm, kernel_hbm, after_ref, w0a_ref, lift_ref, kernel_ref, sems):
-    fetch_lift, fetch = fetch_all(((lift_hbm, lift_ref), (kernel_hbm, kernel_ref)), sems)
-    fetch_lift.wait()
+def first_kernel(lift_ref, kernel_ref, w0a_ref):
     rest = lift_ref[...]
     terms = []
     for _ in range(3):
@@ -139,7 +145,6 @@
     for t in range(4):
         diff = jnp.bitwise_and(row - (4 * t + iota((16, 128), 1) // 32), 15)
         masks.append((diff == 15, diff == 0, diff == 1))
-    fetch.wait()
     for ox in range(3):
         for oy in range(3):
             at = 9 * ox + 3 * oy
@@ -200,25 +205,14 @@
     lax.fori_loop(0, 9, one, 0, unroll=3)
 
 
-def middle_kernel(k1a_hbm, k2_hbm, after_ref, w1a_ref, w2_ref, k1a_ref, k2_ref, sems):
-    fetches = fetch_all(((k1a_hbm, k1a_ref), (k2_hbm, k2_ref)), sems)
-    for fetch, ref, out_ref, depth in zip(fetches, (k1a_ref, k2_ref), (w1a_ref, w2_ref), (8, 4)):
-        fetch.wait()
-        bands(ref, out_ref, depth)
+def middle_kernel(k1a_ref, k2_ref, after_ref, w1a_ref, w2_ref):
+    bands(k1a_ref, w1a_ref, 8)
+    bands(k2_ref, w2_ref, 4)
 
 
 def last_kernel(
-    head_hbm, dest_hbm, k1b_hbm, k0b_hbm, after_ref, w1b_ref, w0b_ref, headed_ref, rank_ref,
-    head_ref, dest_ref, k1b_ref, k0b_ref, sems,
+    head_ref, dest_ref, k1b_ref, k0b_ref, after_ref, w1b_ref, w0b_ref, headed_ref, rank_ref
 ):
-    fetches = fetch_all(
-        (
-            (head_hbm, head_ref), (dest_hbm, dest_ref), (k1b_hbm, k1b_ref), (k0b_hbm, k0b_ref)
-        ),
-        sems,
-    )
-    for fetch in fetches:
-        fetch.wait()
     bands(k1b_ref, w1b_ref, 8)
     bands(k0b_ref, w0b_ref, 16)
 
@@ -246,71 +240,18 @@
     rank_ref[...] = rank.astype(i32)
 
 
-def first_weights(kernel, lift, after):
-    hbm = pl.BlockSpec(memory_space=pltpu.HBM)
-    any_ = pl.BlockSpec(memory_space=pl.ANY)
+def in_vmem(kernel, shapes, values, after=()):
     vmem = pl.BlockSpec(memory_space=pltpu.VMEM)
     return pl.pallas_call(
-        first_kernel,
-        out_shape=jax.ShapeDtypeStruct((768, 512), bf16),
-        in_specs=[hbm, hbm, any_],
-        out_specs=vmem,
-        scratch_shapes=[
-            pltpu.VMEM((4, 32), f32),
-            pltpu.VMEM((27, 32, 32), bf16),
-            pltpu.SemaphoreType.DMA((2,)),
-        ],
-        compiler_params=pltpu.CompilerParams(vmem_limit_bytes=8 * 2**20),
-        cost_estimate=pl.CostEstimate(flops=500_000, bytes_accessed=2_000_000, transcendentals=0),
-    )(lift, kernel, after)
-
-
-def middle_weights(kernels, after):
-    hbm = pl.BlockSpec(memory_space=pltpu.HBM)
-    any_ = pl.BlockSpec(memory_space=pl.ANY)
-    vmem = pl.BlockSpec(memory_space=pltpu.VMEM)
-    return pl.pallas_call(
-        middle_kernel,
-        out_shape=(
-            jax.ShapeDtypeStruct((9, 256, 256), bf16),
-            jax.ShapeDtypeStruct((9, 128, 128), bf16),
-        ),
-        in_specs=[hbm, hbm, any_],
-        out_specs=(vmem,) * 2,
-        scratch_shapes=[pltpu.VMEM((27, 32, 32), bf16)] * 2 + [pltpu.SemaphoreType.DMA((2,))],
-        compiler_params=pltpu.CompilerParams(vmem_limit_bytes=12 * 2**20),
-        cost_estimate=pl.CostEstimate(
-            flops=5_000_000, bytes_accessed=5_000_000, transcendentals=0
-        ),
-    )(*kernels, after)
-
-
-def last_weights(head, dest, kernels, after):
-    hbm = pl.BlockSpec(memory_space=pltpu.HBM)
-    any_ = pl.BlockSpec(memory_space=pl.ANY)
-    vmem = pl.BlockSpec(memory_space=pltpu.VMEM)
-    return pl.pallas_call(
-        last_kernel,
-        out_shape=(
-            jax.ShapeDtypeStruct((9, 256, 256), bf16),
-            jax.ShapeDtypeStruct((9, 512, 512), bf16),
-            jax.ShapeDtypeStruct((512, 128), bf16),
-            jax.ShapeDtypeStruct((16, 128), i32),
-        ),
-        in_specs=[hbm] * 4 + [any_],
-        out_specs=(vmem,) * 4,
-        scratch_shapes=[
-            pltpu.VMEM((3, 32), bf16),
-            pltpu.VMEM((16, 128), i32),
-            pltpu.VMEM((27, 32, 32), bf16),
-            pltpu.VMEM((27, 32, 32), bf16),
-            pltpu.SemaphoreType.DMA((4,)),
-        ],
+        kernel,
+        out_shape=tuple(pltpu.VMEM(shape, dtype) for shape, dtype in shapes),
+        in_specs=[vmem] * len(values) + [pl.BlockSpec(memory_space=pl.ANY)] * len(after),
+        out_specs=(vmem,) * len(shapes),
         compiler_params=pltpu.CompilerParams(vmem_limit_bytes=16 * 2**20),
         cost_estimate=pl.CostEstimate(
             flops=5_000_000, bytes_accessed=5_000_000, transcendentals=0
         ),
-    )(head, dest, *kernels, after)
+    )(*values, *after)
 
 
 def lanes_of(ref):
@@ -360,10 +301,7 @@
 def own_part(own, w0a, pool):
     return pl.pallas_call(
         own_kernel,
-        out_shape=(
-            jax.ShapeDtypeStruct((320, 512), bf16),
-            jax.ShapeDtypeStruct((224, 256), bf16),
-        ),
+        out_shape=(pltpu.VMEM((320, 512), bf16), pltpu.VMEM((224, 256), bf16)),
         scratch_shapes=[pltpu.VMEM((COLS * 32, 768), bf16), pltpu.VMEM((224, 512), bf16)],
         compiler_params=pltpu.CompilerParams(vmem_limit_bytes=16 * 2**20),
         cost_estimate=pl.CostEstimate(
@@ -382,7 +320,7 @@
     w1a_ref,
     w2_ref,
     w1b_ref,
-    w0b_hbm,
+    w0b_ref,
     head_ref,
     pool_ref,
     grow_ref,
@@ -396,7 +334,6 @@
     dest_ref,
     rank_ref,
     out_ref,
-    w0b_ref,
     even,
     odd,
     taps,
@@ -410,11 +347,7 @@
     um,
     u0,
     up,
-    sem,
 ):
-    fetch = pltpu.make_async_copy(w0b_hbm, w0b_ref, sem)
-    fetch.start()
-
     low = lanes_of(low_ref)
     high = lanes_of(high_ref)
     own = lanes_of(own_ref)
@@ -497,7 +430,6 @@
         up[at : at + 16, :] = odd_here
         up[at + 16 : at + 32, :] = ue_ref[9:25, :].astype(bf16)
 
-    fetch.wait()
     total = None
     for ox in range(3):
         for oy, ref in enumerate((um, u0, up)):
@@ -575,15 +507,12 @@
 
 def network(own, low, high, fine, weights, head, fixed, pos, vel, where, dest, rank):
     vmem = pl.BlockSpec(memory_space=pltpu.VMEM)
-    specs = [vmem] * 22
-    specs[9] = pl.BlockSpec(memory_space=pl.ANY)
     return pl.pallas_call(
         network_kernel,
-        out_shape=jax.ShapeDtypeStruct((216, 128), bf16),
-        in_specs=specs,
+        out_shape=pltpu.VMEM((216, 128), bf16),
+        in_specs=[vmem] * 22,
         out_specs=vmem,
         scratch_shapes=[
-            pltpu.VMEM((9, 512, 512), bf16),
             pltpu.VMEM((32, 2048), f32),
             pltpu.VMEM((32, 2048), f32),
             pltpu.VMEM((COLS * 32, 768), bf16),
@@ -597,7 +526,6 @@
             pltpu.VMEM((320, 512), bf16),
             pltpu.VMEM((320, 512), bf16),
             pltpu.VMEM((320, 512), bf16),
-            pltpu.SemaphoreType.DMA,
         ],
         compiler_params=pltpu.CompilerParams(vmem_limit_bytes=36 * 2**20),
         cost_estimate=pl.CostEstimate(
@@ -654,13 +582,20 @@
     fixed = constants()
     dest = destination.reshape(16, 128)
 
-    mine = deposit(velocity, cell_list, slot_weight)
+    raw = (kernel_0a, lift.T, kernel_1a, kernel_2, kernel_1b, kernel_0b, head, dest)
+    mine, *raw = deposit(velocity, cell_list, slot_weight, raw)
+    kernel_0a, lifting, kernel_1a, kernel_2, kernel_1b, kernel_0b, head, dest = raw
     theirs = mate(mine)
     near = cross(cat([mine, either(theirs[0:1], theirs[1:2])], 0))
     chip = cat([either(mine, theirs), either(theirs, mine)], 0)
 
-    w0a = first_weights(kernel_0a, lift.T, mine)
-    w1a, w2 = middle_weights((kernel_1a, kernel_2), theirs)
+    (w0a,) = in_vmem(first_kernel, [((768, 512), bf16)], (lifting, kernel_0a))
+    w1a, w2 = in_vmem(
+        middle_kernel,
+        [((9, 256, 256), bf16), ((9, 128, 128), bf16)],
+        (kernel_1a, kernel_2),
+        (theirs,),
+    )
     near, w0a, w1a, w2 = barrier(near, w0a, w1a, w2)
     far = mate(near)
     left, right = either(near, far), either(far, near)
@@ -672,7 +607,12 @@
     )
     own = either(wide[0:8], wide[2:10])
     fine = own_part(own, w0a, fixed[0])
-    w1b, w0b, headed, rank = last_weights(head, dest, (kernel_1b, kernel_0b), own)
+    w1b, w0b, headed, rank = in_vmem(
+        last_kernel,
+        [((9, 256, 256), bf16), ((9, 512, 512), bf16), ((512, 128), bf16), ((16, 128), i32)],
+        (head, dest, kernel_1b, kernel_0b),
+        (own,),
+    )
     weights = (w0a, w1a, w2, w1b, w0b)
     near, fine, weights, headed, rank = barrier(near, fine, weights, headed, rank)
     far = mate(either(near[2:10], near[0:8]))

time: 50.7 us -> 47.4 us (0.935)
  local copies, waits for them, and re-layouts: 1.94 us -> 0.29 us
  Pallas kernels: 16.9 us -> 15.4 us
  waiting for transfers between devices: 9.83 us -> 11.1 us
  starting transfers between devices: 20.4 us -> 19.2 us
    unnamed x45 -> x29, local copies, waits for them, and re-layouts: 1.74 us -> 0.1 us
    pallas_call x6, Pallas kernels: 16.9 us -> 15.4 us  [the longest x1 6.42 us: network(): pl.pallas_call(network_kernel, out_shape=pltpu.VMEM((216, 128), bf16), in...]
    ppermute x10, starting transfers between devices: 20.4 us -> 19.2 us  [exchange(): return lax.ppermute(value, ('gx', 'gy'), pairs)]
    ppermute x10, waiting for transfers between devices: 9.83 us -> 11.1 us  [exchange(): return lax.ppermute(value, ('gx', 'gy'), pairs)]
  transfers between devices with their start and end apart: 10 -> 10, of which waited for: 8 -> 9; matrix products, arithmetic and copies ran while one was open for 0% -> 0% of each run, Pallas kernels for 12% -> 10%
where the time goes in v2:
time: 47.4 us; the launch traced here: 47.3 us
  starting transfers between devices  19.2 us (41%)
  Pallas kernels  15.4 us (32%)
  waiting for transfers between devices  11.1 us (23%)
  other arithmetic  0.9 us (2%)
    ppermute x10, starting transfers between devices, exchange(): return lax.ppermute(value, ('gx', 'gy'), pairs)  19.2 us
    ppermute x10, waiting for transfers between devices, exchange(): return lax.ppermute(value, ('gx', 'gy'), pairs)  11.1 us
    pallas_call x1, Pallas kernels, network(): pl.pallas_call(network_kernel, out_shape=pltpu.VMEM((216, 128), bf16), in...  6.42 us
    pallas_call x1, Pallas kernels, deposit(): pl.pallas_call(deposit_kernel, out_shape=(pltpu.VMEM((2, 32, 256), bf16),...  4.29 us
    pallas_call x3, Pallas kernels, in_vmem(): pl.pallas_call(kernel, out_shape=tuple((pltpu.VMEM(shape, dtype) for shap...  3.37 us
    pallas_call x1, Pallas kernels, own_part(): pl.pallas_call(own_kernel, out_shape=(pltpu.VMEM((320, 512), bf16), pltpu...  1.3 us
  transfers between devices with their start and end apart: 10, of which 9 were waited for; matrix products, arithmetic and copies ran while one was open for 0% of the time, Pallas kernels for 10%

profile of v2, /device:TPU:1, one launch (start us, length us, event | category | flops | bytes accessed | tf_op | source)
XLA Modules:
  0.0 47.3 jit_solution(11595714710839763970)
XLA Ops:
  0.0 4.3 %shard_map.181 = (bf16[2,32,256]{2,1,0:T(8,128)(2,1)S(1)}, bf16[27,32,32]{2,1,0:T(8,128)(2,1)S(1)}, f32[4,32]{1,0:T(4,128)S(1)}, bf16[27,32,32]{2,1,0:T(8,128)(2...) custom-call(f32[3,2048]{1,0:T(4,128)} %refs_0_.1, ...), custom_call_target="tpu_custom_call" | custom-call | flops 2000000 | bytes 1000000 | tf_op jit(solution)/shard_map/pallas_call | solution.py:111
  4.3 3.3 %collective-permute-start = (bf16[2,32,256]{2,1,0:T(8,128)(2,1)S(1)}, bf16[2,32,256]{2,1,0:T(8,128)(2,1)S(1)}, u32[]{:S(2)}, u32[]{:S(2)}) collective-permute-start(bf16[2,32,256]{2,1,0:T(8,128)(2,1)S(1)} %get-tuple-element.36), channel_id=1, source_target_pairs={{0,8},{1,9},{2,10},{3,11},{4,12},{5,13},{6,14},{7,15},{8,0},{9,1},... | collective-permute-start | bytes 98312 | tf_op jit(solution)/shard_map/ppermute | solution.py:543
  7.6 0.9 %collective-permute-done.after_ref = bf16[2,32,256]{2,1,0:T(8,128)(2,1)S(1)} collective-permute-done((bf16[2,32,256]{2,1,0:T(8,128)(2,1)S(1)}, bf16[2,32,256]{2,1,0:T(8,128)(2,1)S(1)}, u32[]{:S(2)}, u32[]{:S(2)}) %collective-permute-start) | collective-permute-done | bytes 32800 | tf_op jit(solution)/shard_map/ppermute | solution.py:543
  8.5 0.1 collective-permute-start.1
  8.6 0.5 shard_map.182.w0a_ref
  9.1 0.0 copy-start.1
  9.1 1.2 %shard_map.183 = (bf16[9,256,256]{2,1,0:T(8,128)(2,1)S(1)}, bf16[9,128,128]{2,1,0:T(8,128)(2,1)S(1)}) custom-call(bf16[27,32,32]{2,1,0:T(8,128)(2,1)S(1)} %get-tuple-element.39.k1a_ref, bf16[27,32,32]{2,1,0:T(8,128)(2,1)S(1)} %get-tuple-element.40.k2_ref, bf16[2,32,256]{2,1,0:T(8,128)(2,1)S(1)} %collective-permute-done.after_ref), custom_call_target="tpu_custom_call" | custom-call | flops 5000000 | bytes 5000000 | tf_op jit(solution)/shard_map/pallas_call | solution.py:245
  10.2 1.9 %collective-permute-done.1 = bf16[3,32,256]{2,1,0:T(8,128)(2,1)S(1)} collective-permute-done((bf16[3,32,256]{2,1,0:T(8,128)(2,1)S(1)}, bf16[3,32,256]{2,1,0:T(8,128)(2,1)S(1)}, u32[]{:S(2)}, u32[]{:S(2)}) %collective-permute-start.1) | collective-permute-done | bytes 49184 | tf_op jit(solution)/shard_map/ppermute | solution.py:543
  12.1 3.7 %collective-permute-start.2 = (bf16[3,32,256]{2,1,0:T(8,128)(2,1)S(1)}, bf16[3,32,256]{2,1,0:T(8,128)(2,1)S(1)}, u32[]{:S(2)}, u32[]{:S(2)}) collective-permute-start(bf16[3,32,256]{2,1,0:T(8,128)(2,1)S(1)} %collective-permute-done.1), channel_id=1, source_target_pairs={{0,8},{1,9},{2,10},{3,11},{4,12},{5,13},{6,14},{7,15},{8,0},{9,1},... | collective-permute-start | bytes 147464 | tf_op jit(solution)/shard_map/ppermute | solution.py:543
  15.8 0.9 %collective-permute-done.2 = bf16[3,32,256]{2,1,0:T(8,128)(2,1)S(1)} collective-permute-done((bf16[3,32,256]{2,1,0:T(8,128)(2,1)S(1)}, bf16[3,32,256]{2,1,0:T(8,128)(2,1)S(1)}, u32[]{:S(2)}, u32[]{:S(2)}) %collective-permute-start.2) | collective-permute-done | bytes 49184 | tf_op jit(solution)/shard_map/ppermute | solution.py:543
  16.8 0.1 maximum_select_fusion
  16.9 3.9 %collective-permute-start.3 = (bf16[10,12,256]{2,1,0:T(8,128)(2,1)S(1)}, bf16[10,12,256]{2,1,0:T(8,128)(2,1)S(1)}, u32[]{:S(2)}, u32[]{:S(2)}) collective-permute-start(bf16[10,12,256]{2,1,0:T(8,128)(2,1)S(1)} %maximum_select_fusion), channel_id=1, source_target_pairs={{0,1},{1,2},{2,3},{3,4},{4,5},{5,6},{6,7},{7,0},{8,15},{9,8},{10,9... | collective-permute-start | bytes 184328 | tf_op jit(solution)/shard_map/ppermute | solution.py:543
  20.8 0.0 copy-done.1
  20.8 0.0 copy-start.7
  20.8 0.0 copy-start.8
  20.8 1.3 %shard_map.184 = (bf16[320,512]{1,0:T(8,128)(2,1)S(1)}, bf16[224,256]{1,0:T(8,128)(2,1)S(1)}) custom-call(bf16[8,32,256]{2,1,0:T(8,128)(2,1)S(1)} %fusion.own_ref.after_ref, bf16[768,512]{1,0:T(8,128)(2,1)S(1)} %shard_map.182.w0a_ref, bf16[512,256]{1,0:T(8,128)(2,1)S(1)} %copy-done.1), custom_call_target="tpu_custom_call" | custom-call | flops 2000000000 | bytes 2000000 | tf_op jit(solution)/shard_map/pallas_call | solution.py:302
  22.1 0.0 copy-start
  22.1 0.0 copy-start.2
  22.2 0.0 copy-start.3
  22.2 0.0 copy-start.4
  22.2 0.0 copy-start.5
  22.2 0.0 copy-start.6
  22.2 1.8 %shard_map.185 = (bf16[9,256,256]{2,1,0:T(8,128)(2,1)S(1)}, bf16[9,512,512]{2,1,0:T(8,128)(2,1)S(1)}, bf16[512,128]{1,0:T(8,128)(2,1)S(1)}, s32[16,128]{1,0:T(8,128)S(1)}) custom-call(bf16[3,32]{1,0:T(4,128)(2,1)S(1)} %get-tuple-element.49.head_ref, s32[16,128]{1,0:T(8,128)S(1)} %get-tuple-element.50.dest_ref, ...), custom_call_target="tpu_custom_call" | custom-call | flops 5000000 | bytes 5000000 | tf_op jit(solution)/shard_map/pallas_call | solution.py:245
  24.0 0.0 collective-permute-done.3
  24.0 0.1 collective-permute-start.4
  24.1 0.0 copy-done.7
  24.1 0.0 copy-done.8
  24.1 1.2 %collective-permute-done.4 = bf16[8,12,256]{2,1,0:T(8,128)(2,1)S(1)} collective-permute-done((bf16[8,12,256]{2,1,0:T(8,128)(2,1)S(1)}, bf16[8,12,256]{2,1,0:T(8,128)(2,1)S(1)}, u32[]{:S(2)}, u32[]{:S(2)}) %collective-permute-start.4) | collective-permute-done | bytes 49184 | tf_op jit(solution)/shard_map/ppermute | solution.py:543
  25.3 0.0 copy-done
  25.4 0.0 copy-done.2
  25.4 0.0 copy-done.3
  25.4 0.0 copy-done.4
  25.4 0.0 copy-done.5
  25.4 0.0 copy-done.6
  25.4 6.4 %shard_map.186 = bf16[216,128]{1,0:T(8,128)(2,1)S(1)} custom-call(bf16[8,32,256]{2,1,0:T(8,128)(2,1)S(1)} %fusion.own_ref.after_ref, bf16[8,12,256]{2,1,0:T(8,128)(2,1)S(1)} %get-tuple-element.78.low_ref, bf16[8,12,256]{2,1,0:T(8,128)(2,1)S(1)} %get-tuple-element.77.high_ref, bf16[320,512]{1,0:T(8,128)(2,1)S(1)} %get-tuple-element.58.own_e0_ref, ...), custom_call_target="tpu_custom_call" | custom-call | flops 3000000000 | bytes 10000000 | tf_op jit(solution)/shard_map/pallas_call | solution.py:510
  31.9 0.2 collective-permute-start.5
  32.1 0.1 collective-permute-start.6
  32.3 0.9 %collective-permute-done.5 = bf16[72,128]{1,0:T(8,128)(2,1)S(1)} collective-permute-done((bf16[72,128]{1,0:T(8,128)(2,1)S(1)}, bf16[72,128]{1,0:T(8,128)(2,1)S(1)}, u32[]{:S(2)}, u32[]{:S(2)}) %collective-permute-start.5) | collective-permute-done | bytes 18464 | tf_op jit(solution)/shard_map/ppermute | solution.py:543
  33.1 2.3 %collective-permute-done.6 = bf16[72,128]{1,0:T(8,128)(2,1)S(1)} collective-permute-done((bf16[72,128]{1,0:T(8,128)(2,1)S(1)}, bf16[72,128]{1,0:T(8,128)(2,1)S(1)}, u32[]{:S(2)}, u32[]{:S(2)}) %collective-permute-start.6) | collective-permute-done | bytes 18464 | tf_op jit(solution)/shard_map/ppermute | solution.py:543
  35.5 3.7 %collective-permute-start.7 = (bf16[72,128]{1,0:T(8,128)(2,1)S(1)}, bf16[72,128]{1,0:T(8,128)(2,1)S(1)}, u32[]{:S(2)}, u32[]{:S(2)}) collective-permute-start(bf16[72,128]{1,0:T(8,128)(2,1)S(1)} %get-tuple-element.89), channel_id=1, source_target_pairs={{0,8},{1,9},{2,10},{3,11},{4,12},{5,13},{6,14},{7,15},{8,0},{9,1},... | collective-permute-start | bytes 55304 | tf_op jit(solution)/shard_map/ppermute | solution.py:543
  39.2 0.8 %collective-permute-done.7 = bf16[72,128]{1,0:T(8,128)(2,1)S(1)} collective-permute-done((bf16[72,128]{1,0:T(8,128)(2,1)S(1)}, bf16[72,128]{1,0:T(8,128)(2,1)S(1)}, u32[]{:S(2)}, u32[]{:S(2)}) %collective-permute-start.7) | collective-permute-done | bytes 18464 | tf_op jit(solution)/shard_map/ppermute | solution.py:543
  40.0 1.3 %collective-permute-start.8 = (bf16[144,128]{1,0:T(8,128)(2,1)S(1)}, bf16[144,128]{1,0:T(8,128)(2,1)S(1)}, u32[]{:S(2)}, u32[]{:S(2)}) collective-permute-start(bf16[144,128]{1,0:T(8,128)(2,1)S(1)} %pad_maximum_fusion.4), channel_id=1, source_target_pairs={{0,1},{1,2},{2,3},{3,4},{4,5},{5,6},{6,7},{7,0},{8,15},{9,8},{10,9... | collective-permute-start | bytes 110600 | tf_op jit(solution)/shard_map/ppermute | solution.py:543
  41.3 1.5 %collective-permute-done.8 = bf16[144,128]{1,0:T(8,128)(2,1)S(1)} collective-permute-done((bf16[144,128]{1,0:T(8,128)(2,1)S(1)}, bf16[144,128]{1,0:T(8,128)(2,1)S(1)}, u32[]{:S(2)}, u32[]{:S(2)}) %collective-permute-start.8) | collective-permute-done | bytes 36896 | tf_op jit(solution)/shard_map/ppermute | solution.py:543
  42.8 2.7 %collective-permute-start.9 = (bf16[72,128]{1,0:T(8,128)(2,1)S(1)}, bf16[72,128]{1,0:T(8,128)(2,1)S(1)}, u32[]{:S(2)}, u32[]{:S(2)}) collective-permute-start(bf16[72,128]{1,0:T(8,128)(2,1)S(1)} %slice.148), channel_id=1, source_target_pairs={{0,8},{1,9},{2,10},{3,11},{4,12},{5,13},{6,14},{7,15},{8,0},{9,1},... | collective-permute-start | bytes 55304 | tf_op jit(solution)/shard_map/ppermute | solution.py:543
  45.6 0.8 %collective-permute-done.9 = bf16[72,128]{1,0:T(8,128)(2,1)S(1)} collective-permute-done((bf16[72,128]{1,0:T(8,128)(2,1)S(1)}, bf16[72,128]{1,0:T(8,128)(2,1)S(1)}, u32[]{:S(2)}, u32[]{:S(2)}) %collective-permute-start.9) | collective-permute-done | bytes 18464 | tf_op jit(solution)/shard_map/ppermute | solution.py:543
  46.6 0.7 %reshape.45 = f32[9,6,512]{2,1,0:T(8,128)} convert(bf16[9,6,512]{2,1,0:T(8,128)(2,1)S(1)} %constant_dynamic-update-slice_fusion.5) | non-fusion elementwise | flops 27648 | bytes 165888 | tf_op jit(solution)/shard_map/reshape | solution.py:656
  (42 shorter events, 0.4 us)
Async XLA Ops:
  4.3 4.2 %collective-permute-start = (bf16[2,32,256]{2,1,0:T(8,128)(2,1)S(1)}, bf16[2,32,256]{2,1,0:T(8,128)(2,1)S(1)}, u32[]{:S(2)}, u32[]{:S(2)}) collective-permute-start(bf16[2,32,256]{2,1,0:T(8,128)(2,1)S(1)} %get-tuple-element.36), channel_id=1, source_target_pairs={{0,8},{1,9},{2,10},{3,11},{4,12},{5,13},{6,14},{7,15},{8,0},{9,1},... | collective-permute-start | bytes 98312 | tf_op jit(solution)/shard_map/ppermute | solution.py:543
  8.5 3.6 %collective-permute-start.1 = (bf16[3,32,256]{2,1,0:T(8,128)(2,1)S(1)}, bf16[3,32,256]{2,1,0:T(8,128)(2,1)S(1)}, u32[]{:S(2)}, u32[]{:S(2)}) collective-permute-start(bf16[3,32,256]{2,1,0:T(8,128)(2,1)S(1)} %pad_maximum_fusion.3), channel_id=1, source_target_pairs={{0,248},{1,249},{2,250},{3,251},{4,252},{5,253},{6,254},{7,255},{8... | collective-permute-start | bytes 147464 | tf_op jit(solution)/shard_map/ppermute | solution.py:543
  9.1 11.7 %copy-start.1 = (bf16[512,256]{1,0:T(8,128)(2,1)S(1)}, bf16[512,256]{1,0:T(8,128)(2,1)}, u32[]{:S(2)}) copy-start(bf16[512,256]{1,0:T(8,128)(2,1)} %constant.24.clone.pool_ref) | copy-start | bytes 786436
  12.1 4.5 %collective-permute-start.2 = (bf16[3,32,256]{2,1,0:T(8,128)(2,1)S(1)}, bf16[3,32,256]{2,1,0:T(8,128)(2,1)S(1)}, u32[]{:S(2)}, u32[]{:S(2)}) collective-permute-start(bf16[3,32,256]{2,1,0:T(8,128)(2,1)S(1)} %collective-permute-done.1), channel_id=1, source_target_pairs={{0,8},{1,9},{2,10},{3,11},{4,12},{5,13},{6,14},{7,15},{8,0},{9,1},... | collective-permute-start | bytes 147464 | tf_op jit(solution)/shard_map/ppermute | solution.py:543
  16.9 7.1 %collective-permute-start.3 = (bf16[10,12,256]{2,1,0:T(8,128)(2,1)S(1)}, bf16[10,12,256]{2,1,0:T(8,128)(2,1)S(1)}, u32[]{:S(2)}, u32[]{:S(2)}) collective-permute-start(bf16[10,12,256]{2,1,0:T(8,128)(2,1)S(1)} %maximum_select_fusion), channel_id=1, source_target_pairs={{0,1},{1,2},{2,3},{3,4},{4,5},{5,6},{6,7},{7,0},{8,15},{9,8},{10,9... | collective-permute-start | bytes 184328 | tf_op jit(solution)/shard_map/ppermute | solution.py:543
  20.8 3.3 %copy-start.7 = (f32[3,2048]{1,0:T(4,128)S(1)}, f32[3,2048]{1,0:T(4,128)}, u32[]{:S(2)}) copy-start(f32[3,2048]{1,0:T(4,128)} %refs_0_.1) | copy-start | bytes 73732
  20.8 3.3 %copy-start.8 = (f32[3,2048]{1,0:T(4,128)S(1)}, f32[3,2048]{1,0:T(4,128)}, u32[]{:S(2)}) copy-start(f32[3,2048]{1,0:T(4,128)} %param.19) | copy-start | bytes 73732
  22.1 3.2 %copy-start = (s32[2048]{0:T(1024)S(1)}, s32[2048]{0:T(1024)}, u32[]{:S(2)}) copy-start(s32[2048]{0:T(1024)} %param.23) | copy-start | bytes 24580
  22.1 3.2 %copy-start.2 = (bf16[256,512]{1,0:T(8,128)(2,1)S(1)}, bf16[256,512]{1,0:T(8,128)(2,1)}, u32[]{:S(2)}) copy-start(bf16[256,512]{1,0:T(8,128)(2,1)} %constant.25.clone.grow_ref) | copy-start | bytes 786436
  22.2 3.2 %copy-start.3 = (bf16[96,384]{1,0:T(8,128)(2,1)S(1)}, bf16[96,384]{1,0:T(8,128)(2,1)}, u32[]{:S(2)}) copy-start(bf16[96,384]{1,0:T(8,128)(2,1)} %constant.28.clone.rowpool_ref) | copy-start | bytes 221188
  22.2 3.2 %copy-start.4 = (bf16[256,128]{1,0:T(8,128)(2,1)S(1)}, bf16[256,128]{1,0:T(8,128)(2,1)}, u32[]{:S(2)}) copy-start(bf16[256,128]{1,0:T(8,128)(2,1)} %constant.26.clone.pool1_ref) | copy-start | bytes 196612
  22.2 3.2 %copy-start.5 = (bf16[128,256]{1,0:T(8,128)(2,1)S(1)}, bf16[128,256]{1,0:T(8,128)(2,1)}, u32[]{:S(2)}) copy-start(bf16[128,256]{1,0:T(8,128)(2,1)} %constant.27.clone.grow1_ref) | copy-start | bytes 196612
  22.2 3.2 %copy-start.6 = (bf16[256,64]{1,0:T(8,128)(2,1)S(1)}, bf16[256,64]{1,0:T(8,128)(2,1)}, u32[]{:S(2)}) copy-start(bf16[256,64]{1,0:T(8,128)(2,1)} %constant.29.clone.rowgrow_ref) | copy-start | bytes 98308
  24.0 1.3 %collective-permute-start.4 = (bf16[8,12,256]{2,1,0:T(8,128)(2,1)S(1)}, bf16[8,12,256]{2,1,0:T(8,128)(2,1)S(1)}, u32[]{:S(2)}, u32[]{:S(2)}) collective-permute-start(bf16[8,12,256]{2,1,0:T(8,128)(2,1)S(1)} %broadcast_select_fusion.2), channel_id=1, source_target_pairs={{0,8},{1,9},{2,10},{3,11},{4,12},{5,13},{6,14},{7,15},{8,0},{9,1},... | collective-permute-start | bytes 147464 | tf_op jit(solution)/shard_map/ppermute | solution.py:543
  31.9 1.3 %collective-permute-start.5 = (bf16[72,128]{1,0:T(8,128)(2,1)S(1)}, bf16[72,128]{1,0:T(8,128)(2,1)S(1)}, u32[]{:S(2)}, u32[]{:S(2)}) collective-permute-start(bf16[72,128]{1,0:T(8,128)(2,1)S(1)} %get-tuple-element.84), channel_id=1, source_target_pairs={{0,8},{1,9},{2,10},{3,11},{4,12},{5,13},{6,14},{7,15},{8,0},{9,1},... | collective-permute-start | bytes 55304 | tf_op jit(solution)/shard_map/ppermute | solution.py:543
  32.1 3.3 %collective-permute-start.6 = (bf16[72,128]{1,0:T(8,128)(2,1)S(1)}, bf16[72,128]{1,0:T(8,128)(2,1)S(1)}, u32[]{:S(2)}, u32[]{:S(2)}) collective-permute-start(bf16[72,128]{1,0:T(8,128)(2,1)S(1)} %get-tuple-element.85), channel_id=1, source_target_pairs={{0,248},{1,249},{2,250},{3,251},{4,252},{5,253},{6,254},{7,255},{8... | collective-permute-start | bytes 55304 | tf_op jit(solution)/shard_map/ppermute | solution.py:543
  35.5 4.5 %collective-permute-start.7 = (bf16[72,128]{1,0:T(8,128)(2,1)S(1)}, bf16[72,128]{1,0:T(8,128)(2,1)S(1)}, u32[]{:S(2)}, u32[]{:S(2)}) collective-permute-start(bf16[72,128]{1,0:T(8,128)(2,1)S(1)} %get-tuple-element.89), channel_id=1, source_target_pairs={{0,8},{1,9},{2,10},{3,11},{4,12},{5,13},{6,14},{7,15},{8,0},{9,1},... | collective-permute-start | bytes 55304 | tf_op jit(solution)/shard_map/ppermute | solution.py:543
  40.0 2.8 %collective-permute-start.8 = (bf16[144,128]{1,0:T(8,128)(2,1)S(1)}, bf16[144,128]{1,0:T(8,128)(2,1)S(1)}, u32[]{:S(2)}, u32[]{:S(2)}) collective-permute-start(bf16[144,128]{1,0:T(8,128)(2,1)S(1)} %pad_maximum_fusion.4), channel_id=1, source_target_pairs={{0,1},{1,2},{2,3},{3,4},{4,5},{5,6},{6,7},{7,0},{8,15},{9,8},{10,9... | collective-permute-start | bytes 110600 | tf_op jit(solution)/shard_map/ppermute | solution.py:543
  42.8 3.5 %collective-permute-start.9 = (bf16[72,128]{1,0:T(8,128)(2,1)S(1)}, bf16[72,128]{1,0:T(8,128)(2,1)S(1)}, u32[]{:S(2)}, u32[]{:S(2)}) collective-permute-start(bf16[72,128]{1,0:T(8,128)(2,1)S(1)} %slice.148), channel_id=1, source_target_pairs={{0,8},{1,9},{2,10},{3,11},{4,12},{5,13},{6,14},{7,15},{8,0},{9,1},... | collective-permute-start | bytes 55304 | tf_op jit(solution)/shard_map/ppermute | solution.py:543

commit v3 on v2

--- a/solution.py
+++ b/solution.py
@@ -74,19 +74,29 @@
 
     fetch_vel.wait()
     fetch_cells.wait()
-    entries, picked = [], []
+    entries = [dense(cells_ref, s) for s in range(4)]
+    tables = [
+        [
+            jnp.broadcast_to(vel_ref[q : q + 1, r * 128 : (r + 1) * 128], (8, 128))
+            for q in range(3)
+        ]
+        for r in range(16)
+    ]
+    picked = []
     for s in range(4):
-        entry = dense(cells_ref, s)
-        lane = jnp.bitwise_and(entry, 127)
-        row = jnp.right_shift(entry, 7)
-        found = [jnp.zeros((32, 128), f32) for _ in range(3)]
-        for r in range(16):
-            here = row == r
+        pieces = [[], [], []]
+        for begin in range(0, 32, 8):
+            entry = entries[s][begin : begin + 8]
+            lane = jnp.bitwise_and(entry, 127)
+            row = jnp.right_shift(entry, 7)
+            found = [jnp.zeros((8, 128), f32) for _ in range(3)]
+            for r in range(16):
+                here = row == r
+                for q in range(3):
+                    found[q] = jnp.where(here, pick_lanes(tables[r][q], lane), found[q])
             for q in range(3):
-                table = jnp.broadcast_to(vel_ref[q : q + 1, r * 128 : (r + 1) * 128], (32, 128))
-                found[q] = jnp.where(here, pick_lanes(table, lane), found[q])
-        entries.append(entry)
-        picked.append(found)
+                pieces[q].append(found[q])
+        picked.append([jnp.concatenate(piece, axis=0) for piece in pieces])
     fetch_weight.wait()
     totals = [jnp.zeros((32, 128), f32) for _ in range(4)]
     for s in range(4):
@@ -395,12 +405,13 @@
 
     def middle(ref, blocks, weight_ref, stride, size, pad):
         shifted = [ref[pad + oy - 1 : pad + oy - 1 + size, :].astype(bf16) for oy in range(3)]
-        total = None
-        for ox in range(3):
-            for oy in range(3):
-                piece = shifted[oy][ox * stride : ox * stride + blocks * stride]
-                term = dot(piece, weight_ref[ox * 3 + oy])
-                total = term if total is None else total + term
+        pieces = [
+            shifted[oy][ox * stride : ox * stride + blocks * stride]
+            for ox in range(3)
+            for oy in range(3)
+        ]
+        width = weight_ref.shape[2]
+        total = dot(jnp.concatenate(pieces, axis=1), weight_ref[...].reshape(9 * width, width))
         return gelu(total).astype(bf16)
 
     e1 = middle(p1_ref, 12, w1a_ref, 32, 448, 8)
@@ -430,11 +441,8 @@
         up[at : at + 16, :] = odd_here
         up[at + 16 : at + 32, :] = ue_ref[9:25, :].astype(bf16)
 
-    total = None
-    for ox in range(3):
-        for oy, ref in enumerate((um, u0, up)):
-            term = dot(ref[ox * 32 : ox * 32 + 256, :], w0b_ref[ox * 3 + oy])
-            total = term if total is None else total + term
+    pieces = [ref[ox * 32 : ox * 32 + 256, :] for ox in range(3) for ref in (um, u0, up)]
+    total = dot(jnp.concatenate(pieces, axis=1), w0b_ref[...].reshape(9 * 512, 512))
     change = dot(gelu(total).astype(bf16), head_ref[...])
 
     lane16 = iota((32, 128), 1) // 16
@@ -451,12 +459,18 @@
     y = jnp.bitwise_and(jnp.right_shift(cell, 4), 31)
     row = jnp.bitwise_and(y, 1) * 16 + jnp.right_shift(y, 1)
     lane = jnp.right_shift(cell, 9) * 16 + jnp.bitwise_and(cell, 15)
-    kick = [jnp.zeros((16, 128), f32) for _ in range(3)]
-    for r in range(32):
-        here = row == r
+    pieces = [[], [], []]
+    for begin in (0, 8):
+        row_here, lane_here = row[begin : begin + 8], lane[begin : begin + 8]
+        found = [jnp.zeros((8, 128), f32) for _ in range(3)]
+        for r in range(32):
+            here = row_here == r
+            for comp in range(3):
+                source = jnp.broadcast_to(tables[comp][r : r + 1], (8, 128))
+                found[comp] = jnp.where(here, pick_lanes(source, lane_here), found[comp])
         for comp in range(3):
-            source = jnp.broadcast_to(tables[comp][r : r + 1], (16, 128))
-            kick[comp] = jnp.where(here, pick_lanes(source, lane), kick[comp])
+            pieces[comp].append(found[comp])
+    kick = [jnp.concatenate(piece, axis=0) for piece in pieces]
     payload = []
     speeds = [vel_ref[comp] + kick[comp] for comp in range(3)]
     for comp in range(3):
@@ -570,6 +584,9 @@
     def along_y(value):
         return exchange(value, count_x, count_y, lambda i, j: (i, j - 1 if i % 2 else j + 1))
 
+    def along(value, step):
+        return exchange(value, count_x, count_y, lambda i, j: (i, j + step))
+
     def either(if_first, if_second):
         return jnp.where(first_core, if_first, if_second)
 
@@ -642,11 +659,7 @@
     groups = (behind, level, ahead)
     down = cat([group[0:24] for group in groups], 0)
     upward = cat([group[48:72] for group in groups], 0)
-    passed = mate(either(down, upward))
-    near = along_y(cat([either(upward, down), passed], 0))
-    far = mate(near[72:])
-    near = near[:72]
-    upward, down = either(near, far), either(far, near)
+    upward, down = along(upward, 1), along(down, -1)
     blocks = []
     for a in range(3):
         blocks.append(down[24 * a : 24 * a + 24])

time: 47.4 us -> 41.8 us (0.88)
  the two profiles are of different devices: /device:TPU:1 before, /device:TPU:96 now
where the time goes in v3:
time: 41.8 us; the launch traced here: 41.7 us
  starting transfers between devices  16.2 us (39%)
  Pallas kernels  13.6 us (33%)
  waiting for transfers between devices  10.2 us (24%)
  other arithmetic  0.88 us (2%)
  between operations  0.44 us (1%)
    ppermute x9, starting transfers between devices, exchange(): return lax.ppermute(value, ('gx', 'gy'), pairs)  16.2 us
    ppermute x9, waiting for transfers between devices, exchange(): return lax.ppermute(value, ('gx', 'gy'), pairs)  10.2 us
    pallas_call x1, Pallas kernels, network(): pl.pallas_call(network_kernel, out_shape=pltpu.VMEM((216, 128), bf16), in...  6.21 us
    pallas_call x3, Pallas kernels, in_vmem(): pl.pallas_call(kernel, out_shape=tuple((pltpu.VMEM(shape, dtype) for shap...  3.37 us
    pallas_call x1, Pallas kernels, deposit(): pl.pallas_call(deposit_kernel, out_shape=(pltpu.VMEM((2, 32, 256), bf16),...  2.77 us
    pallas_call x1, Pallas kernels, own_part(): pl.pallas_call(own_kernel, out_shape=(pltpu.VMEM((320, 512), bf16), pltpu...  1.3 us
  transfers between devices with their start and end apart: 9, of which 7 were waited for; matrix products, arithmetic and copies ran while one was open for 0% of the time, Pallas kernels for 11%

profile of v3, /device:TPU:96, one launch (start us, length us, event | category | flops | bytes accessed | tf_op | source)
XLA Modules:
  0.0 41.7 jit_solution(18397918812553532640)
XLA Ops:
  0.0 2.8 %shard_map.181 = (bf16[2,32,256]{2,1,0:T(8,128)(2,1)S(1)}, bf16[27,32,32]{2,1,0:T(8,128)(2,1)S(1)}, f32[4,32]{1,0:T(4,128)S(1)}, bf16[27,32,32]{2,1,0:T(8,128)(2...) custom-call(f32[3,2048]{1,0:T(4,128)} %refs_0_.1, ...), custom_call_target="tpu_custom_call" | custom-call | flops 2000000 | bytes 1000000 | tf_op jit(solution)/shard_map/pallas_call | solution.py:121
  2.8 0.1 collective-permute-start
  2.9 1.2 %collective-permute-done.after_ref = bf16[2,32,256]{2,1,0:T(8,128)(2,1)S(1)} collective-permute-done((bf16[2,32,256]{2,1,0:T(8,128)(2,1)S(1)}, bf16[2,32,256]{2,1,0:T(8,128)(2,1)S(1)}, u32[]{:S(2)}, u32[]{:S(2)}) %collective-permute-start) | collective-permute-done | bytes 32800 | tf_op jit(solution)/shard_map/ppermute | solution.py:557
  4.1 5.1 %collective-permute-start.1 = (bf16[3,32,256]{2,1,0:T(8,128)(2,1)S(1)}, bf16[3,32,256]{2,1,0:T(8,128)(2,1)S(1)}, u32[]{:S(2)}, u32[]{:S(2)}) collective-permute-start(bf16[3,32,256]{2,1,0:T(8,128)(2,1)S(1)} %pad_maximum_fusion.3), channel_id=1, source_target_pairs={{0,248},{1,249},{2,250},{3,251},{4,252},{5,253},{6,254},{7,255},{8... | collective-permute-start | bytes 147464 | tf_op jit(solution)/shard_map/ppermute | solution.py:557
  9.1 0.5 %shard_map.182.w0a_ref = bf16[768,512]{1,0:T(8,128)(2,1)S(1)} custom-call(f32[4,32]{1,0:T(4,128)S(1)} %get-tuple-element.37.lift_ref, bf16[27,32,32]{2,1,0:T(8,128)(2,1)S(1)} %get-tuple-element.38.kernel_ref), custom_call_target="tpu_custom_call" | custom-call | flops 5000000 | bytes 5000000 | tf_op jit(solution)/shard_map/pallas_call | solution.py:255
  9.6 0.0 copy-start.1
  9.6 1.2 %shard_map.183 = (bf16[9,256,256]{2,1,0:T(8,128)(2,1)S(1)}, bf16[9,128,128]{2,1,0:T(8,128)(2,1)S(1)}) custom-call(bf16[27,32,32]{2,1,0:T(8,128)(2,1)S(1)} %get-tuple-element.39.k1a_ref, bf16[27,32,32]{2,1,0:T(8,128)(2,1)S(1)} %get-tuple-element.40.k2_ref, bf16[2,32,256]{2,1,0:T(8,128)(2,1)S(1)} %collective-permute-done.after_ref), custom_call_target="tpu_custom_call" | custom-call | flops 5000000 | bytes 5000000 | tf_op jit(solution)/shard_map/pallas_call | solution.py:255
  10.8 0.2 collective-permute-done.1
  11.0 0.0 collective-permute-start.2
  11.0 1.2 %collective-permute-done.2 = bf16[3,32,256]{2,1,0:T(8,128)(2,1)S(1)} collective-permute-done((bf16[3,32,256]{2,1,0:T(8,128)(2,1)S(1)}, bf16[3,32,256]{2,1,0:T(8,128)(2,1)S(1)}, u32[]{:S(2)}, u32[]{:S(2)}) %collective-permute-start.2) | collective-permute-done | bytes 49184 | tf_op jit(solution)/shard_map/ppermute | solution.py:557
  12.4 0.1 maximum_select_fusion
  12.4 3.2 %collective-permute-start.3 = (bf16[10,12,256]{2,1,0:T(8,128)(2,1)S(1)}, bf16[10,12,256]{2,1,0:T(8,128)(2,1)S(1)}, u32[]{:S(2)}, u32[]{:S(2)}) collective-permute-start(bf16[10,12,256]{2,1,0:T(8,128)(2,1)S(1)} %maximum_select_fusion), channel_id=1, source_target_pairs={{0,1},{1,2},{2,3},{3,4},{4,5},{5,6},{6,7},{7,0},{8,15},{9,8},{10,9... | collective-permute-start | bytes 184328 | tf_op jit(solution)/shard_map/ppermute | solution.py:557
  15.7 0.0 copy-done.1
  15.7 0.0 copy-start.7
  15.7 0.0 copy-start.8
  15.7 1.3 %shard_map.184 = (bf16[320,512]{1,0:T(8,128)(2,1)S(1)}, bf16[224,256]{1,0:T(8,128)(2,1)S(1)}) custom-call(bf16[8,32,256]{2,1,0:T(8,128)(2,1)S(1)} %fusion.own_ref.after_ref, bf16[768,512]{1,0:T(8,128)(2,1)S(1)} %shard_map.182.w0a_ref, bf16[512,256]{1,0:T(8,128)(2,1)S(1)} %copy-done.1), custom_call_target="tpu_custom_call" | custom-call | flops 2000000000 | bytes 2000000 | tf_op jit(solution)/shard_map/pallas_call | solution.py:312
  17.0 0.0 copy-start
  17.0 0.0 copy-start.2
  17.0 0.0 copy-start.3
  17.1 0.0 copy-start.4
  17.1 0.0 copy-start.5
  17.1 0.0 copy-start.6
  17.1 1.8 %shard_map.185 = (bf16[9,256,256]{2,1,0:T(8,128)(2,1)S(1)}, bf16[9,512,512]{2,1,0:T(8,128)(2,1)S(1)}, bf16[512,128]{1,0:T(8,128)(2,1)S(1)}, s32[16,128]{1,0:T(8,128)S(1)}) custom-call(bf16[3,32]{1,0:T(4,128)(2,1)S(1)} %get-tuple-element.49.head_ref, s32[16,128]{1,0:T(8,128)S(1)} %get-tuple-element.50.dest_ref, ...), custom_call_target="tpu_custom_call" | custom-call | flops 5000000 | bytes 5000000 | tf_op jit(solution)/shard_map/pallas_call | solution.py:255
  18.8 0.0 collective-permute-done.3
  18.9 0.1 collective-permute-start.4
  19.0 0.0 copy-done.7
  19.0 0.0 copy-done.8
  19.0 1.2 %collective-permute-done.4 = bf16[8,12,256]{2,1,0:T(8,128)(2,1)S(1)} collective-permute-done((bf16[8,12,256]{2,1,0:T(8,128)(2,1)S(1)}, bf16[8,12,256]{2,1,0:T(8,128)(2,1)S(1)}, u32[]{:S(2)}, u32[]{:S(2)}) %collective-permute-start.4) | collective-permute-done | bytes 49184 | tf_op jit(solution)/shard_map/ppermute | solution.py:557
  20.2 0.0 copy-done
  20.2 0.0 copy-done.2
  20.3 0.0 copy-done.3
  20.3 0.0 copy-done.4
  20.3 0.0 copy-done.5
  20.3 0.0 copy-done.6
  20.3 6.2 %shard_map.186 = bf16[216,128]{1,0:T(8,128)(2,1)S(1)} custom-call(bf16[8,32,256]{2,1,0:T(8,128)(2,1)S(1)} %fusion.own_ref.after_ref, bf16[8,12,256]{2,1,0:T(8,128)(2,1)S(1)} %get-tuple-element.78.low_ref, bf16[8,12,256]{2,1,0:T(8,128)(2,1)S(1)} %get-tuple-element.77.high_ref, bf16[320,512]{1,0:T(8,128)(2,1)S(1)} %get-tuple-element.58.own_e0_ref, ...), custom_call_target="tpu_custom_call" | custom-call | flops 3000000000 | bytes 10000000 | tf_op jit(solution)/shard_map/pallas_call | solution.py:524
  26.5 0.2 collective-permute-start.5
  26.8 5.0 %collective-permute-start.6 = (bf16[72,128]{1,0:T(8,128)(2,1)S(1)}, bf16[72,128]{1,0:T(8,128)(2,1)S(1)}, u32[]{:S(2)}, u32[]{:S(2)}) collective-permute-start(bf16[72,128]{1,0:T(8,128)(2,1)S(1)} %get-tuple-element.83), channel_id=1, source_target_pairs={{0,248},{1,249},{2,250},{3,251},{4,252},{5,253},{6,254},{7,255},{8... | collective-permute-start | bytes 55304 | tf_op jit(solution)/shard_map/ppermute | solution.py:557
  31.8 0.0 collective-permute-done.5
  31.8 1.5 %collective-permute-done.6 = bf16[72,128]{1,0:T(8,128)(2,1)S(1)} collective-permute-done((bf16[72,128]{1,0:T(8,128)(2,1)S(1)}, bf16[72,128]{1,0:T(8,128)(2,1)S(1)}, u32[]{:S(2)}, u32[]{:S(2)}) %collective-permute-start.6) | collective-permute-done | bytes 18464 | tf_op jit(solution)/shard_map/ppermute | solution.py:557
  33.3 2.5 %collective-permute-start.8 = (bf16[72,128]{1,0:T(8,128)(2,1)S(1)}, bf16[72,128]{1,0:T(8,128)(2,1)S(1)}, u32[]{:S(2)}, u32[]{:S(2)}) collective-permute-start(bf16[72,128]{1,0:T(8,128)(2,1)S(1)} %pad_maximum_fusion.5), channel_id=1, source_target_pairs={{0,1},{1,2},{2,3},{3,4},{4,5},{5,6},{6,7},{7,0},{8,9},{9,10},{10,1... | collective-permute-start | bytes 55304 | tf_op jit(solution)/shard_map/ppermute | solution.py:557
  35.8 0.0 collective-permute-start.7
  35.9 1.4 %collective-permute-done.8 = bf16[72,128]{1,0:T(8,128)(2,1)S(1)} collective-permute-done((bf16[72,128]{1,0:T(8,128)(2,1)S(1)}, bf16[72,128]{1,0:T(8,128)(2,1)S(1)}, u32[]{:S(2)}, u32[]{:S(2)}) %collective-permute-start.8) | collective-permute-done | bytes 18464 | tf_op jit(solution)/shard_map/ppermute | solution.py:557
  37.3 3.5 %collective-permute-done.7 = bf16[72,128]{1,0:T(8,128)(2,1)S(1)} collective-permute-done((bf16[72,128]{1,0:T(8,128)(2,1)S(1)}, bf16[72,128]{1,0:T(8,128)(2,1)S(1)}, u32[]{:S(2)}, u32[]{:S(2)}) %collective-permute-start.7) | collective-permute-done | bytes 18464 | tf_op jit(solution)/shard_map/ppermute | solution.py:557
  41.0 0.7 %reshape.45 = f32[9,6,512]{2,1,0:T(8,128)} convert(bf16[9,6,512]{2,1,0:T(8,128)(2,1)S(1)} %constant_dynamic-update-slice_fusion.5) | non-fusion elementwise | flops 27648 | bytes 165888 | tf_op jit(solution)/shard_map/reshape | solution.py:669
  (40 shorter events, 0.4 us)
Async XLA Ops:
  2.8 1.3 %collective-permute-start = (bf16[2,32,256]{2,1,0:T(8,128)(2,1)S(1)}, bf16[2,32,256]{2,1,0:T(8,128)(2,1)S(1)}, u32[]{:S(2)}, u32[]{:S(2)}) collective-permute-start(bf16[2,32,256]{2,1,0:T(8,128)(2,1)S(1)} %get-tuple-element.36), channel_id=1, source_target_pairs={{0,8},{1,9},{2,10},{3,11},{4,12},{5,13},{6,14},{7,15},{8,0},{9,1},... | collective-permute-start | bytes 98312 | tf_op jit(solution)/shard_map/ppermute | solution.py:557
  4.1 6.9 %collective-permute-start.1 = (bf16[3,32,256]{2,1,0:T(8,128)(2,1)S(1)}, bf16[3,32,256]{2,1,0:T(8,128)(2,1)S(1)}, u32[]{:S(2)}, u32[]{:S(2)}) collective-permute-start(bf16[3,32,256]{2,1,0:T(8,128)(2,1)S(1)} %pad_maximum_fusion.3), channel_id=1, source_target_pairs={{0,248},{1,249},{2,250},{3,251},{4,252},{5,253},{6,254},{7,255},{8... | collective-permute-start | bytes 147464 | tf_op jit(solution)/shard_map/ppermute | solution.py:557
  9.6 6.1 %copy-start.1 = (bf16[512,256]{1,0:T(8,128)(2,1)S(1)}, bf16[512,256]{1,0:T(8,128)(2,1)}, u32[]{:S(2)}) copy-start(bf16[512,256]{1,0:T(8,128)(2,1)} %constant.24.clone.pool_ref) | copy-start | bytes 786436
  11.0 1.2 %collective-permute-start.2 = (bf16[3,32,256]{2,1,0:T(8,128)(2,1)S(1)}, bf16[3,32,256]{2,1,0:T(8,128)(2,1)S(1)}, u32[]{:S(2)}, u32[]{:S(2)}) collective-permute-start(bf16[3,32,256]{2,1,0:T(8,128)(2,1)S(1)} %collective-permute-done.1), channel_id=1, source_target_pairs={{0,8},{1,9},{2,10},{3,11},{4,12},{5,13},{6,14},{7,15},{8,0},{9,1},... | collective-permute-start | bytes 147464 | tf_op jit(solution)/shard_map/ppermute | solution.py:557
  12.4 6.4 %collective-permute-start.3 = (bf16[10,12,256]{2,1,0:T(8,128)(2,1)S(1)}, bf16[10,12,256]{2,1,0:T(8,128)(2,1)S(1)}, u32[]{:S(2)}, u32[]{:S(2)}) collective-permute-start(bf16[10,12,256]{2,1,0:T(8,128)(2,1)S(1)} %maximum_select_fusion), channel_id=1, source_target_pairs={{0,1},{1,2},{2,3},{3,4},{4,5},{5,6},{6,7},{7,0},{8,15},{9,8},{10,9... | collective-permute-start | bytes 184328 | tf_op jit(solution)/shard_map/ppermute | solution.py:557
  15.7 3.3 %copy-start.7 = (f32[3,2048]{1,0:T(4,128)S(1)}, f32[3,2048]{1,0:T(4,128)}, u32[]{:S(2)}) copy-start(f32[3,2048]{1,0:T(4,128)} %refs_0_.1) | copy-start | bytes 73732
  15.7 3.3 %copy-start.8 = (f32[3,2048]{1,0:T(4,128)S(1)}, f32[3,2048]{1,0:T(4,128)}, u32[]{:S(2)}) copy-start(f32[3,2048]{1,0:T(4,128)} %param.19) | copy-start | bytes 73732
  17.0 3.2 %copy-start = (s32[2048]{0:T(1024)S(1)}, s32[2048]{0:T(1024)}, u32[]{:S(2)}) copy-start(s32[2048]{0:T(1024)} %param.23) | copy-start | bytes 24580
  17.0 3.2 %copy-start.2 = (bf16[256,512]{1,0:T(8,128)(2,1)S(1)}, bf16[256,512]{1,0:T(8,128)(2,1)}, u32[]{:S(2)}) copy-start(bf16[256,512]{1,0:T(8,128)(2,1)} %constant.25.clone.grow_ref) | copy-start | bytes 786436
  17.0 3.2 %copy-start.3 = (bf16[96,384]{1,0:T(8,128)(2,1)S(1)}, bf16[96,384]{1,0:T(8,128)(2,1)}, u32[]{:S(2)}) copy-start(bf16[96,384]{1,0:T(8,128)(2,1)} %constant.28.clone.rowpool_ref) | copy-start | bytes 221188
  17.1 3.2 %copy-start.4 = (bf16[256,128]{1,0:T(8,128)(2,1)S(1)}, bf16[256,128]{1,0:T(8,128)(2,1)}, u32[]{:S(2)}) copy-start(bf16[256,128]{1,0:T(8,128)(2,1)} %constant.26.clone.pool1_ref) | copy-start | bytes 196612
  17.1 3.2 %copy-start.5 = (bf16[128,256]{1,0:T(8,128)(2,1)S(1)}, bf16[128,256]{1,0:T(8,128)(2,1)}, u32[]{:S(2)}) copy-start(bf16[128,256]{1,0:T(8,128)(2,1)} %constant.27.clone.grow1_ref) | copy-start | bytes 196612
  17.1 3.2 %copy-start.6 = (bf16[256,64]{1,0:T(8,128)(2,1)S(1)}, bf16[256,64]{1,0:T(8,128)(2,1)}, u32[]{:S(2)}) copy-start(bf16[256,64]{1,0:T(8,128)(2,1)} %constant.29.clone.rowgrow_ref) | copy-start | bytes 98308
  18.9 1.3 %collective-permute-start.4 = (bf16[8,12,256]{2,1,0:T(8,128)(2,1)S(1)}, bf16[8,12,256]{2,1,0:T(8,128)(2,1)S(1)}, u32[]{:S(2)}, u32[]{:S(2)}) collective-permute-start(bf16[8,12,256]{2,1,0:T(8,128)(2,1)S(1)} %broadcast_select_fusion.2), channel_id=1, source_target_pairs={{0,8},{1,9},{2,10},{3,11},{4,12},{5,13},{6,14},{7,15},{8,0},{9,1},... | collective-permute-start | bytes 147464 | tf_op jit(solution)/shard_map/ppermute | solution.py:557
  26.5 5.2 %collective-permute-start.5 = (bf16[72,128]{1,0:T(8,128)(2,1)S(1)}, bf16[72,128]{1,0:T(8,128)(2,1)S(1)}, u32[]{:S(2)}, u32[]{:S(2)}) collective-permute-start(bf16[72,128]{1,0:T(8,128)(2,1)S(1)} %get-tuple-element.82), channel_id=1, source_target_pairs={{0,8},{1,9},{2,10},{3,11},{4,12},{5,13},{6,14},{7,15},{8,0},{9,1},... | collective-permute-start | bytes 55304 | tf_op jit(solution)/shard_map/ppermute | solution.py:557
  26.8 6.5 %collective-permute-start.6 = (bf16[72,128]{1,0:T(8,128)(2,1)S(1)}, bf16[72,128]{1,0:T(8,128)(2,1)S(1)}, u32[]{:S(2)}, u32[]{:S(2)}) collective-permute-start(bf16[72,128]{1,0:T(8,128)(2,1)S(1)} %get-tuple-element.83), channel_id=1, source_target_pairs={{0,248},{1,249},{2,250},{3,251},{4,252},{5,253},{6,254},{7,255},{8... | collective-permute-start | bytes 55304 | tf_op jit(solution)/shard_map/ppermute | solution.py:557
  33.3 4.0 %collective-permute-start.8 = (bf16[72,128]{1,0:T(8,128)(2,1)S(1)}, bf16[72,128]{1,0:T(8,128)(2,1)S(1)}, u32[]{:S(2)}, u32[]{:S(2)}) collective-permute-start(bf16[72,128]{1,0:T(8,128)(2,1)S(1)} %pad_maximum_fusion.5), channel_id=1, source_target_pairs={{0,1},{1,2},{2,3},{3,4},{4,5},{5,6},{6,7},{7,0},{8,9},{9,10},{10,1... | collective-permute-start | bytes 55304 | tf_op jit(solution)/shard_map/ppermute | solution.py:557
  35.8 5.0 %collective-permute-start.7 = (bf16[72,128]{1,0:T(8,128)(2,1)S(1)}, bf16[72,128]{1,0:T(8,128)(2,1)S(1)}, u32[]{:S(2)}, u32[]{:S(2)}) collective-permute-start(bf16[72,128]{1,0:T(8,128)(2,1)S(1)} %pad_maximum_fusion.4), channel_id=1, source_target_pairs={{0,7},{1,0},{2,1},{3,2},{4,3},{5,4},{6,5},{7,6},{8,15},{9,8},{10,9... | collective-permute-start | bytes 55304 | tf_op jit(solution)/shard_map/ppermute | solution.py:557

commit v4 on v3

--- a/solution.py
+++ b/solution.py
@@ -59,8 +59,8 @@
 
 def deposit_kernel(*refs):
     vel_hbm, cells_hbm, weight_hbm = refs[:3]
-    raw_in, out_ref, raw_out = refs[3:11], refs[11], refs[12:20]
-    stage, vel_ref, cells_ref, weight_ref, sems, raw_sems = refs[20:]
+    raw_in, out_ref, raw_out = refs[3:10], refs[10], refs[11:18]
+    stage, vel_ref, cells_ref, weight_ref, sems, raw_sems = refs[18:]
     fetch_vel, fetch_cells, fetch_weight = fetch_all(
         ((vel_hbm, vel_ref), (cells_hbm, cells_ref), (weight_hbm, weight_ref)), sems
     )
@@ -124,15 +124,15 @@
             pltpu.VMEM((2, 32, 256), bf16),
             *(pltpu.VMEM(value.shape, value.dtype) for value in raw),
         ),
-        in_specs=[pl.BlockSpec(memory_space=pltpu.HBM)] * 11,
-        out_specs=[pl.BlockSpec(memory_space=pltpu.VMEM)] * 9,
+        in_specs=[pl.BlockSpec(memory_space=pltpu.HBM)] * 10,
+        out_specs=[pl.BlockSpec(memory_space=pltpu.VMEM)] * 8,
         scratch_shapes=[
             pltpu.VMEM((128, 128), f32),
             pltpu.VMEM((3, 2048), f32),
             pltpu.VMEM((4, 8, 16, 32), i32),
             pltpu.VMEM((4, 8, 16, 32), f32),
             pltpu.SemaphoreType.DMA((3,)),
-            pltpu.SemaphoreType.DMA((8,)),
+            pltpu.SemaphoreType.DMA((7,)),
         ],
         cost_estimate=pl.CostEstimate(flops=2_000_000, bytes_accessed=1_000_000, transcendentals=0),
     )(velocity, jnp.swapaxes(cells, 2, 3), jnp.swapaxes(weight, 2, 3), *raw)
@@ -599,9 +599,9 @@
     fixed = constants()
     dest = destination.reshape(16, 128)
 
-    raw = (kernel_0a, lift.T, kernel_1a, kernel_2, kernel_1b, kernel_0b, head, dest)
+    raw = (kernel_0a, lift.T, kernel_1a, kernel_2, kernel_1b, kernel_0b, dest)
     mine, *raw = deposit(velocity, cell_list, slot_weight, raw)
-    kernel_0a, lifting, kernel_1a, kernel_2, kernel_1b, kernel_0b, head, dest = raw
+    kernel_0a, lifting, kernel_1a, kernel_2, kernel_1b, kernel_0b, dest = raw
     theirs = mate(mine)
     near = cross(cat([mine, either(theirs[0:1], theirs[1:2])], 0))
     chip = cat([either(mine, theirs), either(theirs, mine)], 0)

time: 41.8 us -> 41.7 us (level)
  no operation moved by 1% of the time
where the time goes in v4:
time: 41.7 us; the launch traced here: 41.6 us
  starting transfers between devices  16.2 us (39%)
  Pallas kernels  13.6 us (33%)
  waiting for transfers between devices  10.2 us (24%)
  other arithmetic  0.88 us (2%)
  between operations  0.46 us (1%)
    ppermute x9, starting transfers between devices, exchange(): return lax.ppermute(value, ('gx', 'gy'), pairs)  16.2 us
    ppermute x9, waiting for transfers between devices, exchange(): return lax.ppermute(value, ('gx', 'gy'), pairs)  10.2 us
    pallas_call x1, Pallas kernels, network(): pl.pallas_call(network_kernel, out_shape=pltpu.VMEM((216, 128), bf16), in...  6.2 us
    pallas_call x3, Pallas kernels, in_vmem(): pl.pallas_call(kernel, out_shape=tuple((pltpu.VMEM(shape, dtype) for shap...  3.37 us
    pallas_call x1, Pallas kernels, deposit(): pl.pallas_call(deposit_kernel, out_shape=(pltpu.VMEM((2, 32, 256), bf16),...  2.69 us
    pallas_call x1, Pallas kernels, own_part(): pl.pallas_call(own_kernel, out_shape=(pltpu.VMEM((320, 512), bf16), pltpu...  1.3 us
  transfers between devices with their start and end apart: 9, of which 7 were waited for; matrix products, arithmetic and copies ran while one was open for 0% of the time, Pallas kernels for 11%

profile of v4, /device:TPU:96, one launch (start us, length us, event | category | flops | bytes accessed | tf_op | source)
XLA Modules:
  0.0 41.6 jit_solution(2692180672605789364)
XLA Ops:
  0.0 2.7 %shard_map.181 = (bf16[2,32,256]{2,1,0:T(8,128)(2,1)S(1)}, bf16[27,32,32]{2,1,0:T(8,128)(2,1)S(1)}, f32[4,32]{1,0:T(4,128)S(1)}, bf16[27,32,32]{2,1,0:T(8,128)(2...) custom-call(f32[3,2048]{1,0:T(4,128)} %refs_0_.1, ...), custom_call_target="tpu_custom_call" | custom-call | flops 2000000 | bytes 1000000 | tf_op jit(solution)/shard_map/pallas_call | solution.py:121
  2.7 0.1 collective-permute-start
  2.8 1.2 %collective-permute-done.after_ref = bf16[2,32,256]{2,1,0:T(8,128)(2,1)S(1)} collective-permute-done((bf16[2,32,256]{2,1,0:T(8,128)(2,1)S(1)}, bf16[2,32,256]{2,1,0:T(8,128)(2,1)S(1)}, u32[]{:S(2)}, u32[]{:S(2)}) %collective-permute-start) | collective-permute-done | bytes 32800 | tf_op jit(solution)/shard_map/ppermute | solution.py:557
  4.0 5.1 %collective-permute-start.1 = (bf16[3,32,256]{2,1,0:T(8,128)(2,1)S(1)}, bf16[3,32,256]{2,1,0:T(8,128)(2,1)S(1)}, u32[]{:S(2)}, u32[]{:S(2)}) collective-permute-start(bf16[3,32,256]{2,1,0:T(8,128)(2,1)S(1)} %pad_maximum_fusion.3), channel_id=1, source_target_pairs={{0,248},{1,249},{2,250},{3,251},{4,252},{5,253},{6,254},{7,255},{8... | collective-permute-start | bytes 147464 | tf_op jit(solution)/shard_map/ppermute | solution.py:557
  9.1 0.5 %shard_map.182.w0a_ref = bf16[768,512]{1,0:T(8,128)(2,1)S(1)} custom-call(f32[4,32]{1,0:T(4,128)S(1)} %get-tuple-element.36.lift_ref, bf16[27,32,32]{2,1,0:T(8,128)(2,1)S(1)} %get-tuple-element.37.kernel_ref), custom_call_target="tpu_custom_call" | custom-call | flops 5000000 | bytes 5000000 | tf_op jit(solution)/shard_map/pallas_call | solution.py:255
  9.5 0.0 copy-start.2
  9.5 1.2 %shard_map.183 = (bf16[9,256,256]{2,1,0:T(8,128)(2,1)S(1)}, bf16[9,128,128]{2,1,0:T(8,128)(2,1)S(1)}) custom-call(bf16[27,32,32]{2,1,0:T(8,128)(2,1)S(1)} %get-tuple-element.38.k1a_ref, bf16[27,32,32]{2,1,0:T(8,128)(2,1)S(1)} %get-tuple-element.39.k2_ref, bf16[2,32,256]{2,1,0:T(8,128)(2,1)S(1)} %collective-permute-done.after_ref), custom_call_target="tpu_custom_call" | custom-call | flops 5000000 | bytes 5000000 | tf_op jit(solution)/shard_map/pallas_call | solution.py:255
  10.7 0.2 collective-permute-done.1
  10.9 0.0 collective-permute-start.2
  10.9 1.2 %collective-permute-done.2 = bf16[3,32,256]{2,1,0:T(8,128)(2,1)S(1)} collective-permute-done((bf16[3,32,256]{2,1,0:T(8,128)(2,1)S(1)}, bf16[3,32,256]{2,1,0:T(8,128)(2,1)S(1)}, u32[]{:S(2)}, u32[]{:S(2)}) %collective-permute-start.2) | collective-permute-done | bytes 49184 | tf_op jit(solution)/shard_map/ppermute | solution.py:557
  12.3 0.1 maximum_select_fusion
  12.4 3.2 %collective-permute-start.3 = (bf16[10,12,256]{2,1,0:T(8,128)(2,1)S(1)}, bf16[10,12,256]{2,1,0:T(8,128)(2,1)S(1)}, u32[]{:S(2)}, u32[]{:S(2)}) collective-permute-start(bf16[10,12,256]{2,1,0:T(8,128)(2,1)S(1)} %maximum_select_fusion), channel_id=1, source_target_pairs={{0,1},{1,2},{2,3},{3,4},{4,5},{5,6},{6,7},{7,0},{8,15},{9,8},{10,9... | collective-permute-start | bytes 184328 | tf_op jit(solution)/shard_map/ppermute | solution.py:557
  15.6 0.0 copy-done.2
  15.6 0.0 copy-start
  15.6 0.0 copy-start.8
  15.6 0.0 copy-start.9
  15.6 1.3 %shard_map.184 = (bf16[320,512]{1,0:T(8,128)(2,1)S(1)}, bf16[224,256]{1,0:T(8,128)(2,1)S(1)}) custom-call(bf16[8,32,256]{2,1,0:T(8,128)(2,1)S(1)} %fusion.own_ref.after_ref, bf16[768,512]{1,0:T(8,128)(2,1)S(1)} %shard_map.182.w0a_ref, bf16[512,256]{1,0:T(8,128)(2,1)S(1)} %copy-done.2), custom_call_target="tpu_custom_call" | custom-call | flops 2000000000 | bytes 2000000 | tf_op jit(solution)/shard_map/pallas_call | solution.py:312
  16.9 0.0 copy-start.1
  17.0 0.0 copy-start.3
  17.0 0.0 copy-start.4
  17.0 0.0 copy-start.5
  17.0 0.0 copy-start.6
  17.0 0.0 copy-start.7
  17.0 0.0 copy-done
  17.0 1.8 %shard_map.185 = (bf16[9,256,256]{2,1,0:T(8,128)(2,1)S(1)}, bf16[9,512,512]{2,1,0:T(8,128)(2,1)S(1)}, bf16[512,128]{1,0:T(8,128)(2,1)S(1)}, s32[16,128]{1,0:T(8,128)S(1)}) custom-call(bf16[3,32]{1,0:T(4,128)(2,1)S(1)} %copy-done, s32[16,128]{1,0:T(8,128)S(1)} %get-tuple-element.48.dest_ref, bf16[27,32,32]{2,1,0:T(8,128)(2,1)S(1)} %get-tuple-element.49.k1b_ref, ...), custom_call_target="tpu_custom_call" | custom-call | flops 5000000 | bytes 5000000 | tf_op jit(solution)/shard_map/pallas_call | solution.py:255
  18.8 0.0 collective-permute-done.3
  18.8 0.1 collective-permute-start.4
  18.9 0.0 copy-done.8
  18.9 0.0 copy-done.9
  19.0 1.2 %collective-permute-done.4 = bf16[8,12,256]{2,1,0:T(8,128)(2,1)S(1)} collective-permute-done((bf16[8,12,256]{2,1,0:T(8,128)(2,1)S(1)}, bf16[8,12,256]{2,1,0:T(8,128)(2,1)S(1)}, u32[]{:S(2)}, u32[]{:S(2)}) %collective-permute-start.4) | collective-permute-done | bytes 49184 | tf_op jit(solution)/shard_map/ppermute | solution.py:557
  20.2 0.0 copy-done.1
  20.2 0.0 copy-done.3
  20.2 0.0 copy-done.4
  20.2 0.0 copy-done.5
  20.2 0.0 copy-done.6
  20.2 0.0 copy-done.7
  20.2 6.2 %shard_map.186 = bf16[216,128]{1,0:T(8,128)(2,1)S(1)} custom-call(bf16[8,32,256]{2,1,0:T(8,128)(2,1)S(1)} %fusion.own_ref.after_ref, bf16[8,12,256]{2,1,0:T(8,128)(2,1)S(1)} %get-tuple-element.76.low_ref, bf16[8,12,256]{2,1,0:T(8,128)(2,1)S(1)} %get-tuple-element.75.high_ref, bf16[320,512]{1,0:T(8,128)(2,1)S(1)} %get-tuple-element.56.own_e0_ref, ...), custom_call_target="tpu_custom_call" | custom-call | flops 3000000000 | bytes 10000000 | tf_op jit(solution)/shard_map/pallas_call | solution.py:524
  26.5 0.2 collective-permute-start.5
  26.7 5.0 %collective-permute-start.6 = (bf16[72,128]{1,0:T(8,128)(2,1)S(1)}, bf16[72,128]{1,0:T(8,128)(2,1)S(1)}, u32[]{:S(2)}, u32[]{:S(2)}) collective-permute-start(bf16[72,128]{1,0:T(8,128)(2,1)S(1)} %get-tuple-element.81), channel_id=1, source_target_pairs={{0,248},{1,249},{2,250},{3,251},{4,252},{5,253},{6,254},{7,255},{8... | collective-permute-start | bytes 55304 | tf_op jit(solution)/shard_map/ppermute | solution.py:557
  31.7 0.0 collective-permute-done.5
  31.7 1.5 %collective-permute-done.6 = bf16[72,128]{1,0:T(8,128)(2,1)S(1)} collective-permute-done((bf16[72,128]{1,0:T(8,128)(2,1)S(1)}, bf16[72,128]{1,0:T(8,128)(2,1)S(1)}, u32[]{:S(2)}, u32[]{:S(2)}) %collective-permute-start.6) | collective-permute-done | bytes 18464 | tf_op jit(solution)/shard_map/ppermute | solution.py:557
  33.3 2.5 %collective-permute-start.8 = (bf16[72,128]{1,0:T(8,128)(2,1)S(1)}, bf16[72,128]{1,0:T(8,128)(2,1)S(1)}, u32[]{:S(2)}, u32[]{:S(2)}) collective-permute-start(bf16[72,128]{1,0:T(8,128)(2,1)S(1)} %pad_maximum_fusion.5), channel_id=1, source_target_pairs={{0,1},{1,2},{2,3},{3,4},{4,5},{5,6},{6,7},{7,0},{8,9},{9,10},{10,1... | collective-permute-start | bytes 55304 | tf_op jit(solution)/shard_map/ppermute | solution.py:557
  35.8 0.0 collective-permute-start.7
  35.8 1.4 %collective-permute-done.8 = bf16[72,128]{1,0:T(8,128)(2,1)S(1)} collective-permute-done((bf16[72,128]{1,0:T(8,128)(2,1)S(1)}, bf16[72,128]{1,0:T(8,128)(2,1)S(1)}, u32[]{:S(2)}, u32[]{:S(2)}) %collective-permute-start.8) | collective-permute-done | bytes 18464 | tf_op jit(solution)/shard_map/ppermute | solution.py:557
  37.3 3.5 %collective-permute-done.7 = bf16[72,128]{1,0:T(8,128)(2,1)S(1)} collective-permute-done((bf16[72,128]{1,0:T(8,128)(2,1)S(1)}, bf16[72,128]{1,0:T(8,128)(2,1)S(1)}, u32[]{:S(2)}, u32[]{:S(2)}) %collective-permute-start.7) | collective-permute-done | bytes 18464 | tf_op jit(solution)/shard_map/ppermute | solution.py:557
  41.0 0.7 %reshape.45 = f32[9,6,512]{2,1,0:T(8,128)} convert(bf16[9,6,512]{2,1,0:T(8,128)(2,1)S(1)} %constant_dynamic-update-slice_fusion.5) | non-fusion elementwise | flops 27648 | bytes 165888 | tf_op jit(solution)/shard_map/reshape | solution.py:669
  (40 shorter events, 0.4 us)
Async XLA Ops:
  2.7 1.3 %collective-permute-start = (bf16[2,32,256]{2,1,0:T(8,128)(2,1)S(1)}, bf16[2,32,256]{2,1,0:T(8,128)(2,1)S(1)}, u32[]{:S(2)}, u32[]{:S(2)}) collective-permute-start(bf16[2,32,256]{2,1,0:T(8,128)(2,1)S(1)} %get-tuple-element.35), channel_id=1, source_target_pairs={{0,8},{1,9},{2,10},{3,11},{4,12},{5,13},{6,14},{7,15},{8,0},{9,1},... | collective-permute-start | bytes 98312 | tf_op jit(solution)/shard_map/ppermute | solution.py:557
  4.0 6.9 %collective-permute-start.1 = (bf16[3,32,256]{2,1,0:T(8,128)(2,1)S(1)}, bf16[3,32,256]{2,1,0:T(8,128)(2,1)S(1)}, u32[]{:S(2)}, u32[]{:S(2)}) collective-permute-start(bf16[3,32,256]{2,1,0:T(8,128)(2,1)S(1)} %pad_maximum_fusion.3), channel_id=1, source_target_pairs={{0,248},{1,249},{2,250},{3,251},{4,252},{5,253},{6,254},{7,255},{8... | collective-permute-start | bytes 147464 | tf_op jit(solution)/shard_map/ppermute | solution.py:557
  9.5 6.1 %copy-start.2 = (bf16[512,256]{1,0:T(8,128)(2,1)S(1)}, bf16[512,256]{1,0:T(8,128)(2,1)}, u32[]{:S(2)}) copy-start(bf16[512,256]{1,0:T(8,128)(2,1)} %constant.24.clone.pool_ref) | copy-start | bytes 786436
  10.9 1.2 %collective-permute-start.2 = (bf16[3,32,256]{2,1,0:T(8,128)(2,1)S(1)}, bf16[3,32,256]{2,1,0:T(8,128)(2,1)S(1)}, u32[]{:S(2)}, u32[]{:S(2)}) collective-permute-start(bf16[3,32,256]{2,1,0:T(8,128)(2,1)S(1)} %collective-permute-done.1), channel_id=1, source_target_pairs={{0,8},{1,9},{2,10},{3,11},{4,12},{5,13},{6,14},{7,15},{8,0},{9,1},... | collective-permute-start | bytes 147464 | tf_op jit(solution)/shard_map/ppermute | solution.py:557
  12.4 6.4 %collective-permute-start.3 = (bf16[10,12,256]{2,1,0:T(8,128)(2,1)S(1)}, bf16[10,12,256]{2,1,0:T(8,128)(2,1)S(1)}, u32[]{:S(2)}, u32[]{:S(2)}) collective-permute-start(bf16[10,12,256]{2,1,0:T(8,128)(2,1)S(1)} %maximum_select_fusion), channel_id=1, source_target_pairs={{0,1},{1,2},{2,3},{3,4},{4,5},{5,6},{6,7},{7,0},{8,15},{9,8},{10,9... | collective-permute-start | bytes 184328 | tf_op jit(solution)/shard_map/ppermute | solution.py:557
  15.6 1.4 %copy-start = (bf16[3,32]{1,0:T(4,128)(2,1)S(1)}, bf16[3,32]{1,0:T(4,128)(2,1)}, u32[]{:S(2)}) copy-start(bf16[3,32]{1,0:T(4,128)(2,1)} %head_ref.1) | copy-start | bytes 580
  15.6 3.3 %copy-start.8 = (f32[3,2048]{1,0:T(4,128)S(1)}, f32[3,2048]{1,0:T(4,128)}, u32[]{:S(2)}) copy-start(f32[3,2048]{1,0:T(4,128)} %refs_0_.1) | copy-start | bytes 73732
  15.6 3.3 %copy-start.9 = (f32[3,2048]{1,0:T(4,128)S(1)}, f32[3,2048]{1,0:T(4,128)}, u32[]{:S(2)}) copy-start(f32[3,2048]{1,0:T(4,128)} %param.19) | copy-start | bytes 73732
  16.9 3.2 %copy-start.1 = (s32[2048]{0:T(1024)S(1)}, s32[2048]{0:T(1024)}, u32[]{:S(2)}) copy-start(s32[2048]{0:T(1024)} %param.23) | copy-start | bytes 24580
  17.0 3.2 %copy-start.3 = (bf16[256,512]{1,0:T(8,128)(2,1)S(1)}, bf16[256,512]{1,0:T(8,128)(2,1)}, u32[]{:S(2)}) copy-start(bf16[256,512]{1,0:T(8,128)(2,1)} %constant.25.clone.grow_ref) | copy-start | bytes 786436
  17.0 3.2 %copy-start.4 = (bf16[96,384]{1,0:T(8,128)(2,1)S(1)}, bf16[96,384]{1,0:T(8,128)(2,1)}, u32[]{:S(2)}) copy-start(bf16[96,384]{1,0:T(8,128)(2,1)} %constant.28.clone.rowpool_ref) | copy-start | bytes 221188
  17.0 3.2 %copy-start.5 = (bf16[256,128]{1,0:T(8,128)(2,1)S(1)}, bf16[256,128]{1,0:T(8,128)(2,1)}, u32[]{:S(2)}) copy-start(bf16[256,128]{1,0:T(8,128)(2,1)} %constant.26.clone.pool1_ref) | copy-start | bytes 196612
  17.0 3.2 %copy-start.6 = (bf16[128,256]{1,0:T(8,128)(2,1)S(1)}, bf16[128,256]{1,0:T(8,128)(2,1)}, u32[]{:S(2)}) copy-start(bf16[128,256]{1,0:T(8,128)(2,1)} %constant.27.clone.grow1_ref) | copy-start | bytes 196612
  17.0 3.2 %copy-start.7 = (bf16[256,64]{1,0:T(8,128)(2,1)S(1)}, bf16[256,64]{1,0:T(8,128)(2,1)}, u32[]{:S(2)}) copy-start(bf16[256,64]{1,0:T(8,128)(2,1)} %constant.29.clone.rowgrow_ref) | copy-start | bytes 98308
  18.8 1.3 %collective-permute-start.4 = (bf16[8,12,256]{2,1,0:T(8,128)(2,1)S(1)}, bf16[8,12,256]{2,1,0:T(8,128)(2,1)S(1)}, u32[]{:S(2)}, u32[]{:S(2)}) collective-permute-start(bf16[8,12,256]{2,1,0:T(8,128)(2,1)S(1)} %broadcast_select_fusion.2), channel_id=1, source_target_pairs={{0,8},{1,9},{2,10},{3,11},{4,12},{5,13},{6,14},{7,15},{8,0},{9,1},... | collective-permute-start | bytes 147464 | tf_op jit(solution)/shard_map/ppermute | solution.py:557
  26.5 5.2 %collective-permute-start.5 = (bf16[72,128]{1,0:T(8,128)(2,1)S(1)}, bf16[72,128]{1,0:T(8,128)(2,1)S(1)}, u32[]{:S(2)}, u32[]{:S(2)}) collective-permute-start(bf16[72,128]{1,0:T(8,128)(2,1)S(1)} %get-tuple-element.80), channel_id=1, source_target_pairs={{0,8},{1,9},{2,10},{3,11},{4,12},{5,13},{6,14},{7,15},{8,0},{9,1},... | collective-permute-start | bytes 55304 | tf_op jit(solution)/shard_map/ppermute | solution.py:557
  26.7 6.5 %collective-permute-start.6 = (bf16[72,128]{1,0:T(8,128)(2,1)S(1)}, bf16[72,128]{1,0:T(8,128)(2,1)S(1)}, u32[]{:S(2)}, u32[]{:S(2)}) collective-permute-start(bf16[72,128]{1,0:T(8,128)(2,1)S(1)} %get-tuple-element.81), channel_id=1, source_target_pairs={{0,248},{1,249},{2,250},{3,251},{4,252},{5,253},{6,254},{7,255},{8... | collective-permute-start | bytes 55304 | tf_op jit(solution)/shard_map/ppermute | solution.py:557
  33.3 4.0 %collective-permute-start.8 = (bf16[72,128]{1,0:T(8,128)(2,1)S(1)}, bf16[72,128]{1,0:T(8,128)(2,1)S(1)}, u32[]{:S(2)}, u32[]{:S(2)}) collective-permute-start(bf16[72,128]{1,0:T(8,128)(2,1)S(1)} %pad_maximum_fusion.5), channel_id=1, source_target_pairs={{0,1},{1,2},{2,3},{3,4},{4,5},{5,6},{6,7},{7,0},{8,9},{9,10},{10,1... | collective-permute-start | bytes 55304 | tf_op jit(solution)/shard_map/ppermute | solution.py:557
  35.8 5.0 %collective-permute-start.7 = (bf16[72,128]{1,0:T(8,128)(2,1)S(1)}, bf16[72,128]{1,0:T(8,128)(2,1)S(1)}, u32[]{:S(2)}, u32[]{:S(2)}) collective-permute-start(bf16[72,128]{1,0:T(8,128)(2,1)S(1)} %pad_maximum_fusion.4), channel_id=1, source_target_pairs={{0,7},{1,0},{2,1},{3,2},{4,3},{5,4},{6,5},{7,6},{8,15},{9,8},{10,9... | collective-permute-start | bytes 55304 | tf_op jit(solution)/shard_map/ppermute | solution.py:557

commit v5 on v4

--- a/solution.py
+++ b/solution.py
@@ -603,17 +603,18 @@
     mine, *raw = deposit(velocity, cell_list, slot_weight, raw)
     kernel_0a, lifting, kernel_1a, kernel_2, kernel_1b, kernel_0b, dest = raw
     theirs = mate(mine)
+    (w0a,) = in_vmem(first_kernel, [((768, 512), bf16)], (lifting, kernel_0a))
+    theirs, w0a = barrier(theirs, w0a)
     near = cross(cat([mine, either(theirs[0:1], theirs[1:2])], 0))
     chip = cat([either(mine, theirs), either(theirs, mine)], 0)
 
-    (w0a,) = in_vmem(first_kernel, [((768, 512), bf16)], (lifting, kernel_0a))
     w1a, w2 = in_vmem(
         middle_kernel,
         [((9, 256, 256), bf16), ((9, 128, 128), bf16)],
         (kernel_1a, kernel_2),
         (theirs,),
     )
-    near, w0a, w1a, w2 = barrier(near, w0a, w1a, w2)
+    near, w1a, w2 = barrier(near, w1a, w2)
     far = mate(near)
     left, right = either(near, far), either(far, near)
     wide = cat([left[2:3], left[0:2], chip, right], 0)
@@ -652,8 +653,8 @@
     )
 
     behind, level, ahead = packed[0:72], packed[72:144], packed[144:216]
+    from_cross = cross(either(behind, ahead))
     from_mate = mate(either(ahead, behind))
-    from_cross = cross(either(behind, ahead))
     behind = either(from_mate, from_cross)
     ahead = either(from_cross, from_mate)
     groups = (behind, level, ahead)

time: 41.7 us -> 41.7 us (level)
  no operation moved by 1% of the time
where the time goes in v5:
time: 41.7 us; the launch traced here: 41.6 us
  starting transfers between devices  16.2 us (39%)
  Pallas kernels  13.6 us (33%)
  waiting for transfers between devices  10.2 us (24%)
  other arithmetic  0.88 us (2%)
  between operations  0.46 us (1%)
    ppermute x9, starting transfers between devices, exchange(): return lax.ppermute(value, ('gx', 'gy'), pairs)  16.2 us
    ppermute x9, waiting for transfers between devices, exchange(): return lax.ppermute(value, ('gx', 'gy'), pairs)  10.2 us
    pallas_call x1, Pallas kernels, network(): pl.pallas_call(network_kernel, out_shape=pltpu.VMEM((216, 128), bf16), in...  6.2 us
    pallas_call x3, Pallas kernels, in_vmem(): pl.pallas_call(kernel, out_shape=tuple((pltpu.VMEM(shape, dtype) for shap...  3.37 us
    pallas_call x1, Pallas kernels, deposit(): pl.pallas_call(deposit_kernel, out_shape=(pltpu.VMEM((2, 32, 256), bf16),...  2.69 us
    pallas_call x1, Pallas kernels, own_part(): pl.pallas_call(own_kernel, out_shape=(pltpu.VMEM((320, 512), bf16), pltpu...  1.3 us
  transfers between devices with their start and end apart: 9, of which 7 were waited for; matrix products, arithmetic and copies ran while one was open for 0% of the time, Pallas kernels for 11%

profile of v5, /device:TPU:96, one launch (start us, length us, event | category | flops | bytes accessed | tf_op | source)
XLA Modules:
  0.0 41.6 jit_solution(17562434069346247815)
XLA Ops:
  0.0 2.7 %shard_map.181 = (bf16[2,32,256]{2,1,0:T(8,128)(2,1)S(1)}, bf16[27,32,32]{2,1,0:T(8,128)(2,1)S(1)}, f32[4,32]{1,0:T(4,128)S(1)}, bf16[27,32,32]{2,1,0:T(8,128)(2...) custom-call(f32[3,2048]{1,0:T(4,128)} %refs_0_.1, ...), custom_call_target="tpu_custom_call" | custom-call | flops 2000000 | bytes 1000000 | tf_op jit(solution)/shard_map/pallas_call | solution.py:121
  2.7 0.1 collective-permute-start
  2.8 0.5 %shard_map.182.w0a_ref = bf16[768,512]{1,0:T(8,128)(2,1)S(1)} custom-call(f32[4,32]{1,0:T(4,128)S(1)} %get-tuple-element.37.lift_ref, bf16[27,32,32]{2,1,0:T(8,128)(2,1)S(1)} %get-tuple-element.38.kernel_ref), custom_call_target="tpu_custom_call" | custom-call | flops 5000000 | bytes 5000000 | tf_op jit(solution)/shard_map/pallas_call | solution.py:255
  3.3 0.0 copy-start.2
  3.3 0.7 %collective-permute-done.after_ref = bf16[2,32,256]{2,1,0:T(8,128)(2,1)S(1)} collective-permute-done((bf16[2,32,256]{2,1,0:T(8,128)(2,1)S(1)}, bf16[2,32,256]{2,1,0:T(8,128)(2,1)S(1)}, u32[]{:S(2)}, u32[]{:S(2)}) %collective-permute-start) | collective-permute-done | bytes 32800 | tf_op jit(solution)/shard_map/ppermute | solution.py:557
  4.0 5.1 %collective-permute-start.1 = (bf16[3,32,256]{2,1,0:T(8,128)(2,1)S(1)}, bf16[3,32,256]{2,1,0:T(8,128)(2,1)S(1)}, u32[]{:S(2)}, u32[]{:S(2)}) collective-permute-start(bf16[3,32,256]{2,1,0:T(8,128)(2,1)S(1)} %pad_maximum_fusion.3), channel_id=1, source_target_pairs={{0,248},{1,249},{2,250},{3,251},{4,252},{5,253},{6,254},{7,255},{8... | collective-permute-start | bytes 147464 | tf_op jit(solution)/shard_map/ppermute | solution.py:557
  9.1 1.2 %shard_map.183 = (bf16[9,256,256]{2,1,0:T(8,128)(2,1)S(1)}, bf16[9,128,128]{2,1,0:T(8,128)(2,1)S(1)}) custom-call(bf16[27,32,32]{2,1,0:T(8,128)(2,1)S(1)} %get-tuple-element.40.k1a_ref, bf16[27,32,32]{2,1,0:T(8,128)(2,1)S(1)} %get-tuple-element.41.k2_ref, bf16[2,32,256]{2,1,0:T(8,128)(2,1)S(1)} %collective-permute-done.after_ref), custom_call_target="tpu_custom_call" | custom-call | flops 5000000 | bytes 5000000 | tf_op jit(solution)/shard_map/pallas_call | solution.py:255
  10.2 0.7 %collective-permute-done.1 = bf16[3,32,256]{2,1,0:T(8,128)(2,1)S(1)} collective-permute-done((bf16[3,32,256]{2,1,0:T(8,128)(2,1)S(1)}, bf16[3,32,256]{2,1,0:T(8,128)(2,1)S(1)}, u32[]{:S(2)}, u32[]{:S(2)}) %collective-permute-start.1) | collective-permute-done | bytes 49184 | tf_op jit(solution)/shard_map/ppermute | solution.py:557
  10.9 0.0 collective-permute-start.2
  10.9 1.2 %collective-permute-done.2 = bf16[3,32,256]{2,1,0:T(8,128)(2,1)S(1)} collective-permute-done((bf16[3,32,256]{2,1,0:T(8,128)(2,1)S(1)}, bf16[3,32,256]{2,1,0:T(8,128)(2,1)S(1)}, u32[]{:S(2)}, u32[]{:S(2)}) %collective-permute-start.2) | collective-permute-done | bytes 49184 | tf_op jit(solution)/shard_map/ppermute | solution.py:557
  12.3 0.1 maximum_select_fusion
  12.4 3.2 %collective-permute-start.3 = (bf16[10,12,256]{2,1,0:T(8,128)(2,1)S(1)}, bf16[10,12,256]{2,1,0:T(8,128)(2,1)S(1)}, u32[]{:S(2)}, u32[]{:S(2)}) collective-permute-start(bf16[10,12,256]{2,1,0:T(8,128)(2,1)S(1)} %maximum_select_fusion), channel_id=1, source_target_pairs={{0,1},{1,2},{2,3},{3,4},{4,5},{5,6},{6,7},{7,0},{8,15},{9,8},{10,9... | collective-permute-start | bytes 184328 | tf_op jit(solution)/shard_map/ppermute | solution.py:557
  15.6 0.0 copy-done.2
  15.6 0.0 copy-start
  15.6 0.0 copy-start.8
  15.6 0.0 copy-start.9
  15.6 1.3 %shard_map.184 = (bf16[320,512]{1,0:T(8,128)(2,1)S(1)}, bf16[224,256]{1,0:T(8,128)(2,1)S(1)}) custom-call(bf16[8,32,256]{2,1,0:T(8,128)(2,1)S(1)} %fusion.own_ref.after_ref, bf16[768,512]{1,0:T(8,128)(2,1)S(1)} %shard_map.182.w0a_ref, bf16[512,256]{1,0:T(8,128)(2,1)S(1)} %copy-done.2), custom_call_target="tpu_custom_call" | custom-call | flops 2000000000 | bytes 2000000 | tf_op jit(solution)/shard_map/pallas_call | solution.py:312
  16.9 0.0 copy-start.1
  17.0 0.0 copy-start.3
  17.0 0.0 copy-start.4
  17.0 0.0 copy-start.5
  17.0 0.0 copy-start.6
  17.0 0.0 copy-start.7
  17.0 0.0 copy-done
  17.0 1.8 %shard_map.185 = (bf16[9,256,256]{2,1,0:T(8,128)(2,1)S(1)}, bf16[9,512,512]{2,1,0:T(8,128)(2,1)S(1)}, bf16[512,128]{1,0:T(8,128)(2,1)S(1)}, s32[16,128]{1,0:T(8,128)S(1)}) custom-call(bf16[3,32]{1,0:T(4,128)(2,1)S(1)} %copy-done, s32[16,128]{1,0:T(8,128)S(1)} %get-tuple-element.50.dest_ref, bf16[27,32,32]{2,1,0:T(8,128)(2,1)S(1)} %get-tuple-element.51.k1b_ref, ...), custom_call_target="tpu_custom_call" | custom-call | flops 5000000 | bytes 5000000 | tf_op jit(solution)/shard_map/pallas_call | solution.py:255
  18.8 0.0 collective-permute-done.3
  18.8 0.1 collective-permute-start.4
  18.9 0.0 copy-done.8
  18.9 0.0 copy-done.9
  19.0 1.2 %collective-permute-done.4 = bf16[8,12,256]{2,1,0:T(8,128)(2,1)S(1)} collective-permute-done((bf16[8,12,256]{2,1,0:T(8,128)(2,1)S(1)}, bf16[8,12,256]{2,1,0:T(8,128)(2,1)S(1)}, u32[]{:S(2)}, u32[]{:S(2)}) %collective-permute-start.4) | collective-permute-done | bytes 49184 | tf_op jit(solution)/shard_map/ppermute | solution.py:557
  20.2 0.0 copy-done.1
  20.2 0.0 copy-done.3
  20.2 0.0 copy-done.4
  20.2 0.0 copy-done.5
  20.2 0.0 copy-done.6
  20.2 0.0 copy-done.7
  20.2 6.2 %shard_map.186 = bf16[216,128]{1,0:T(8,128)(2,1)S(1)} custom-call(bf16[8,32,256]{2,1,0:T(8,128)(2,1)S(1)} %fusion.own_ref.after_ref, bf16[8,12,256]{2,1,0:T(8,128)(2,1)S(1)} %get-tuple-element.78.low_ref, bf16[8,12,256]{2,1,0:T(8,128)(2,1)S(1)} %get-tuple-element.77.high_ref, bf16[320,512]{1,0:T(8,128)(2,1)S(1)} %get-tuple-element.58.own_e0_ref, ...), custom_call_target="tpu_custom_call" | custom-call | flops 3000000000 | bytes 10000000 | tf_op jit(solution)/shard_map/pallas_call | solution.py:524
  26.5 0.2 collective-permute-start.5
  26.7 5.0 %collective-permute-start.6 = (bf16[72,128]{1,0:T(8,128)(2,1)S(1)}, bf16[72,128]{1,0:T(8,128)(2,1)S(1)}, u32[]{:S(2)}, u32[]{:S(2)}) collective-permute-start(bf16[72,128]{1,0:T(8,128)(2,1)S(1)} %get-tuple-element.83), channel_id=1, source_target_pairs={{0,248},{1,249},{2,250},{3,251},{4,252},{5,253},{6,254},{7,255},{8... | collective-permute-start | bytes 55304 | tf_op jit(solution)/shard_map/ppermute | solution.py:557
  31.7 0.0 collective-permute-done.5
  31.7 1.5 %collective-permute-done.6 = bf16[72,128]{1,0:T(8,128)(2,1)S(1)} collective-permute-done((bf16[72,128]{1,0:T(8,128)(2,1)S(1)}, bf16[72,128]{1,0:T(8,128)(2,1)S(1)}, u32[]{:S(2)}, u32[]{:S(2)}) %collective-permute-start.6) | collective-permute-done | bytes 18464 | tf_op jit(solution)/shard_map/ppermute | solution.py:557
  33.3 2.5 %collective-permute-start.8 = (bf16[72,128]{1,0:T(8,128)(2,1)S(1)}, bf16[72,128]{1,0:T(8,128)(2,1)S(1)}, u32[]{:S(2)}, u32[]{:S(2)}) collective-permute-start(bf16[72,128]{1,0:T(8,128)(2,1)S(1)} %pad_maximum_fusion.5), channel_id=1, source_target_pairs={{0,1},{1,2},{2,3},{3,4},{4,5},{5,6},{6,7},{7,0},{8,9},{9,10},{10,1... | collective-permute-start | bytes 55304 | tf_op jit(solution)/shard_map/ppermute | solution.py:557
  35.8 0.0 collective-permute-start.7
  35.8 1.4 %collective-permute-done.8 = bf16[72,128]{1,0:T(8,128)(2,1)S(1)} collective-permute-done((bf16[72,128]{1,0:T(8,128)(2,1)S(1)}, bf16[72,128]{1,0:T(8,128)(2,1)S(1)}, u32[]{:S(2)}, u32[]{:S(2)}) %collective-permute-start.8) | collective-permute-done | bytes 18464 | tf_op jit(solution)/shard_map/ppermute | solution.py:557
  37.3 3.5 %collective-permute-done.7 = bf16[72,128]{1,0:T(8,128)(2,1)S(1)} collective-permute-done((bf16[72,128]{1,0:T(8,128)(2,1)S(1)}, bf16[72,128]{1,0:T(8,128)(2,1)S(1)}, u32[]{:S(2)}, u32[]{:S(2)}) %collective-permute-start.7) | collective-permute-done | bytes 18464 | tf_op jit(solution)/shard_map/ppermute | solution.py:557
  41.0 0.7 %reshape.45 = f32[9,6,512]{2,1,0:T(8,128)} convert(bf16[9,6,512]{2,1,0:T(8,128)(2,1)S(1)} %constant_dynamic-update-slice_fusion.5) | non-fusion elementwise | flops 27648 | bytes 165888 | tf_op jit(solution)/shard_map/reshape | solution.py:670
  (40 shorter events, 0.4 us)
Async XLA Ops:
  2.7 1.3 %collective-permute-start = (bf16[2,32,256]{2,1,0:T(8,128)(2,1)S(1)}, bf16[2,32,256]{2,1,0:T(8,128)(2,1)S(1)}, u32[]{:S(2)}, u32[]{:S(2)}) collective-permute-start(bf16[2,32,256]{2,1,0:T(8,128)(2,1)S(1)} %get-tuple-element.36), channel_id=1, source_target_pairs={{0,8},{1,9},{2,10},{3,11},{4,12},{5,13},{6,14},{7,15},{8,0},{9,1},... | collective-permute-start | bytes 98312 | tf_op jit(solution)/shard_map/ppermute | solution.py:557
  3.3 12.3 %copy-start.2 = (bf16[512,256]{1,0:T(8,128)(2,1)S(1)}, bf16[512,256]{1,0:T(8,128)(2,1)}, u32[]{:S(2)}) copy-start(bf16[512,256]{1,0:T(8,128)(2,1)} %constant.24.clone.pool_ref) | copy-start | bytes 786436
  4.0 6.9 %collective-permute-start.1 = (bf16[3,32,256]{2,1,0:T(8,128)(2,1)S(1)}, bf16[3,32,256]{2,1,0:T(8,128)(2,1)S(1)}, u32[]{:S(2)}, u32[]{:S(2)}) collective-permute-start(bf16[3,32,256]{2,1,0:T(8,128)(2,1)S(1)} %pad_maximum_fusion.3), channel_id=1, source_target_pairs={{0,248},{1,249},{2,250},{3,251},{4,252},{5,253},{6,254},{7,255},{8... | collective-permute-start | bytes 147464 | tf_op jit(solution)/shard_map/ppermute | solution.py:557
  10.9 1.2 %collective-permute-start.2 = (bf16[3,32,256]{2,1,0:T(8,128)(2,1)S(1)}, bf16[3,32,256]{2,1,0:T(8,128)(2,1)S(1)}, u32[]{:S(2)}, u32[]{:S(2)}) collective-permute-start(bf16[3,32,256]{2,1,0:T(8,128)(2,1)S(1)} %collective-permute-done.1), channel_id=1, source_target_pairs={{0,8},{1,9},{2,10},{3,11},{4,12},{5,13},{6,14},{7,15},{8,0},{9,1},... | collective-permute-start | bytes 147464 | tf_op jit(solution)/shard_map/ppermute | solution.py:557
  12.4 6.4 %collective-permute-start.3 = (bf16[10,12,256]{2,1,0:T(8,128)(2,1)S(1)}, bf16[10,12,256]{2,1,0:T(8,128)(2,1)S(1)}, u32[]{:S(2)}, u32[]{:S(2)}) collective-permute-start(bf16[10,12,256]{2,1,0:T(8,128)(2,1)S(1)} %maximum_select_fusion), channel_id=1, source_target_pairs={{0,1},{1,2},{2,3},{3,4},{4,5},{5,6},{6,7},{7,0},{8,15},{9,8},{10,9... | collective-permute-start | bytes 184328 | tf_op jit(solution)/shard_map/ppermute | solution.py:557
  15.6 1.4 %copy-start = (bf16[3,32]{1,0:T(4,128)(2,1)S(1)}, bf16[3,32]{1,0:T(4,128)(2,1)}, u32[]{:S(2)}) copy-start(bf16[3,32]{1,0:T(4,128)(2,1)} %head_ref.1) | copy-start | bytes 580
  15.6 3.3 %copy-start.8 = (f32[3,2048]{1,0:T(4,128)S(1)}, f32[3,2048]{1,0:T(4,128)}, u32[]{:S(2)}) copy-start(f32[3,2048]{1,0:T(4,128)} %refs_0_.1) | copy-start | bytes 73732
  15.6 3.3 %copy-start.9 = (f32[3,2048]{1,0:T(4,128)S(1)}, f32[3,2048]{1,0:T(4,128)}, u32[]{:S(2)}) copy-start(f32[3,2048]{1,0:T(4,128)} %param.19) | copy-start | bytes 73732
  16.9 3.2 %copy-start.1 = (s32[2048]{0:T(1024)S(1)}, s32[2048]{0:T(1024)}, u32[]{:S(2)}) copy-start(s32[2048]{0:T(1024)} %param.23) | copy-start | bytes 24580
  17.0 3.2 %copy-start.3 = (bf16[256,512]{1,0:T(8,128)(2,1)S(1)}, bf16[256,512]{1,0:T(8,128)(2,1)}, u32[]{:S(2)}) copy-start(bf16[256,512]{1,0:T(8,128)(2,1)} %constant.25.clone.grow_ref) | copy-start | bytes 786436
  17.0 3.2 %copy-start.4 = (bf16[96,384]{1,0:T(8,128)(2,1)S(1)}, bf16[96,384]{1,0:T(8,128)(2,1)}, u32[]{:S(2)}) copy-start(bf16[96,384]{1,0:T(8,128)(2,1)} %constant.28.clone.rowpool_ref) | copy-start | bytes 221188
  17.0 3.2 %copy-start.5 = (bf16[256,128]{1,0:T(8,128)(2,1)S(1)}, bf16[256,128]{1,0:T(8,128)(2,1)}, u32[]{:S(2)}) copy-start(bf16[256,128]{1,0:T(8,128)(2,1)} %constant.26.clone.pool1_ref) | copy-start | bytes 196612
  17.0 3.2 %copy-start.6 = (bf16[128,256]{1,0:T(8,128)(2,1)S(1)}, bf16[128,256]{1,0:T(8,128)(2,1)}, u32[]{:S(2)}) copy-start(bf16[128,256]{1,0:T(8,128)(2,1)} %constant.27.clone.grow1_ref) | copy-start | bytes 196612
  17.0 3.2 %copy-start.7 = (bf16[256,64]{1,0:T(8,128)(2,1)S(1)}, bf16[256,64]{1,0:T(8,128)(2,1)}, u32[]{:S(2)}) copy-start(bf16[256,64]{1,0:T(8,128)(2,1)} %constant.29.clone.rowgrow_ref) | copy-start | bytes 98308
  18.8 1.3 %collective-permute-start.4 = (bf16[8,12,256]{2,1,0:T(8,128)(2,1)S(1)}, bf16[8,12,256]{2,1,0:T(8,128)(2,1)S(1)}, u32[]{:S(2)}, u32[]{:S(2)}) collective-permute-start(bf16[8,12,256]{2,1,0:T(8,128)(2,1)S(1)} %broadcast_select_fusion.2), channel_id=1, source_target_pairs={{0,8},{1,9},{2,10},{3,11},{4,12},{5,13},{6,14},{7,15},{8,0},{9,1},... | collective-permute-start | bytes 147464 | tf_op jit(solution)/shard_map/ppermute | solution.py:557
  26.5 5.2 %collective-permute-start.5 = (bf16[72,128]{1,0:T(8,128)(2,1)S(1)}, bf16[72,128]{1,0:T(8,128)(2,1)S(1)}, u32[]{:S(2)}, u32[]{:S(2)}) collective-permute-start(bf16[72,128]{1,0:T(8,128)(2,1)S(1)} %get-tuple-element.82), channel_id=1, source_target_pairs={{0,8},{1,9},{2,10},{3,11},{4,12},{5,13},{6,14},{7,15},{8,0},{9,1},... | collective-permute-start | bytes 55304 | tf_op jit(solution)/shard_map/ppermute | solution.py:557
  26.7 6.5 %collective-permute-start.6 = (bf16[72,128]{1,0:T(8,128)(2,1)S(1)}, bf16[72,128]{1,0:T(8,128)(2,1)S(1)}, u32[]{:S(2)}, u32[]{:S(2)}) collective-permute-start(bf16[72,128]{1,0:T(8,128)(2,1)S(1)} %get-tuple-element.83), channel_id=1, source_target_pairs={{0,248},{1,249},{2,250},{3,251},{4,252},{5,253},{6,254},{7,255},{8... | collective-permute-start | bytes 55304 | tf_op jit(solution)/shard_map/ppermute | solution.py:557
  33.3 4.0 %collective-permute-start.8 = (bf16[72,128]{1,0:T(8,128)(2,1)S(1)}, bf16[72,128]{1,0:T(8,128)(2,1)S(1)}, u32[]{:S(2)}, u32[]{:S(2)}) collective-permute-start(bf16[72,128]{1,0:T(8,128)(2,1)S(1)} %pad_maximum_fusion.5), channel_id=1, source_target_pairs={{0,1},{1,2},{2,3},{3,4},{4,5},{5,6},{6,7},{7,0},{8,9},{9,10},{10,1... | collective-permute-start | bytes 55304 | tf_op jit(solution)/shard_map/ppermute | solution.py:557
  35.8 5.0 %collective-permute-start.7 = (bf16[72,128]{1,0:T(8,128)(2,1)S(1)}, bf16[72,128]{1,0:T(8,128)(2,1)S(1)}, u32[]{:S(2)}, u32[]{:S(2)}) collective-permute-start(bf16[72,128]{1,0:T(8,128)(2,1)S(1)} %pad_maximum_fusion.4), channel_id=1, source_target_pairs={{0,7},{1,0},{2,1},{3,2},{4,3},{5,4},{6,5},{7,6},{8,15},{9,8},{10,9... | collective-permute-start | bytes 55304 | tf_op jit(solution)/shard_map/ppermute | solution.py:557
